TPU v7x, 32 devices: a whole 2x2x4 slice. The times are simulated.
32 devices in a mesh: batch: 8 (over y, x, core), frames: 4 (over z).
Axes of the slice: x: 2, y: 2, z: 4, core: 2. Of those that a mesh axis runs over, the one named last changes fastest.
Arguments:
- params: float32 [869376], P('batch'), may hold values from -8 to 8
- first_moment: float32 [869376], P('batch'), may hold values from -6.4349833e-06 to 6.4349833e-06
- second_moment: float32 [869376], P('batch'), may hold values from 1.1502503e-12 to 4.601001e-12
- mixture: float32 [16, 2000], P('batch', 'frames'), may hold values from -6 to 6
- sources: float32 [16, 3, 2000], P('batch', None, 'frames'), may hold values from -6 to 6
- speakers: int32 [16], P('batch'), may hold values from 2 to 3
- lengths: int32 [16], P('batch'), may hold values from 500 to 2000, as said below
Outputs:
- new_params: float32 [869376], P('batch')
- half_params: bfloat16 [869376], P('batch')
- new_first: float32 [869376], P('batch')
- new_second: float32 [869376], P('batch')
- grad_norm: float32 [], replicated
- loss_parts: float32 [2], replicated
Inputs may be any that keep to these rules, and one draw needn't show every extreme that they name: `lengths`: in each run of 2 items of the same index of batch, one item drawn from the seed has length 2000.
All inputs are finite; a program needn't handle non-finite values.
Results may differ from a plain program's by a relative error of at most 0.001.
Values sent between devices are 32-bit elements; how exact they have to be, the bound alone decides.
A program may use at most 384 MiB of HBM per device.

v0:
```python
import functools
import math

import jax
import jax.numpy as jnp
from jax import lax
from jax.experimental import pallas as pl
from jax.experimental.pallas import tpu as pltpu
from jax.sharding import PartitionSpec as P

FILTERS = 64
UNITS = 128
HOP = 50
HALF_PAD = 56
SOURCES = 3
BLOCKS = 2
STEP = 5
GATES = 4 * UNITS

HIGHEST = lax.Precision.HIGHEST
NORM_EPS = 1e-08
CLIP_AT = 0.001
BETA_ONE = 0.5
BETA_TWO = 0.5
LEARN_RATE = 0.05
DECAY_RATE = 0.01
ADAM_EPS = 1e-08
F32 = jnp.float32
BF16 = jnp.bfloat16
VMEM_MAX = 60 * 2**20


def split(a):
    hi = a.astype(BF16)
    return hi, (a - hi.astype(F32)).astype(BF16)


def dot(a, b):
    return jnp.dot(a, b, preferred_element_type=F32)


def dot3(a, w_twice, w_low):
    hi, lo = split(a)
    return dot(jnp.concatenate([hi, lo], 1), w_twice) + dot(hi, w_low)


def dot_rows(a, b):
    return lax.dot_general(a, b, (((0,), (0,)), ((), ())), preferred_element_type=F32)


def dot_rows3(a, b):
    a_hi, a_lo = split(a)
    b_hi, b_lo = split(b)
    return dot_rows(a_hi, b_hi) + dot_rows(a_lo, b_hi) + dot_rows(a_hi, b_lo)


def put_split(w, twice_ref, low_ref):
    hi, lo = split(w)
    twice_ref[...] = jnp.concatenate([hi, hi], 0)
    low_ref[...] = lo


def place(dir_no, chunk_no, count, steps, inter, groups):
    first = jnp.where(dir_no == 0, chunk_no * steps, (count - 1 - chunk_no) * steps)
    if inter:
        return first, 0, 0
    half = first // HOP
    return first, half, pl.multiple_of((first - HOP * half) * groups, 8)


def forward_kernel(inter, first_layer, groups, steps, *refs):
    if first_layer:
        (dir_ref, x_ref, win_ref, wrec_ref, bias_ref, proj_ref,
         h_ref, coef_ref, part_ref,
         wi2, wil, wr2, wrl, pj2, pjl, bias_s, gin, c_s, h_s) = refs
    else:
        (dir_ref, prev_ref, pa_ref, pb_ref, vec_ref, win_ref, wrec_ref, bias_ref, proj_ref,
         x_ref, normed_ref, scale_ref, h_ref, coef_ref, part_ref,
         wi2, wil, wr2, wrl, pj2, pjl, bias_s, gin, c_s, h_s) = refs
    chunk_no = pl.program_id(0)
    count = pl.num_programs(0)
    dir_no = dir_ref[0]
    rows = 2 * HALF_PAD if inter else groups
    valid = HOP * groups

    @pl.when(chunk_no == 0)
    def _():
        column = lax.broadcasted_iota(jnp.int32, (1, GATES), 1)
        scaling = jnp.where((column >= 2 * UNITS) & (column < 3 * UNITS), 1.0, 0.5)
        win = win_ref[...] * scaling
        none = jnp.zeros_like(win)
        for half in range(2):
            put_split(jnp.concatenate([win, none] if half == 0 else [none, win], 0), wi2.at[half], wil.at[half])
        put_split(wrec_ref[...] * scaling, wr2, wrl)
        bias_s[...] = jnp.broadcast_to(bias_ref[...] * scaling, bias_s.shape)
        proj = proj_ref[...]
        none = jnp.zeros_like(proj)
        for half in range(2):
            put_split(jnp.concatenate([proj, none] if half == 0 else [none, proj], 1), pj2.at[half], pjl.at[half])
        c_s[...] = jnp.zeros_like(c_s)
        h_s[...] = jnp.zeros_like(h_s)
        h_ref[0] = jnp.zeros((rows, UNITS), F32)
        h_ref[h_ref.shape[0] - 1] = jnp.zeros((rows, UNITS), F32)
        if not first_layer:
            mixed = pa_ref[:valid] + pb_ref[:valid] + vec_ref[0:1]
            total = 2.0 * valid * FILTERS
            mean = jnp.sum(mixed) / total
            spread = jnp.sum(mixed * mixed) / total - mean * mean
            scale = lax.rsqrt(jnp.full((1, 128), spread + NORM_EPS, F32))
            normed = (mixed - mean) * scale
            normed_ref[:valid] = normed
            x_ref[:valid] = prev_ref[:valid] + vec_ref[1:2] * normed + vec_ref[2:3]
            x_ref[valid:] = jnp.zeros((x_ref.shape[0] - valid, 128), F32)
            normed_ref[valid:] = jnp.zeros((x_ref.shape[0] - valid, 128), F32)
            scale_ref[...] = jnp.broadcast_to(scale, scale_ref.shape)

    first, half, row = place(dir_no, chunk_no, count, steps, inter, groups)
    if inter:
        xs = jnp.concatenate(
            [x_ref[pl.ds(first + u, HALF_PAD, stride=groups), :] for u in range(steps)], 0
        )
        for side in range(2):
            found = dot3(xs, wi2[side], wil[side]) + bias_s[0:1]
            for u in range(steps):
                gin[pl.ds(u * rows + side * HALF_PAD, HALF_PAD)] = found[u * HALF_PAD:(u + 1) * HALF_PAD]
    else:
        xs = x_ref[pl.ds(row, steps * groups), :]
        gin[...] = dot3(xs, wi2[half], wil[half]) + bias_s[0:1]

    h = h_s[...]
    c = c_s[...]
    for u in range(steps):
        v = jnp.where(dir_no == 0, u, steps - 1 - u)
        hi, lo = split(h)
        z = (
            gin[pl.ds(pl.multiple_of(v * rows, 8), rows)]
            + dot(jnp.concatenate([hi, lo], 1), wr2[...])
            + dot(hi, wrl[...])
        )
        th = jnp.tanh(z)
        ti, tf, g, to = (th[:, q * UNITS:(q + 1) * UNITS] for q in range(4))
        i_g = 0.5 * ti + 0.5
        f_g = 0.5 * tf + 0.5
        o_g = 0.5 * to + 0.5
        c_prev = c
        c = f_g * c + i_g * g
        tc = jnp.tanh(c)
        h = o_g * tc
        h_ref[first + v + 1] = h
        coef_ref[u, 0] = tc * (0.25 - 0.25 * to * to)
        coef_ref[u, 1] = o_g * (1.0 - tc * tc)
        coef_ref[u, 2] = g * (0.25 - 0.25 * ti * ti)
        coef_ref[u, 3] = c_prev * (0.25 - 0.25 * tf * tf)
        coef_ref[u, 4] = i_g * (1.0 - g * g)
        coef_ref[u, 5] = f_g
    h_s[...] = h
    c_s[...] = c

    hs = h_ref[pl.ds(first + 1, steps)]
    if inter:
        low_half = hs[:, :HALF_PAD].reshape(steps * HALF_PAD, UNITS)
        top_half = hs[:, HALF_PAD:].reshape(steps * HALF_PAD, UNITS)
        found = dot3(low_half, pj2[0], pjl[0]) + dot3(top_half, pj2[1], pjl[1])
        for u in range(steps):
            part_ref[pl.ds(first + u, HALF_PAD, stride=groups), :] = found[u * HALF_PAD:(u + 1) * HALF_PAD]
    else:
        found = dot3(hs.reshape(steps * groups, UNITS), pj2[half], pjl[half])
        here = pl.ds(row, steps * groups)

        @pl.when(2 * chunk_no < count)
        def _():
            part_ref[here] = found

        @pl.when(2 * chunk_no >= count)
        def _():
            part_ref[here] = part_ref[here] + found


def backward_kernel(inter, last_layer, groups, steps, *refs):
    if last_layer:
        (dir_ref, g_ref, normed_ref, scale_ref, vec_ref, x_ref, h_ref, coef_ref, win_ref, wrec_ref, proj_ref,
         dx_ref, dwin_ref, dwrec_ref, db_ref, dproj_ref, dvec_ref,
         wi2, wil, wrw, wrt, pj2, pjl, dmx, dhc, dzs, dz_s, dc_s, awin, aproj) = refs
    else:
        (dir_ref, res_ref, da_ref, db2_ref, normed_ref, scale_ref, vec_ref, x_ref, h_ref, coef_ref,
         win_ref, wrec_ref, proj_ref,
         g_ref, dx_ref, dwin_ref, dwrec_ref, db_ref, dproj_ref, dvec_ref,
         wi2, wil, wrw, wrt, pj2, pjl, dmx, dhc, dzs, dz_s, dc_s, awin, aproj) = refs
    back_no = pl.program_id(0)
    count = pl.num_programs(0)
    chunk_no = count - 1 - back_no
    dir_no = dir_ref[0]
    rows = 2 * HALF_PAD if inter else groups
    valid = HOP * groups

    @pl.when(back_no == 0)
    def _():
        win_t = win_ref[...].T
        none = jnp.zeros_like(win_t)
        for half in range(2):
            put_split(jnp.concatenate([win_t, none] if half == 0 else [none, win_t], 1), wi2.at[half], wil.at[half])
        hi, lo = split(wrec_ref[...].T)
        wrw[...] = jnp.concatenate([hi, lo], 1)
        wrt[...] = hi
        proj_t = proj_ref[...].T
        none = jnp.zeros_like(proj_t)
        for half in range(2):
            put_split(jnp.concatenate([proj_t, none] if half == 0 else [none, proj_t], 0), pj2.at[half], pjl.at[half])
        dz_s[...] = jnp.zeros_like(dz_s)
        dc_s[...] = jnp.zeros_like(dc_s)
        awin[...] = jnp.zeros_like(awin)
        aproj[...] = jnp.zeros_like(aproj)
        db_ref[...] = jnp.zeros_like(db_ref)
        if not last_layer:
            g_ref[:valid] = res_ref[:valid] + da_ref[:valid] + db2_ref[:valid]
            g_ref[valid:] = jnp.zeros((g_ref.shape[0] - valid, 128), F32)
        g = g_ref[:valid]
        normed = normed_ref[:valid]
        g_n = g * vec_ref[1:2]
        total = 2.0 * valid * FILTERS
        mean_one = jnp.sum(g_n) / total
        mean_two = jnp.sum(g_n * normed) / total
        dmixed = scale_ref[0:1] * (g_n - mean_one - normed * mean_two)
        dmx[:valid] = dmixed
        dmx[valid:] = jnp.zeros((dmx.shape[0] - valid, 128), F32)
        dvec_ref[...] = jnp.zeros_like(dvec_ref)
        dvec_ref[0:1] = jnp.sum(dmixed, 0, keepdims=True)
        dvec_ref[1:2] = jnp.sum(g * normed, 0, keepdims=True)
        dvec_ref[2:3] = jnp.sum(g, 0, keepdims=True)

    first, half, row = place(dir_no, chunk_no, count, steps, inter, groups)
    here = pl.ds(row, steps * groups)
    if inter:
        dms = jnp.concatenate(
            [dmx[pl.ds(first + u, HALF_PAD, stride=groups), :] for u in range(steps)], 0
        )
        for side in range(2):
            found = dot3(dms, pj2[side], pjl[side])
            for u in range(steps):
                dhc[pl.ds(u * rows + side * HALF_PAD, HALF_PAD)] = found[u * HALF_PAD:(u + 1) * HALF_PAD]
    else:
        dms = dmx[here, :]
        dhc[...] = dot3(dms, pj2[half], pjl[half])

    dz = dz_s[...]
    dc_next = dc_s[...]
    for u in reversed(range(steps)):
        v = jnp.where(dir_no == 0, u, steps - 1 - u)
        hi, lo = split(dz)
        wide = dot(hi, wrw[...])
        dh = (
            dhc[pl.ds(pl.multiple_of(v * rows, 8), rows)]
            + wide[:, :UNITS] + wide[:, UNITS:] + dot(lo, wrt[...])
        )
        dc = dh * coef_ref[u, 1] + dc_next
        dz = jnp.concatenate(
            [dc * coef_ref[u, 2], dc * coef_ref[u, 3], dc * coef_ref[u, 4], dh * coef_ref[u, 0]], 1
        )
        dc_next = dc * coef_ref[u, 5]
        if inter:
            dzs[0, pl.ds(pl.multiple_of(v * HALF_PAD, 8), HALF_PAD)] = dz[:HALF_PAD]
            dzs[1, pl.ds(pl.multiple_of(v * HALF_PAD, 8), HALF_PAD)] = dz[HALF_PAD:]
        else:
            dzs[0, pl.ds(pl.multiple_of(v * rows, 8), rows)] = dz
    dz_s[...] = dz
    dc_s[...] = dc_next

    hs = h_ref[pl.ds(first + 1, steps)]
    hp = h_ref[pl.ds(first + 2 * dir_no, steps)]
    if inter:
        xs = jnp.concatenate(
            [x_ref[pl.ds(first + u, HALF_PAD, stride=groups), :] for u in range(steps)], 0
        )
        found = 0.0
        for side in range(2):
            cut = slice(side * HALF_PAD, (side + 1) * HALF_PAD)
            dzc = dzs[side]
            found = found + dot3(dzc, wi2[side], wil[side])
            turned = xs if side == 0 else pltpu.roll(xs, FILTERS, 1)
            awin[...] += dot_rows3(
                jnp.concatenate([turned, hp[:, cut].reshape(steps * HALF_PAD, UNITS)], 1), dzc
            )
            aproj[side] += dot_rows3(hs[:, cut].reshape(steps * HALF_PAD, UNITS), dms)
            db_ref[0:1] += jnp.sum(dzc, 0, keepdims=True)
        for u in range(steps):
            dx_ref[pl.ds(first + u, HALF_PAD, stride=groups), :] = found[u * HALF_PAD:(u + 1) * HALF_PAD]
    else:
        xs = x_ref[here, :]
        dzc = dzs[0]
        turned = jnp.where(half == 0, xs, pltpu.roll(xs, FILTERS, 1))
        awin[...] += dot_rows3(jnp.concatenate([turned, hp.reshape(steps * groups, UNITS)], 1), dzc)
        aproj[half] += dot_rows3(hs.reshape(steps * groups, UNITS), dms)
        db_ref[0:1] += jnp.sum(dzc, 0, keepdims=True)
        found = dot3(dzc, wi2[half], wil[half])

        @pl.when(2 * back_no < count)
        def _():
            dx_ref[here] = found

        @pl.when(2 * back_no >= count)
        def _():
            dx_ref[here] = dx_ref[here] + found

    @pl.when(back_no == count - 1)
    def _():
        dwin_ref[...] = awin[:FILTERS]
        dwrec_ref[...] = awin[2 * FILTERS:]
        dproj_ref[...] = aproj[0, :, :FILTERS] + aproj[1, :, FILTERS:]


def sizes(inter, groups):
    if inter:
        return groups, 2 * HALF_PAD, 8
    return 2 * HOP, groups, 10


def whole(shape):
    return pl.BlockSpec(shape, lambda j: (0,) * len(shape))


def run_forward(layer_no, groups, dir_no, stream, weights):
    inter = layer_no % 2 == 1
    first_layer = layer_no == 0
    length, rows, steps = sizes(inter, groups)
    stream_shape = (HALF_PAD * groups, 128)
    count = length // steps
    coef_block = (steps, 6, rows, UNITS)
    out = [
        ((length + 2, rows, UNITS), whole((length + 2, rows, UNITS))),
        ((length, 6, rows, UNITS), pl.BlockSpec(coef_block, lambda j: (j, 0, 0, 0))),
        (stream_shape, whole(stream_shape)),
    ]
    if not first_layer:
        out = [(stream_shape, whole(stream_shape)), (stream_shape, whole(stream_shape)), ((8, 128), whole((8, 128)))] + out
    operands = list(stream) + list(weights)
    gin_rows = steps * rows
    return pl.pallas_call(
        functools.partial(forward_kernel, inter, first_layer, groups, steps),
        grid=(count,),
        in_specs=[pl.BlockSpec(memory_space=pltpu.SMEM)] + [whole(a.shape) for a in operands],
        out_specs=[spec for _, spec in out],
        out_shape=[jax.ShapeDtypeStruct(shape, F32) for shape, _ in out],
        scratch_shapes=[
            pltpu.VMEM((2, 256, GATES), BF16), pltpu.VMEM((2, 128, GATES), BF16),
            pltpu.VMEM((256, GATES), BF16), pltpu.VMEM((128, GATES), BF16),
            pltpu.VMEM((2, 256, 128), BF16), pltpu.VMEM((2, 128, 128), BF16),
            pltpu.VMEM((8, GATES), F32), pltpu.VMEM((gin_rows, GATES), F32),
            pltpu.VMEM((rows, UNITS), F32), pltpu.VMEM((rows, UNITS), F32),
        ],
        compiler_params=pltpu.CompilerParams(vmem_limit_bytes=VMEM_MAX),
        name="forward_inter" if inter else "forward_intra",
    )(dir_no, *operands)


def run_backward(layer_no, groups, dir_no, grads, normed, scale, vec, x, h_all, coef, weights):
    inter = layer_no % 2 == 1
    last_layer = layer_no == 2 * BLOCKS - 1
    length, rows, steps = sizes(inter, groups)
    stream_shape = (HALF_PAD * groups, 128)
    count = length // steps
    coef_block = (steps, 6, rows, UNITS)
    out = [stream_shape, (FILTERS, GATES), (UNITS, GATES), (8, GATES), (UNITS, FILTERS), (8, 128)]
    if not last_layer:
        out = [stream_shape] + out
    before = list(grads) + [normed, scale, vec, x, h_all]
    return pl.pallas_call(
        functools.partial(backward_kernel, inter, last_layer, groups, steps),
        grid=(count,),
        in_specs=[pl.BlockSpec(memory_space=pltpu.SMEM)]
        + [whole(a.shape) for a in before]
        + [pl.BlockSpec(coef_block, lambda j: (count - 1 - j, 0, 0, 0))]
        + [whole(a.shape) for a in weights],
        out_specs=[whole(shape) for shape in out],
        out_shape=[jax.ShapeDtypeStruct(shape, F32) for shape in out],
        scratch_shapes=[
            pltpu.VMEM((2, 2 * GATES, 128), BF16), pltpu.VMEM((2, GATES, 128), BF16),
            pltpu.VMEM((GATES, 256), BF16), pltpu.VMEM((GATES, 128), BF16),
            pltpu.VMEM((2, 256, 128), BF16), pltpu.VMEM((2, 128, 128), BF16),
            pltpu.VMEM(stream_shape, F32), pltpu.VMEM((steps * rows, UNITS), F32),
            pltpu.VMEM((2, steps * HALF_PAD, GATES) if inter else (1, steps * rows, GATES), F32),
            pltpu.VMEM((rows, GATES), F32), pltpu.VMEM((rows, UNITS), F32),
            pltpu.VMEM((256, GATES), F32), pltpu.VMEM((2, UNITS, 128), F32),
        ],
        compiler_params=pltpu.CompilerParams(vmem_limit_bytes=VMEM_MAX),
        name="backward_inter" if inter else "backward_intra",
    )(dir_no, *before, coef, *weights)


def layout():
    entries = [("encoder", (FILTERS, 2))]
    for layer_no in range(2 * BLOCKS):
        for side_no in range(2):
            entries += [
                ("input", (FILTERS, 4 * UNITS)),
                ("recurrent", (UNITS, 4 * UNITS)),
                ("gate_bias", (4 * UNITS,)),
            ]
        entries += [
            ("project", (2 * UNITS, FILTERS)),
            ("offset", (FILTERS,)),
            ("gain", (FILTERS,)),
            ("shift", (FILTERS,)),
        ]
    entries += [("masker", (FILTERS, SOURCES * FILTERS)), ("decoder", (FILTERS, 2))]
    return entries


SIDE = FILTERS * GATES + UNITS * GATES + GATES
LAYER = 2 * SIDE + 2 * UNITS * FILTERS + 3 * FILTERS


def layer_weights(flat, layer_no, dir_no):
    start = 2 * FILTERS + LAYER * layer_no
    mine = lax.dynamic_slice(flat, (start + SIDE * dir_no,), (SIDE,))
    cut = FILTERS * GATES
    win = mine[:cut].reshape(FILTERS, GATES)
    wrec = mine[cut:cut + UNITS * GATES].reshape(UNITS, GATES)
    bias = mine[cut + UNITS * GATES:].reshape(1, GATES)
    at = start + 2 * SIDE
    proj = lax.dynamic_slice(flat, (at + UNITS * FILTERS * dir_no,), (UNITS * FILTERS,)).reshape(UNITS, FILTERS)
    at += 2 * UNITS * FILTERS
    vec = flat[at:at + 3 * FILTERS].reshape(3, FILTERS)
    vec = jnp.pad(jnp.concatenate([vec, vec], 1), ((0, 5), (0, 0)))
    return win, wrec, bias, proj, vec


def local(params, first_moment, second_moment, mixture, sources, speakers, lengths):
    flat = lax.all_gather(params, "batch", axis=0, tiled=True)
    items = mixture.shape[0]
    frames_size = lax.axis_size("frames")
    samples = mixture.shape[1] * frames_size
    groups = samples // HOP
    core = lax.axis_index("batch") % 2
    depth = lax.axis_index("frames")
    column = 2 * items
    copies = frames_size // column
    mine = depth // copies
    weight = jnp.where(depth % copies == 0, 1.0, 0.0).astype(F32)
    pairs = [[2 * b, 2 * b + 1] for b in range(lax.axis_size("batch") // 2)]
    swap = [(b, b + 1 if b % 2 == 0 else b - 1) for b in range(lax.axis_size("batch"))]

    signals = jnp.concatenate([mixture[:, None], sources], 1)
    signals = lax.all_gather(signals, "frames", axis=2, tiled=True)
    scalars = jnp.stack([speakers, lengths], 1).astype(F32)
    signals = lax.all_gather(signals, "batch", axis=0, tiled=True, axis_index_groups=pairs)
    scalars = lax.all_gather(scalars, "batch", axis=0, tiled=True, axis_index_groups=pairs)
    signal = lax.dynamic_slice_in_dim(signals, mine, 1, 0)[0]
    scalar = lax.dynamic_slice_in_dim(scalars, mine, 1, 0)[0]
    mix = signal[0]
    following = jnp.concatenate([mix[1:], jnp.zeros((1,), F32)])

    def by_row(array):
        return array.reshape(array.shape[:-1] + (groups, HOP)).swapaxes(-1, -2).reshape(array.shape[:-1] + (groups * HOP,))

    mix_row = by_row(mix)
    follow_row = by_row(following)
    encoder = flat[:2 * FILTERS].reshape(FILTERS, 2)
    raw = mix_row[:, None] * encoder[:, 0] + follow_row[:, None] * encoder[:, 1]
    encoded = jax.nn.softplus(raw)

    def later(array):
        three = array.reshape(HOP, groups, -1)
        return jnp.concatenate([three[:, 1:], jnp.zeros_like(three[:, :1])], 1).reshape(array.shape)

    def earlier(array):
        three = array.reshape(HOP, groups, -1)
        return jnp.concatenate([jnp.zeros_like(three[:, :1]), three[:, :-1]], 1).reshape(array.shape)

    pad = ((0, (HALF_PAD - HOP) * groups), (0, 0))
    stream = jnp.pad(jnp.concatenate([encoded, later(encoded)], 1), pad)
    dir_no = core.reshape(1).astype(jnp.int32)

    def exchange(array):
        return lax.ppermute(array, "batch", swap)

    kept = []
    weights = []
    below = (stream,)
    for layer_no in range(2 * BLOCKS):
        *lstm, vec = layer_weights(flat, layer_no, core)
        found = run_forward(layer_no, groups, dir_no, below, lstm)
        if layer_no == 0:
            x = stream
        else:
            x, normed, scale = found[:3]
            kept[-1] += [normed, scale]
        h_all, coef, part = found[-3:]
        kept.append([x, h_all, coef])
        weights.append((lstm, vec))
        below = (x, part, exchange(part), vec)

    prev, pa, pb, vec = below
    valid_rows = HOP * groups
    mixed = (pa + pb + vec[0:1])[:valid_rows]
    total = 2.0 * valid_rows * FILTERS
    mean = jnp.sum(mixed) / total
    spread = jnp.sum(mixed * mixed) / total - mean * mean
    scale = lax.rsqrt(spread + NORM_EPS)
    normed = (mixed - mean) * scale
    separated = prev[:valid_rows] + vec[1:2] * normed + vec[2:3]
    kept[-1] += [jnp.pad(normed, pad), jnp.full((8, 128), scale, F32)]

    position = by_row(jnp.arange(samples).astype(F32))
    valid = jnp.where(position < scalar[1], 1.0, 0.0) * weight
    active = jnp.where(jnp.arange(SOURCES).astype(F32) < scalar[0], 1.0, 0.0)
    target = by_row(signal[1:]) * active[:, None]
    tail = FILTERS * SOURCES * FILTERS
    masker = flat[-tail - 2 * FILTERS:-2 * FILTERS].reshape(FILTERS, SOURCES * FILTERS)
    decoder = flat[-2 * FILTERS:].reshape(FILTERS, 2)

    def previous_frame(array):
        three = array.reshape(HOP, groups, -1)
        top = jnp.concatenate([jnp.zeros_like(three[-1:, :1]), three[-1:, :-1]], 1)
        return jnp.concatenate([top, three[:-1]], 0).reshape(array.shape)

    def head(masker, decoder, separated, encoded):
        summed = separated[:, :FILTERS] + earlier(separated[:, FILTERS:])
        logits = jnp.dot(summed, masker, precision=HIGHEST).reshape(-1, SOURCES, FILTERS)
        masked = jax.nn.sigmoid(logits) * active[:, None] * encoded[:, None, :]
        previous = previous_frame(masked)
        estimate = jnp.einsum("njc,c->nj", masked, decoder[:, 0], precision=HIGHEST) + jnp.einsum(
            "njc,c->nj", previous, decoder[:, 1], precision=HIGHEST
        )
        differ = estimate - target.T
        return jnp.sum(valid[:, None] * (jnp.sqrt(differ * differ + 1.0) - 1.0))

    loss_local, (grad_masker, grad_decoder, grad, grad_encoded) = jax.value_and_grad(head, (0, 1, 2, 3))(
        masker, decoder, separated, encoded
    )
    grads = (jnp.pad(grad, pad),)
    layer_grads = [None] * (2 * BLOCKS)
    lead = jnp.where(core == 0, 1.0, 0.0).astype(F32)
    sides = jnp.stack([lead, 1.0 - lead])
    for layer_no in reversed(range(2 * BLOCKS)):
        lstm, vec = weights[layer_no]
        x, h_all, coef, normed, scale = kept[layer_no]
        win, wrec, _, proj = lstm
        found = run_backward(layer_no, groups, dir_no, grads, normed, scale, vec, x, h_all, coef, (win, wrec, proj))
        g = found[0] if len(found) == 7 else grads[0]
        dx, dwin, dwrec, db, dproj, dvec = found[-6:]
        side = jnp.concatenate([dwin.reshape(-1), dwrec.reshape(-1), db[0]])
        folded = dvec[:3, :FILTERS] + dvec[:3, FILTERS:]
        layer_grads[layer_no] = jnp.concatenate(
            [(sides[:, None] * side).reshape(-1), (sides[:, None] * dproj.reshape(-1)).reshape(-1), lead * folded.reshape(-1)]
        )
        if layer_no:
            grads = (g, dx, exchange(dx))
    grad_groups = (lead * g + dx)[:valid_rows]
    grad_enc = grad_groups[:, :FILTERS] + earlier(grad_groups[:, FILTERS:]) + lead * grad_encoded
    grad_raw = grad_enc * jax.nn.sigmoid(raw)
    grad_encoder = jnp.stack(
        [jnp.sum(grad_raw * mix_row[:, None], 0), jnp.sum(grad_raw * follow_row[:, None], 0)], 1
    )
    gradient = jnp.concatenate(
        [grad_encoder.reshape(-1)] + layer_grads + [lead * grad_masker.reshape(-1), lead * grad_decoder.reshape(-1)]
    )
    loss_sum, count = lax.psum(
        (loss_local * lead, jnp.sum(lengths).astype(F32) / frames_size), ("batch", "frames")
    )
    shard = lax.psum_scatter(gradient, "batch", scatter_dimension=0, tiled=True)
    shard = lax.psum(shard, "frames") / count
    grad_norm = jnp.sqrt(lax.psum(jnp.sum(shard * shard), "batch"))
    clipped = shard * (CLIP_AT / jnp.maximum(grad_norm, CLIP_AT))
    new_first = BETA_ONE * first_moment + (1.0 - BETA_ONE) * clipped
    new_second = BETA_TWO * second_moment + (1.0 - BETA_TWO) * clipped * clipped
    step_size = (
        new_first / (1.0 - BETA_ONE**STEP) / (jnp.sqrt(new_second / (1.0 - BETA_TWO**STEP)) + ADAM_EPS)
    )
    new_params = params - LEARN_RATE * (step_size + DECAY_RATE * params)
    return (
        new_params,
        new_params.astype(BF16),
        new_first,
        new_second,
        grad_norm,
        jnp.stack([loss_sum, count]),
    )


def solution(mesh):
    placed = (
        P("batch"),
        P("batch"),
        P("batch"),
        P("batch", "frames"),
        P("batch", None, "frames"),
        P("batch"),
        P("batch"),
    )
    return jax.shard_map(
        local,
        mesh=mesh,
        in_specs=placed,
        out_specs=(P("batch"), P("batch"), P("batch"), P("batch"), P(), P()),
        check_vma=False,
    )
```

profile of v0, /device:TPU:0, one launch (start us, length us, event | category | flops | bytes accessed | tf_op | source)
XLA Modules:
  0.0 615.5 jit_solution(6837077233340976502)
XLA Ops:
  7.2 2.1 reshape.482
  11.2 38.9 %all_gather.12 = f32[2,4,2000]{1,0,2:T(2,128)S(1)} all-gather(f32[2,4,500]{1,0,2:T(2,128)S(1)} %pad_maximum_fusion), channel_id=1, replica_groups=mesh['batch'=8,'frames'=4] {'frames'}, dimensions={2}, use_global_device_ids=true | all-gather | bytes 80000 | tf_op jit(solution)/shard_map/all_gather | solution.py:443
  50.2 1.7 copy.111
  51.9 1.9 all_gather.13
  56.7 1.5 fusion.27
  67.0 27.8 %forward_intra.2 = (f32[102,40,128]{2,1,0:T(8,128)}, f32[100,6,40,128]{3,2,1,0:T(8,128)}, f32[2240,128]{1,0:T(8,128)}) custom-call(s32[1]{0:T(128)} %bitcast.1.refs_0_, f32[2240,128]{1,0:T(8,128)} %select_maximum_fusion.1.refs_1_.refs_7_, f32[64,512]{1,0:T(8,128)} %slice.322.refs_2_.refs_10_, f32[128,512]{1,0:T(8,128)} %slice.324.refs_3_.refs_11_, ...), custom_call_target="tpu_custom_call" | custom-call | tf_op jit(solution)/shard_map/forward_intra/pallas_call | solution.py:337
  100.4 18.9 %forward_inter.2 = (f32[2240,128]{1,0:T(8,128)}, f32[2240,128]{1,0:T(8,128)}, f32[8,128]{1,0:T(8,128)}, f32[42,112,128]{2,1,0:T(8,128)}, f32[40,6,112,128]{3,2,1,0:T(8,128)}, /*index=5*/f32[2240,128]{1,0:T(8,128)}) custom-call(s32[1]{0:T(128)} %bitcast.1.refs_0_, f32[2240,128]{1,0:T(8,128)} %select_maximum_fusion.1.refs_1_.refs_7_, ...), custom_call_target="tpu_custom_call" | custom-call | tf_op jit(solution)/shard_map/forward_inter/pallas_call | solution.py:337
  123.5 30.0 %forward_intra.3 = (f32[2240,128]{1,0:T(8,128)}, f32[2240,128]{1,0:T(8,128)}, f32[8,128]{1,0:T(8,128)}, f32[102,40,128]{2,1,0:T(8,128)}, f32[100,6,40,128]{3,2,1,0:T(8,128)}, /*index=5*/f32[2240,128]{1,0:T(8,128)}) custom-call(s32[1]{0:T(128)} %bitcast.1.refs_0_, f32[2240,128]{1,0:T(8,128)} %get-tuple-element.55.refs_1_.refs_7_, ...), custom_call_target="tpu_custom_call" | custom-call | tf_op jit(solution)/shard_map/forward_intra/pallas_call | solution.py:337
  157.6 18.9 %forward_inter.3 = (f32[2240,128]{1,0:T(8,128)}, f32[2240,128]{1,0:T(8,128)}, f32[8,128]{1,0:T(8,128)}, f32[42,112,128]{2,1,0:T(8,128)}, f32[40,6,112,128]{3,2,1,0:T(8,128)}, /*index=5*/f32[2240,128]{1,0:T(8,128)}) custom-call(s32[1]{0:T(128)} %bitcast.1.refs_0_, f32[2240,128]{1,0:T(8,128)} %get-tuple-element.57.refs_1_.refs_7_, ...), custom_call_target="tpu_custom_call" | custom-call | tf_op jit(solution)/shard_map/forward_inter/pallas_call | solution.py:337
  176.9 2.3 all-gather.1
  184.0 2.5 fusion.19
  190.6 2.9 multiply_multiply_fusion
  193.5 3.5 copy.120
  197.0 5.7 reshape.460
  203.4 3.0 copy.121
  206.5 5.6 slice.360
  212.1 3.0 select_maximum_fusion
  215.1 5.4 reshape.461
  220.5 4.9 multiply_reduce_fusion
  225.8 6.6 %fusion.17 = f32[1,2000,3]{0,1,2:T(8,128)} fusion(f32[2000,3,64]{0,2,1:T(8,128)S(1)} %get-tuple-element.158, f32[64]{0:T(128)S(1)} %get-tuple-element.106), kind=kOutput, calls=%fused_computation.91 | convolution fusion | flops 4608000 | bytes 1560256 | tf_op jit(solution)/shard_map/jvp(njc,c->nj)/dot_general | solution.py:521
  232.4 3.1 copy.132
  237.8 3.1 copy.123
  240.9 5.8 split.17
  246.9 1.7 pad_add_fusion
  248.6 2.6 reshape.464
  251.2 3.4 copy.125
  254.6 2.9 multiply_reduce_fusion.1
  257.5 3.5 fusion.30
  264.9 24.2 %backward_inter.2 = (f32[2240,128]{1,0:T(8,128)}, f32[64,512]{1,0:T(8,128)}, f32[128,512]{1,0:T(8,128)}, f32[8,512]{1,0:T(8,128)}, f32[128,64]{1,0:T(8,128)}, /*index=5*/f32[8,128]{1,0:T(8,128)}) custom-call(s32[1]{0:T(128)} %bitcast.1.refs_0_, f32[2240,128]{1,0:T(8,128)} %pad.57.refs_1_, f32[2240,128]{1,0:T(8,128)} %pad.58.refs_2_, ...), custom_call_target="tpu_custom_call" | custom-call | tf_op jit(solution)/shard_map/backward_inter/pallas_call | solution.py:366
  290.1 2.0 collective-permute-done.4.refs_3_
  293.2 38.2 %backward_intra.2 = (f32[2240,128]{1,0:T(8,128)}, f32[2240,128]{1,0:T(8,128)}, f32[64,512]{1,0:T(8,128)}, f32[128,512]{1,0:T(8,128)}, f32[8,512]{1,0:T(8,128)}, /*index=5*/f32[128,64]{1,0:T(8,128)}, f32[8,128]{1,0:T(8,128)}) custom-call(s32[1]{0:T(128)} %bitcast.1.refs_0_, f32[2240,128]{1,0:T(8,128)} %pad.57.refs_1_, f32[2240,128]{1,0:T(8,128)} %get-tuple-element.63.refs_2_, ...), custom_call_target="tpu_custom_call" | custom-call | tf_op jit(solution)/shard_map/backward_intra/pallas_call | solution.py:366
  331.8 2.7 convolution_bitcast_fusion
  334.5 1.7 fusion.6
  337.0 3.6 convolution_multiply_fusion
  345.6 25.6 %backward_inter.3 = (f32[2240,128]{1,0:T(8,128)}, f32[2240,128]{1,0:T(8,128)}, f32[64,512]{1,0:T(8,128)}, f32[128,512]{1,0:T(8,128)}, f32[8,512]{1,0:T(8,128)}, /*index=5*/f32[128,64]{1,0:T(8,128)}, f32[8,128]{1,0:T(8,128)}) custom-call(s32[1]{0:T(128)} %bitcast.1.refs_0_, f32[2240,128]{1,0:T(8,128)} %get-tuple-element.68.refs_1_, ...), custom_call_target="tpu_custom_call" | custom-call | tf_op jit(solution)/shard_map/backward_inter/pallas_call | solution.py:366
  377.0 37.8 %backward_intra.3 = (f32[2240,128]{1,0:T(8,128)}, f32[2240,128]{1,0:T(8,128)}, f32[64,512]{1,0:T(8,128)}, f32[128,512]{1,0:T(8,128)}, f32[8,512]{1,0:T(8,128)}, /*index=5*/f32[128,64]{1,0:T(8,128)}, f32[8,128]{1,0:T(8,128)}) custom-call(s32[1]{0:T(128)} %bitcast.1.refs_0_, f32[2240,128]{1,0:T(8,128)} %get-tuple-element.74.refs_1_, ...), custom_call_target="tpu_custom_call" | custom-call | tf_op jit(solution)/shard_map/backward_intra/pallas_call | solution.py:366
  419.1 4.3 broadcast_multiply_fusion.1
  424.8 1.8 mul.477
  426.5 2.7 mul.486
  429.2 1.7 multiply_add_fusion.1
  433.3 33.1 %concatenate.67 = f32[869376]{0:T(1024)} concatenate(f32[128]{0:T(128)S(1)} %reshape.470, f32[197632]{0:T(1024)S(1)} %mul.457, f32[16384]{0:T(1024)S(1)} %bitcast.142, f32[192]{0:T(256)S(1)} %mul.465, f32[197632]{0:T(1024)S(1)} %mul.468, f32[16384]{0:T(1024)S(1)} %bitcast.143, f32[192]{0:T(256)S(1)} %mul.474, f32[197632]{0:T(1024)S(1)} %mul.477, f32[16384]{0:T(1024)} %bitcast.144, ...), dimensions={0} | concatenate | bytes 6955008 | tf_op jit(solution)/shard_map/concatenate | solution.py:554
  468.2 73.4 %all-reduce.25.cloned.1.call-done = f32[869376]{0:T(1024)} async-done(((f32[869376]{0:T(1024)}), f32[869376]{0:T(1024)}) %all-reduce.25.cloned.1.call-update) | async-done | bytes 3477520
  541.6 2.0 dynamic-slice.1
  545.6 40.1 %all-reduce.19 = (f32[]{:T(128)}, f32[1]{0:T(128)}) all-reduce(f32[]{:T(128)S(6)} %div.47, f32[1]{0:T(128)} %bitcast.48), channel_id=1, replica_groups=mesh['batch'=8,'frames'=4] {'batch','frames'}, use_global_device_ids=true, to_apply=%region_8.9 | all-reduce | flops 2 | bytes 16 | tf_op jit(solution)/shard_map/psum | solution.py:557
  585.8 2.4 multiply_reduce_fusion.5
  588.1 1.9 pad_maximum_fusion.9
  590.0 13.6 %psum.30 = f32[]{:T(128)} all-reduce(f32[]{:T(128)} %multiply_reduce_fusion.5), channel_id=1, replica_groups=mesh['batch'=8,'frames'=4] {'batch'}, use_global_device_ids=true, to_apply=%region_10.11 | all-reduce | flops 1 | bytes 8 | tf_op jit(solution)/shard_map/psum | solution.py:562
  604.3 3.0 fusion.20
  (248 shorter events, 65.0 us)
Async XLA Ops:
  7.2 3.2 copy-start.31
  7.2 47.5 %all-gather.4.cloned.1.call-start = ((), (), s32[]{:S(2)}) async-start(), calls=%async_computation.1 | async-start | bytes 3912192 | tf_op jit(solution)/shard_map/all_gather | solution.py:428
  9.3 532.3 %all-reduce.25.cloned.1.call-start = ((), (), s32[]{:S(2)}) async-start(), calls=%async_computation.2 | async-start | bytes 6955008
  54.3 9.1 %copy-start.25 = (f32[2000]{0:T(1024)}, f32[2000]{0:T(1024)S(1)}, u32[]{:S(2)}) copy-start(f32[2000]{0:T(1024)S(1)} %mul.412) | copy-start | bytes 24004
  54.6 8.8 %copy-start.27 = (f32[2000]{0:T(1024)}, f32[2000]{0:T(1024)S(1)}, u32[]{:S(2)}) copy-start(f32[2000]{0:T(1024)S(1)} %mul.407) | copy-start | bytes 24004
  62.2 2.0 copy-start.32
  62.2 2.0 copy-start.34
  94.8 4.6 collective-permute-start
  119.3 3.2 collective-permute-start.1
  153.5 3.0 collective-permute-start.2
  157.6 19.2 %copy-start.44 = (s32[2]{0:T(128)S(1)}, s32[2]{0:T(128)}, u32[]{:S(2)}) copy-start(s32[2]{0:T(128)} %param.12) | copy-start | bytes 28
  157.6 19.2 %copy-start.45 = (s32[2]{0:T(128)S(1)}, s32[2]{0:T(128)}, u32[]{:S(2)}) copy-start(s32[2]{0:T(128)} %param.13) | copy-start | bytes 28
  176.5 7.6 %collective-permute-start.3 = (f32[2240,128]{1,0:T(8,128)}, f32[2240,128]{1,0:T(8,128)}, u32[]{:S(2)}, u32[]{:S(2)}) collective-permute-start(f32[2240,128]{1,0:T(8,128)} %get-tuple-element.60), channel_id=1, source_target_pairs={{0,4},{4,0},{8,12},{12,8},{16,20},{20,16},{24,28},{28,24},{1,5},{5... | collective-permute-start | bytes 3440648 | tf_op jit(solution)/shard_map/ppermute | solution.py:474
  181.9 8.7 %copy-start.7 = (f32[2000,64]{0,1:T(8,128)}, f32[2000,64]{0,1:T(8,128)S(1)}, u32[]{:S(2)}) copy-start(f32[2000,64]{0,1:T(8,128)S(1)} %copy.119) | copy-start | bytes 1536004
  183.8 5.0 copy-start.4
  190.6 2.9 copy-start.6
  193.5 32.3 %copy-start.1 = (f32[2000,3,64]{0,2,1:T(8,128)}, f32[2000,3,64]{0,2,1:T(8,128)S(1)}, u32[]{:S(2)}) copy-start(f32[2000,3,64]{0,2,1:T(8,128)S(1)} %get-tuple-element.158) | copy-start | bytes 4608004
  240.9 5.8 slice-start
  251.2 3.4 copy-start.8
  257.5 3.6 copy-start.2
  261.5 1.6 copy-start.5
  289.1 3.1 collective-permute-start.4
  293.2 41.3 %copy-start = (f32[2000,3,64]{2,1,0:T(4,128)S(1)}, f32[2000,3,64]{2,1,0:T(4,128)}, u32[]{:S(2)}) copy-start(f32[2000,3,64]{2,1,0:T(4,128)} %reshape.461) | copy-start | bytes 4608004
  331.4 14.2 %collective-permute-start.5 = (f32[2240,128]{1,0:T(8,128)}, f32[2240,128]{1,0:T(8,128)}, u32[]{:S(2)}, u32[]{:S(2)}) collective-permute-start(f32[2240,128]{1,0:T(8,128)} %get-tuple-element.69.refs_2_), channel_id=1, source_target_pairs={{0,4},{4,0},{8,12},{12,8},{16,20},{20,16},{24,28},{28,24},{1,5},{5... | collective-permute-start | bytes 3440648 | tf_op jit(solution)/shard_map/ppermute | solution.py:474
  336.2 5.2 copy-start.29
  336.2 5.2 copy-start.19
  337.0 4.5 copy-start.21
  337.0 5.3 copy-start.9
  340.6 2.0 copy-start.40
  340.6 2.7 copy-start.30
  340.6 2.8 copy-start.20
  341.4 2.2 copy-start.22
  341.4 3.4 copy-start.41
  345.6 25.9 %copy-start.36 = (f32[1,512]{1,0:T(1,128)S(1)}, f32[1,512]{1,0:T(1,128)}, u32[]{:S(2)}) copy-start(f32[1,512]{1,0:T(1,128)} %slice.373) | copy-start | bytes 6148
  371.2 3.0 copy-start.24
  371.3 4.7 collective-permute-start.6
  377.0 38.8 %copy-start.43 = (f32[2]{0:T(128)S(1)}, f32[2]{0:T(128)}, u32[]{:S(2)}) copy-start(f32[2]{0:T(128)} %pad_maximum_fusion.8) | copy-start | bytes 28
  414.9 3.4 copy-start.23
  415.8 3.3 copy-start.11
  431.6 1.5 copy-start.39
  431.6 1.6 copy-start.37
  431.6 1.6 copy-start.38
  431.6 1.6 copy-start.42
  466.4 77.3 %copy-start.46 = (s32[2]{0:T(128)S(1)}, s32[2]{0:T(128)}, u32[]{:S(2)}) copy-start(s32[2]{0:T(128)} %param.13) | copy-start | bytes 28
  466.4 137.9 %copy-start.10 = (f32[108672]{0:T(1024)S(1)}, f32[108672]{0:T(1024)}, u32[]{:S(2)}) copy-start(f32[108672]{0:T(1024)} %param.7) | copy-start | bytes 1304068
  466.4 137.9 %copy-start.17 = (f32[108672]{0:T(1024)S(1)}, f32[108672]{0:T(1024)}, u32[]{:S(2)}) copy-start(f32[108672]{0:T(1024)} %param.8) | copy-start | bytes 1304068
  466.4 137.9 %copy-start.18 = (f32[108672]{0:T(1024)S(1)}, f32[108672]{0:T(1024)}, u32[]{:S(2)}) copy-start(f32[108672]{0:T(1024)} %param.9) | copy-start | bytes 1304068
  466.4 119.3 %all-reduce.23.cloned.1.call-start = ((), (), s32[]{:S(2)}) async-start(), calls=%async_computation | async-start | bytes 876544 | tf_op jit(solution)/shard_map/psum | solution.py:561
  (11 other events, 9.9 us)
Sparse Core Ops, SparseCore 0:
  10.5 36.4 all-gather.3
  466.5 75.1 all-reduce.24
  544.6 37.7 all-reduce.22
where the time goes:
time: 623 us; the launch traced here: 615 us
  Pallas kernels  221 us (35%)
  local copies, waits for them, and re-layouts  134 us (22%)
  blocking collectives  96.9 us (16%)
  waiting for transfers between devices  75.5 us (12%)
  other arithmetic  42.8 us (7%)
  between operations  21.3 us (3%)
  matrix products  21.1 us (3%)
    pallas_call x4, Pallas kernels, run_backward(): pl.pallas_call(functools.partial(backward_kernel, inter, last_layer, grou...  126 us
    pallas_call x4, Pallas kernels, run_forward(): pl.pallas_call(functools.partial(forward_kernel, inter, first_layer, grou...  95.6 us
    unnamed x4, waiting for transfers between devices  73.5 us
    psum x1, blocking collectives, local(): lax.psum((loss_local * lead, jnp.sum(lengths).astype(F32) / frames_size),...  40.1 us
    all_gather x1, blocking collectives, local(): signals = lax.all_gather(signals, 'frames', axis=2, tiled=True)  38.9 us
    concatenate x1, local copies, waits for them, and re-layouts, local(): jnp.concatenate([grad_encoder.reshape(-1)] + layer_grads + [lead * grad_m...  33.1 us
    unnamed x113, local copies, waits for them, and re-layouts  16 us
    psum x1, blocking collectives, local(): grad_norm = jnp.sqrt(lax.psum(jnp.sum(shard * shard), 'batch'))  13.6 us
  transfers between devices with their start and end apart: 10, of which 2 were waited for; matrix products, arithmetic and copies ran while one was open for 6% of the time, Pallas kernels for 0%

commit v1 on v0

v1 whole, which is shorter than its diff:
```python
import functools
import math

import jax
import jax.numpy as jnp
from jax import lax
from jax.experimental import pallas as pl
from jax.experimental.pallas import tpu as pltpu
from jax.sharding import PartitionSpec as P

FILTERS = 64
UNITS = 128
HOP = 50
HALF_PAD = 56
SOURCES = 3
BLOCKS = 2
STEP = 5
GATES = 4 * UNITS

HIGHEST = lax.Precision.HIGHEST
NORM_EPS = 1e-08
CLIP_AT = 0.001
BETA_ONE = 0.5
BETA_TWO = 0.5
LEARN_RATE = 0.05
DECAY_RATE = 0.01
ADAM_EPS = 1e-08
F32 = jnp.float32
BF16 = jnp.bfloat16
VMEM_MAX = 60 * 2**20


def split(a):
    hi = a.astype(BF16)
    return hi, (a - hi.astype(F32)).astype(BF16)


def dot(a, b):
    return jnp.dot(a, b, preferred_element_type=F32)


def dot3(a, w_twice, w_low):
    hi, lo = split(a)
    return dot(jnp.concatenate([hi, lo], 1), w_twice) + dot(hi, w_low)


def dot_rows(a, b):
    return lax.dot_general(a, b, (((0,), (0,)), ((), ())), preferred_element_type=F32)


def dot_rows3(a, b):
    a_hi, a_lo = split(a)
    b_hi, b_lo = split(b)
    return dot_rows(a_hi, b_hi) + dot_rows(a_lo, b_hi) + dot_rows(a_hi, b_lo)


SIDE_ROWS = 772
PROJ_ROWS = 2 * SIDE_ROWS
VEC_ROW = PROJ_ROWS + 128
LAYER_ROWS = 1680
HEAD_ROWS = 160
WINDOW = 1688


def window(layer_no):
    at = 2 + 3347 * layer_no
    return at // 16 * 8, at // 2 % 8, at % 2


def pick(ref, base, odd, start, count, stride=1):
    def load(at):
        return ref[pl.ds(at, count, stride=stride), :] if stride > 1 else ref[pl.ds(at, count), :]

    first = load(base + start)
    if not odd:
        return first
    return jnp.concatenate([first[:, 64:], load(base + start + 1)[:, :64]], 1)


def load_weights(ref, base, odd, dir_no, proj_s):
    at = SIDE_ROWS * dir_no
    win = jnp.concatenate([pick(ref, base, odd, at + q, FILTERS, 4) for q in range(4)], 1)
    wrec = jnp.concatenate([pick(ref, base, odd, at + 256 + q, UNITS, 4) for q in range(4)], 1)
    bias = jnp.concatenate([pick(ref, base, odd, at + 768 + q, 1) for q in range(4)], 1)
    pairs = pick(ref, base, odd, PROJ_ROWS + 64 * dir_no, 64)
    proj_s[pl.ds(0, 64, stride=2), :] = pairs
    proj_s[pl.ds(1, 64, stride=2), :] = pltpu.roll(pairs, 64, 1)
    return win, wrec, bias, proj_s[:, :FILTERS]


def load_vec(ref, base, odd):
    first = pick(ref, base, odd, VEC_ROW, 1)
    turned = pltpu.roll(jnp.broadcast_to(first, (8, 128)), 64, 1)[0:1]
    if odd:
        last = ref[base + VEC_ROW + 1:base + VEC_ROW + 2, :]
        last = jnp.concatenate([last[:, 64:], last[:, 64:]], 1)
    else:
        last = ref[base + VEC_ROW + 1:base + VEC_ROW + 2, :]
        last = jnp.concatenate([last[:, :64], last[:, :64]], 1)
    low = lax.broadcasted_iota(jnp.int32, (1, 128), 1) < 64
    return jnp.where(low, first, turned), jnp.where(low, turned, first), last


def put_split(w, twice_ref, low_ref):
    hi, lo = split(w)
    twice_ref[...] = jnp.concatenate([hi, hi], 0)
    low_ref[...] = lo


def place(dir_no, chunk_no, count, steps, inter, groups):
    first = jnp.where(dir_no == 0, chunk_no * steps, (count - 1 - chunk_no) * steps)
    if inter:
        return first, 0, 0
    half = first // HOP
    return first, half, pl.multiple_of((first - HOP * half) * groups, 8)


def norm_stage(prev_ref, pa_ref, pb_ref, flat_ref, base, odd, valid, normed_ref, scale_ref, x_ref):
    offset, gain, shift = load_vec(flat_ref, base, odd)
    mixed = pa_ref[:valid] + pb_ref[:valid] + offset
    total = 2.0 * valid * FILTERS
    mean = jnp.sum(mixed) / total
    spread = jnp.sum(mixed * mixed) / total - mean * mean
    scale = lax.rsqrt(jnp.full((1, 128), spread + NORM_EPS, F32))
    normed = (mixed - mean) * scale
    normed_ref[:valid] = normed
    normed_ref[valid:] = jnp.zeros((normed_ref.shape[0] - valid, 128), F32)
    x_ref[:valid] = prev_ref[:valid] + gain * normed + shift
    x_ref[valid:] = jnp.zeros((x_ref.shape[0] - valid, 128), F32)
    scale_ref[...] = jnp.broadcast_to(scale, scale_ref.shape)


def forward_kernel(layer_no, groups, steps, *refs):
    inter = layer_no % 2 == 1
    first_layer = layer_no == 0
    if first_layer:
        (dir_ref, x_ref, flat_ref,
         h_ref, coef_ref, part_ref,
         wi2, wil, wr2, wrl, pj2, pjl, proj_s, bias_s, gin, c_s, h_s) = refs
    else:
        (dir_ref, prev_ref, pa_ref, pb_ref, below_ref, flat_ref,
         x_ref, normed_ref, scale_ref, h_ref, coef_ref, part_ref,
         wi2, wil, wr2, wrl, pj2, pjl, proj_s, bias_s, gin, c_s, h_s) = refs
    chunk_no = pl.program_id(0)
    count = pl.num_programs(0)
    dir_no = dir_ref[0]
    rows = 2 * HALF_PAD if inter else groups
    valid = HOP * groups

    @pl.when(chunk_no == 0)
    def _():
        column = lax.broadcasted_iota(jnp.int32, (1, GATES), 1)
        scaling = jnp.where((column >= 2 * UNITS) & (column < 3 * UNITS), 1.0, 0.5)
        _, base, odd = window(layer_no)
        win, wrec, bias, proj = load_weights(flat_ref, base, odd, dir_no, proj_s)
        win = win * scaling
        none = jnp.zeros_like(win)
        for half in range(2):
            put_split(jnp.concatenate([win, none] if half == 0 else [none, win], 0), wi2.at[half], wil.at[half])
        put_split(wrec * scaling, wr2, wrl)
        bias_s[...] = jnp.broadcast_to(bias * scaling, bias_s.shape)
        none = jnp.zeros_like(proj)
        for half in range(2):
            put_split(jnp.concatenate([proj, none] if half == 0 else [none, proj], 1), pj2.at[half], pjl.at[half])
        c_s[...] = jnp.zeros_like(c_s)
        h_s[...] = jnp.zeros_like(h_s)
        h_ref[0] = jnp.zeros((rows, UNITS), F32)
        h_ref[h_ref.shape[0] - 1] = jnp.zeros((rows, UNITS), F32)
        if not first_layer:
            _, below_base, below_odd = window(layer_no - 1)
            norm_stage(
                prev_ref, pa_ref, pb_ref, below_ref, below_base, below_odd, valid, normed_ref, scale_ref, x_ref
            )

    first, half, row = place(dir_no, chunk_no, count, steps, inter, groups)
    if inter:
        xs = jnp.concatenate(
            [x_ref[pl.ds(first + u, HALF_PAD, stride=groups), :] for u in range(steps)], 0
        )
        for side in range(2):
            found = dot3(xs, wi2[side], wil[side]) + bias_s[0:1]
            for u in range(steps):
                gin[pl.ds(u * rows + side * HALF_PAD, HALF_PAD)] = found[u * HALF_PAD:(u + 1) * HALF_PAD]
    else:
        xs = x_ref[pl.ds(row, steps * groups), :]
        gin[...] = dot3(xs, wi2[half], wil[half]) + bias_s[0:1]

    h = h_s[...]
    c = c_s[...]
    for u in range(steps):
        v = jnp.where(dir_no == 0, u, steps - 1 - u)
        hi, lo = split(h)
        z = (
            gin[pl.ds(pl.multiple_of(v * rows, 8), rows)]
            + dot(jnp.concatenate([hi, lo], 1), wr2[...])
            + dot(hi, wrl[...])
        )
        th = jnp.tanh(z)
        ti, tf, g, to = (th[:, q * UNITS:(q + 1) * UNITS] for q in range(4))
        i_g = 0.5 * ti + 0.5
        f_g = 0.5 * tf + 0.5
        o_g = 0.5 * to + 0.5
        c_prev = c
        c = f_g * c + i_g * g
        tc = jnp.tanh(c)
        h = o_g * tc
        h_ref[first + v + 1] = h
        coef_ref[u, 0] = tc * (0.25 - 0.25 * to * to)
        coef_ref[u, 1] = o_g * (1.0 - tc * tc)
        coef_ref[u, 2] = g * (0.25 - 0.25 * ti * ti)
        coef_ref[u, 3] = c_prev * (0.25 - 0.25 * tf * tf)
        coef_ref[u, 4] = i_g * (1.0 - g * g)
        coef_ref[u, 5] = f_g
    h_s[...] = h
    c_s[...] = c

    hs = h_ref[pl.ds(first + 1, steps)]
    if inter:
        low_half = hs[:, :HALF_PAD].reshape(steps * HALF_PAD, UNITS)
        top_half = hs[:, HALF_PAD:].reshape(steps * HALF_PAD, UNITS)
        found = dot3(low_half, pj2[0], pjl[0]) + dot3(top_half, pj2[1], pjl[1])
        for u in range(steps):
            part_ref[pl.ds(first + u, HALF_PAD, stride=groups), :] = found[u * HALF_PAD:(u + 1) * HALF_PAD]
    else:
        found = dot3(hs.reshape(steps * groups, UNITS), pj2[half], pjl[half])
        here = pl.ds(row, steps * groups)

        @pl.when(2 * chunk_no < count)
        def _():
            part_ref[here] = found

        @pl.when(2 * chunk_no >= count)
        def _():
            part_ref[here] = part_ref[here] + found


def backward_kernel(layer_no, groups, steps, *refs):
    inter = layer_no % 2 == 1
    last_layer = layer_no == 2 * BLOCKS - 1
    if last_layer:
        (dir_ref, g_ref, hg_ref, normed_ref, scale_ref, x_ref, h_ref, coef_ref, flat_ref,
         dx_ref, grad_ref,
         wi2, wil, wrw, wrt, pj2, pjl, proj_s, dmx, dhc, dzs, dz_s, dc_s, awin, aproj, abias) = refs
    elif layer_no:
        (dir_ref, res_ref, da_ref, db2_ref, normed_ref, scale_ref, x_ref, h_ref, coef_ref, flat_ref,
         g_ref, dx_ref, grad_ref,
         wi2, wil, wrw, wrt, pj2, pjl, proj_s, dmx, dhc, dzs, dz_s, dc_s, awin, aproj, abias) = refs
    else:
        (dir_ref, res_ref, da_ref, db2_ref, column_ref, denc_ref, encoder_ref, loss_ref,
         normed_ref, scale_ref, x_ref, h_ref, coef_ref, flat_ref,
         grad_ref,
         wi2, wil, wrw, wrt, pj2, pjl, proj_s, dmx, dhc, dzs, dz_s, dc_s, awin, aproj, abias, g_ref, dx_ref) = refs
    back_no = pl.program_id(0)
    count = pl.num_programs(0)
    chunk_no = count - 1 - back_no
    dir_no = dir_ref[0]
    rows = 2 * HALF_PAD if inter else groups
    valid = HOP * groups

    @pl.when(back_no == 0)
    def _():
        _, base, odd = window(layer_no)
        win, wrec, _, proj = load_weights(flat_ref, base, odd, dir_no, proj_s)
        win_t = win.T
        none = jnp.zeros_like(win_t)
        for half in range(2):
            put_split(jnp.concatenate([win_t, none] if half == 0 else [none, win_t], 1), wi2.at[half], wil.at[half])
        hi, lo = split(wrec.T)
        wrw[...] = jnp.concatenate([hi, lo], 1)
        wrt[...] = hi
        proj_t = proj.T
        none = jnp.zeros_like(proj_t)
        for half in range(2):
            put_split(jnp.concatenate([proj_t, none] if half == 0 else [none, proj_t], 0), pj2.at[half], pjl.at[half])
        dz_s[...] = jnp.zeros_like(dz_s)
        dc_s[...] = jnp.zeros_like(dc_s)
        awin[...] = jnp.zeros_like(awin)
        aproj[...] = jnp.zeros_like(aproj)
        abias[...] = jnp.zeros_like(abias)
        grad_ref[...] = jnp.zeros_like(grad_ref)
        if not last_layer:
            g_ref[:valid] = res_ref[:valid] + da_ref[:valid] + db2_ref[:valid]
            g_ref[valid:] = jnp.zeros((g_ref.shape[0] - valid, 128), F32)
        g = g_ref[:valid]
        normed = normed_ref[:valid]
        _, gain, _ = load_vec(flat_ref, base, odd)
        g_n = g * gain
        total = 2.0 * valid * FILTERS
        mean_one = jnp.sum(g_n) / total
        mean_two = jnp.sum(g_n * normed) / total
        dmixed = scale_ref[0:1] * (g_n - mean_one - normed * mean_two)
        dmx[:valid] = dmixed
        dmx[valid:] = jnp.zeros((dmx.shape[0] - valid, 128), F32)
        lead = jnp.where(dir_no == 0, 1.0, 0.0)

        def fold(array):
            found = lead * jnp.sum(array, 0, keepdims=True)
            return found[:, :FILTERS] + found[:, FILTERS:]

        grad_ref[VEC_ROW:VEC_ROW + 1] = jnp.concatenate([fold(dmixed), fold(g * normed)], 1)
        grad_ref[VEC_ROW + 1:VEC_ROW + 2] = jnp.concatenate([fold(g), jnp.zeros((1, FILTERS), F32)], 1)
        if last_layer:
            grad_ref[LAYER_ROWS:] = hg_ref[...] * lead

    first, half, row = place(dir_no, chunk_no, count, steps, inter, groups)
    here = pl.ds(row, steps * groups)
    if inter:
        dms = jnp.concatenate(
            [dmx[pl.ds(first + u, HALF_PAD, stride=groups), :] for u in range(steps)], 0
        )
        for side in range(2):
            found = dot3(dms, pj2[side], pjl[side])
            for u in range(steps):
                dhc[pl.ds(u * rows + side * HALF_PAD, HALF_PAD)] = found[u * HALF_PAD:(u + 1) * HALF_PAD]
    else:
        dms = dmx[here, :]
        dhc[...] = dot3(dms, pj2[half], pjl[half])

    dz = dz_s[...]
    dc_next = dc_s[...]
    for u in reversed(range(steps)):
        v = jnp.where(dir_no == 0, u, steps - 1 - u)
        hi, lo = split(dz)
        wide = dot(hi, wrw[...])
        dh = (
            dhc[pl.ds(pl.multiple_of(v * rows, 8), rows)]
            + wide[:, :UNITS] + wide[:, UNITS:] + dot(lo, wrt[...])
        )
        dc = dh * coef_ref[u, 1] + dc_next
        dz = jnp.concatenate(
            [dc * coef_ref[u, 2], dc * coef_ref[u, 3], dc * coef_ref[u, 4], dh * coef_ref[u, 0]], 1
        )
        dc_next = dc * coef_ref[u, 5]
        if inter:
            dzs[0, pl.ds(pl.multiple_of(v * HALF_PAD, 8), HALF_PAD)] = dz[:HALF_PAD]
            dzs[1, pl.ds(pl.multiple_of(v * HALF_PAD, 8), HALF_PAD)] = dz[HALF_PAD:]
        else:
            dzs[0, pl.ds(pl.multiple_of(v * rows, 8), rows)] = dz
    dz_s[...] = dz
    dc_s[...] = dc_next

    hs = h_ref[pl.ds(first + 1, steps)]
    hp = h_ref[pl.ds(first + 2 * dir_no, steps)]
    if inter:
        xs = jnp.concatenate(
            [x_ref[pl.ds(first + u, HALF_PAD, stride=groups), :] for u in range(steps)], 0
        )
        found = 0.0
        for side in range(2):
            cut = slice(side * HALF_PAD, (side + 1) * HALF_PAD)
            dzc = dzs[side]
            found = found + dot3(dzc, wi2[side], wil[side])
            turned = xs if side == 0 else pltpu.roll(xs, FILTERS, 1)
            awin[...] += dot_rows3(
                jnp.concatenate([turned, hp[:, cut].reshape(steps * HALF_PAD, UNITS)], 1), dzc
            )
            aproj[side] += dot_rows3(hs[:, cut].reshape(steps * HALF_PAD, UNITS), dms)
            abias[0:1] += jnp.sum(dzc, 0, keepdims=True)
        for u in range(steps):
            dx_ref[pl.ds(first + u, HALF_PAD, stride=groups), :] = found[u * HALF_PAD:(u + 1) * HALF_PAD]
    else:
        xs = x_ref[here, :]
        dzc = dzs[0]
        turned = jnp.where(half == 0, xs, pltpu.roll(xs, FILTERS, 1))
        awin[...] += dot_rows3(jnp.concatenate([turned, hp.reshape(steps * groups, UNITS)], 1), dzc)
        aproj[half] += dot_rows3(hs.reshape(steps * groups, UNITS), dms)
        abias[0:1] += jnp.sum(dzc, 0, keepdims=True)
        found = dot3(dzc, wi2[half], wil[half])

        @pl.when(2 * back_no < count)
        def _():
            dx_ref[here] = found

        @pl.when(2 * back_no >= count)
        def _():
            dx_ref[here] = dx_ref[here] + found

    @pl.when(back_no == count - 1)
    def _():
        at = SIDE_ROWS * dir_no
        for q in range(4):
            cut = slice(q * UNITS, (q + 1) * UNITS)
            grad_ref[pl.ds(at + q, FILTERS, stride=4), :] = awin[:FILTERS, cut]
            grad_ref[pl.ds(at + 256 + q, UNITS, stride=4), :] = awin[2 * FILTERS:, cut]
            grad_ref[pl.ds(at + 768 + q, 1), :] = abias[0:1, cut]
        proj_s[...] = aproj[0] + pltpu.roll(aproj[1], FILTERS, 1)
        even = proj_s[pl.ds(0, 64, stride=2), :]
        odd_rows = proj_s[pl.ds(1, 64, stride=2), :]
        grad_ref[pl.ds(PROJ_ROWS + 64 * dir_no, 64), :] = jnp.concatenate(
            [even[:, :FILTERS], odd_rows[:, :FILTERS]], 1
        )
        if layer_no == 0:
            lead = jnp.where(dir_no == 0, 1.0, 0.0)
            streams = lead * g_ref[:valid] + dx_ref[:valid]
            column = column_ref[...]
            mix, following = column[:, 0:1], column[:, 1:2]
            raw = mix * encoder_ref[0:1] + following * encoder_ref[1:2]
            group_at = lax.broadcasted_iota(jnp.int32, (valid, FILTERS), 0) % groups
            shifted = jnp.where(group_at == 0, 0.0, pltpu.roll(pltpu.roll(streams, FILTERS, 1), 1, 0)[:, :FILTERS])
            grad_raw = (streams[:, :FILTERS] + shifted + lead * denc_ref[...]) * jax.nn.sigmoid(raw)
            grad_ref[LAYER_ROWS:LAYER_ROWS + 1] = jnp.concatenate(
                [jnp.sum(grad_raw * mix, 0, keepdims=True), jnp.sum(grad_raw * following, 0, keepdims=True)], 1
            )
            grad_ref[LAYER_ROWS + 1:LAYER_ROWS + 2] = loss_ref[0:1] * lead


def head_kernel(groups, prev_ref, pa_ref, pb_ref, below_ref, stream_ref, column_ref, active_ref, masker_ref, decoder_ref,
                normed_ref, scale_ref, g_ref, hg_ref, denc_ref, loss_ref,
                sep, sig_s, now_s, before_s, slope_s, mk2, mkl, mt2, mtl, dk2, dkl, dt2, dtl, amask, adec, m_low, m_top):
    valid = HOP * groups
    block = 10 * groups
    _, below_base, below_odd = window(2 * BLOCKS - 1)
    norm_stage(prev_ref, pa_ref, pb_ref, below_ref, below_base, below_odd, valid, normed_ref, scale_ref, sep)
    put_split(masker_ref[...], mk2, mkl)
    put_split(masker_ref[...].T, mt2, mtl)
    put_split(decoder_ref[...], dk2, dkl)
    put_split(decoder_ref[...].T, dt2, dtl)
    amask[...] = jnp.zeros_like(amask)
    adec[...] = jnp.zeros_like(adec)
    active = active_ref[0:1]

    def rows(n):
        return pl.ds(pl.multiple_of(n * block, 8), block)

    def summed_of(n):
        here = sep[rows(n), :]
        group_at = lax.broadcasted_iota(jnp.int32, (block, FILTERS), 0) % groups
        shifted = pltpu.roll(pltpu.roll(here, FILTERS, 1), 1, 0)[:, :FILTERS]
        return here[:, :FILTERS] + jnp.where(group_at == 0, 0.0, shifted)

    def frames_of(n):
        encoded = stream_ref[rows(n), :][:, :FILTERS]
        return jnp.concatenate([encoded, encoded, encoded], 1)

    def ahead(n, carry):
        logits = dot3(summed_of(n), mk2[...], mkl[...])
        sig = jax.nn.sigmoid(logits)
        sig_s[rows(n), :] = sig
        both = dot3(sig * active * frames_of(n), dk2[...], dkl[...])
        now_s[rows(n), :] = both[:, :128]
        before_s[pl.ds(pl.multiple_of(n * block + groups, 8), block), :] = both[:, 128:]
        return carry

    lax.fori_loop(0, HOP // 10, ahead, 0)
    at = lax.broadcasted_iota(jnp.int32, (groups, 128), 0)
    before_s[:groups] = jnp.where(at == 0, 0.0, pltpu.roll(before_s[valid:], 1, 0))

    def losses(n, total):
        column = column_ref[rows(n), :]
        lane = lax.broadcasted_iota(jnp.int32, (block, 128), 1)
        target = jnp.where(lane < SOURCES, column, 0.0)
        kept = jnp.broadcast_to(column[:, SOURCES:SOURCES + 1], (block, 128))
        differ = now_s[rows(n), :] + before_s[rows(n), :] - target
        root = jnp.sqrt(differ * differ + 1.0)
        slope_s[rows(n), :] = kept * differ / root
        return total + jnp.sum(kept * (root - 1.0), 0, keepdims=True)

    total = lax.fori_loop(0, HOP // 10, losses, jnp.zeros((1, 128), F32))
    loss_ref[...] = jnp.broadcast_to(jnp.sum(total, 1, keepdims=True), loss_ref.shape)
    slope_s[valid:] = jnp.where(at == groups - 1, 0.0, pltpu.roll(slope_s[:groups], groups - 1, 0))

    def back(n, carry):
        slopes = jnp.concatenate(
            [slope_s[rows(n), :], slope_s[pl.ds(pl.multiple_of(n * block + groups, 8), block), :]], 1
        )
        sig = sig_s[rows(n), :]
        frames = frames_of(n)
        dmasked = dot3(slopes, dt2[...], dtl[...]) * active
        by_sig = dmasked * sig
        denc_ref[rows(n), :] = (
            by_sig[:, :FILTERS] + by_sig[:, FILTERS:2 * FILTERS] + by_sig[:, 2 * FILTERS:]
        )
        dlogits = by_sig * frames * (1.0 - sig)
        dsummed = dot3(dlogits, mt2[...], mtl[...])
        group_at = lax.broadcasted_iota(jnp.int32, (block, FILTERS), 0) % groups
        shifted = jnp.where(group_at == groups - 1, 0.0, pltpu.roll(dsummed, block - 1, 0))
        g_ref[rows(n), :] = jnp.concatenate([dsummed, shifted], 1)
        amask[...] += dot_rows3(summed_of(n), dlogits)
        adec[...] += dot_rows3(sig * active * frames, slopes)
        return carry

    lax.fori_loop(0, HOP // 10, back, 0)
    g_ref[valid:] = jnp.zeros((g_ref.shape[0] - valid, 128), F32)
    m_low[...] = amask[:, :128]
    m_top[...] = jnp.concatenate([amask[:, 128:], jnp.zeros((FILTERS, FILTERS), F32)], 1)
    low_even, low_odd = m_low[pl.ds(0, 32, stride=2), :], m_low[pl.ds(1, 32, stride=2), :]
    top_even, top_odd = m_top[pl.ds(0, 32, stride=2), :], m_top[pl.ds(1, 32, stride=2), :]
    hg_ref[pl.ds(0, 32, stride=3), :] = low_even
    hg_ref[pl.ds(1, 32, stride=3), :] = jnp.concatenate([top_even[:, :FILTERS], low_odd[:, :FILTERS]], 1)
    hg_ref[pl.ds(2, 32, stride=3), :] = jnp.concatenate([low_odd[:, FILTERS:], top_odd[:, :FILTERS]], 1)
    columns = []
    for tap in range(2):
        found = 0.0
        for j in range(SOURCES):
            found = found + adec[j * FILTERS:(j + 1) * FILTERS, 128 * tap + j:128 * tap + j + 1]
        columns.append(jnp.broadcast_to(found, (FILTERS, 128)))
    lane = lax.broadcasted_iota(jnp.int32, (FILTERS, 128), 1)
    hg_ref[96:HEAD_ROWS] = jnp.where(lane == 0, columns[0], jnp.where(lane == 1, columns[1], 0.0))


def assemble(flat, layers):
    lane = lax.broadcasted_iota(jnp.int32, (FILTERS, 128), 1)
    row = lax.broadcasted_iota(jnp.int32, (FILTERS, 128), 0)
    encoder = jnp.broadcast_to(layers[0][LAYER_ROWS:LAYER_ROWS + 1], (FILTERS, 128))
    first_tap = jnp.sum(jnp.where(lane == row, encoder, 0.0), 1, keepdims=True)
    second_tap = jnp.sum(jnp.where(lane == row + FILTERS, encoder, 0.0), 1, keepdims=True)

    def interleave(a, b):
        return jnp.sum(jnp.where(lane == 2 * row, a, jnp.where(lane == 2 * row + 1, b, 0.0)), 0, keepdims=True)

    flat[0:1] = interleave(first_tap, second_tap)
    for layer_no, ref in enumerate(layers):
        first, inner, odd = window(layer_no)
        base = first + inner
        if odd:
            whole_rows = ref[:LAYER_ROWS - 6]
            turned = pltpu.roll(whole_rows, FILTERS, 1)
            flat[base:base + 1, FILTERS:] = turned[0:1, FILTERS:]
            wide_low = lax.broadcasted_iota(jnp.int32, (LAYER_ROWS - 7, 128), 1) < FILTERS
            flat[base + 1:base + LAYER_ROWS - 6] = jnp.where(wide_low, turned[:-1], turned[1:])
        else:
            flat[base:base + LAYER_ROWS - 6] = ref[:LAYER_ROWS - 6]
    flat[6695:6791] = layers[3][LAYER_ROWS:LAYER_ROWS + 96]
    decoder = layers[3][LAYER_ROWS + 96:LAYER_ROWS + HEAD_ROWS]
    flat[6791:6792] = interleave(decoder[:, 0:1], decoder[:, 1:2])
    flat[6792:] = jnp.zeros((flat.shape[0] - 6792, 128), F32)


def finish_kernel(chips, depths, entries, width, r0, r1, r2, r3, p_ref, m_ref, v_ref,
                  new_ref, half_ref, first_ref, second_ref, stats_ref,
                  flat, pair_in, sent, plane_in, held, depth_in, mine, found, note, depth_notes, notes,
                  pair_sem, plane_sem, depth_sem, spread_sem, note_sem, notes_sem):
    b = lax.axis_index("batch")
    z = lax.axis_index("frames")
    core = lax.rem(b, 2)
    chip = b // 2
    piece = width // depths
    rows = p_ref.shape[0]

    def start(shard):
        return pl.multiple_of(shard * entries // 1024 * 8, 8)

    def send(src, dst, sems, slot, device):
        copy = pltpu.make_async_remote_copy(
            src_ref=src, dst_ref=dst, send_sem=sems.at[0, slot], recv_sem=sems.at[1, slot],
            device_id=device, device_id_type=pl.DeviceIdType.MESH,
        )
        copy.start()
        return copy

    barrier = pltpu.get_barrier_semaphore()
    for step in range(1, 2 * chips):
        pl.semaphore_signal(
            barrier, inc=1, device_id=(lax.rem(b + step, 2 * chips), z), device_id_type=pl.DeviceIdType.MESH
        )
    for step in range(1, depths):
        pl.semaphore_signal(
            barrier, inc=1, device_id=(b, lax.rem(z + step, depths)), device_id_type=pl.DeviceIdType.MESH
        )
    assemble(flat, (r0, r1, r2, r3))
    note[...] = jnp.broadcast_to(r0[LAYER_ROWS + 1:LAYER_ROWS + 2], note.shape)
    pl.semaphore_wait(barrier, 2 * chips - 1 + depths - 1)

    order = list(range(1, chips)) + [0]
    pairs = {}
    for step in order:
        other = 2 * lax.rem(chip + step, chips) + 1 - core
        pairs[step] = send(
            flat.at[pl.ds(start(other), width)], pair_in.at[step], pair_sem, step, (2 * chip + 1 - core, z)
        )
    loss_copies = [
        send(note, depth_notes.at[step - 1], note_sem, step - 1, (b, lax.rem(z + step, depths)))
        for step in range(1, depths)
    ]
    planes = []
    for step in order:
        pairs[step].wait_recv()
        owner = 2 * lax.rem(chip + step, chips) + core
        total = flat[pl.ds(start(owner), width), :] + pair_in[step]
        if step:
            sent[step - 1] = total
            planes.append(send(sent.at[step - 1], plane_in.at[step - 1], plane_sem, step - 1, (owner, z)))
        else:
            held[...] = total
    for step in order:
        pairs[step].wait_send()
    total = held[...]
    for step in range(1, chips):
        planes[step - 1].wait()
        total = total + plane_in[step - 1]
    held[...] = total
    copies = []
    for step in range(1, depths):
        other = lax.rem(z + step, depths)
        copies.append(
            send(held.at[pl.ds(pl.multiple_of(other * piece, 8), piece)], depth_in.at[step - 1], depth_sem, step - 1, (b, other))
        )
    here = pl.ds(pl.multiple_of(z * piece, 8), piece)
    total = held[here, :]
    for step in range(1, depths):
        copies[step - 1].wait()
        total = total + depth_in[step - 1]
    mine[...] = total
    copies = [
        send(mine, found.at[here], spread_sem, step - 1, (b, lax.rem(z + step, depths)))
        for step in range(1, depths)
    ]
    losses = note[...]
    for step in range(1, depths):
        loss_copies[step - 1].wait()
        losses = losses + depth_notes[step - 1]
    for copy in copies:
        copy.wait()
    found[here, :] = mine[...]

    at = b * entries - start(b) * 128
    row_at, lane_at = at // 128, lax.rem(at, 128)
    gradient = found[pl.ds(row_at, rows), :]
    counted = gradient
    if entries % 128:
        lane = lax.broadcasted_iota(jnp.int32, (rows, 128), 1)
        row = lax.broadcasted_iota(jnp.int32, (rows, 128), 0)
        turn = lax.rem(128 - lane_at, 128)
        gradient = jnp.where(
            lane < 128 - lane_at, pltpu.roll(gradient, turn, 1), pltpu.roll(found[pl.ds(row_at + 1, rows), :], turn, 1)
        )
        counted = jnp.where(128 * row + lane < entries, gradient, 0.0)
    squares = jnp.sum(jnp.sum(counted * counted, 0, keepdims=True), 1, keepdims=True)
    lane = lax.broadcasted_iota(jnp.int32, note.shape, 1)
    note[...] = jnp.where(lane == 2, squares, losses)
    copies = [
        send(note, notes.at[b], notes_sem, step - 1, (lax.rem(b + step, 2 * chips), z))
        for step in range(1, 2 * chips)
    ]
    for copy in copies:
        copy.wait()
    notes[b] = note[...]
    totals = notes[0]
    for other in range(1, 2 * chips):
        totals = totals + notes[other]
    count = jnp.sum(jnp.where(lane == 1, totals, 0.0), 1, keepdims=True)[0:1]
    norm = jnp.sqrt(jnp.sum(jnp.where(lane == 2, totals, 0.0), 1, keepdims=True)[0:1]) / count
    stats_ref[...] = jnp.where(lane == 2, norm, totals)
    clipped = gradient / count * (CLIP_AT / jnp.maximum(norm, CLIP_AT))
    new_first = BETA_ONE * m_ref[...] + (1.0 - BETA_ONE) * clipped
    new_second = BETA_TWO * v_ref[...] + (1.0 - BETA_TWO) * clipped * clipped
    step_size = (
        new_first / (1.0 - BETA_ONE**STEP) / (jnp.sqrt(new_second / (1.0 - BETA_TWO**STEP)) + ADAM_EPS)
    )
    params = p_ref[...]
    new_params = params - LEARN_RATE * (step_size + DECAY_RATE * params)
    new_ref[...] = new_params
    half_ref[...] = new_params.astype(BF16)
    first_ref[...] = new_first
    second_ref[...] = new_second


def sizes(inter, groups):
    if inter:
        return groups, 2 * HALF_PAD, 8
    return 2 * HOP, groups, 10


def whole(shape):
    return pl.BlockSpec(shape, lambda j: (0,) * len(shape))


def layer_spec(layer_no):
    first, _, _ = window(layer_no)
    return pl.BlockSpec((pl.Element(WINDOW), pl.Element(128)), lambda j: (first, 0))


def run_forward(layer_no, groups, dir_no, stream, flat):
    inter = layer_no % 2 == 1
    length, rows, steps = sizes(inter, groups)
    stream_shape = (HALF_PAD * groups, 128)
    coef_block = (steps, 6, rows, UNITS)
    out = [
        ((length + 2, rows, UNITS), whole((length + 2, rows, UNITS))),
        ((length, 6, rows, UNITS), pl.BlockSpec(coef_block, lambda j: (j, 0, 0, 0))),
        (stream_shape, whole(stream_shape)),
    ]
    layers = [layer_no]
    if layer_no:
        out = [(stream_shape, whole(stream_shape)), (stream_shape, whole(stream_shape)), ((8, 128), whole((8, 128)))] + out
        layers = [layer_no - 1, layer_no]
    return pl.pallas_call(
        functools.partial(forward_kernel, layer_no, groups, steps),
        grid=(length // steps,),
        in_specs=[pl.BlockSpec(memory_space=pltpu.SMEM)]
        + [whole(a.shape) for a in stream]
        + [layer_spec(n) for n in layers],
        out_specs=[spec for _, spec in out],
        out_shape=[jax.ShapeDtypeStruct(shape, F32) for shape, _ in out],
        scratch_shapes=[
            pltpu.VMEM((2, 256, GATES), BF16), pltpu.VMEM((2, 128, GATES), BF16),
            pltpu.VMEM((256, GATES), BF16), pltpu.VMEM((128, GATES), BF16),
            pltpu.VMEM((2, 256, 128), BF16), pltpu.VMEM((2, 128, 128), BF16),
            pltpu.VMEM((UNITS, 128), F32),
            pltpu.VMEM((8, GATES), F32), pltpu.VMEM((steps * rows, GATES), F32),
            pltpu.VMEM((rows, UNITS), F32), pltpu.VMEM((rows, UNITS), F32),
        ],
        compiler_params=pltpu.CompilerParams(vmem_limit_bytes=VMEM_MAX),
        name="forward_inter" if inter else "forward_intra",
    )(dir_no, *stream, *[flat for _ in layers])


def run_backward(layer_no, groups, dir_no, before, coef, flat):
    inter = layer_no % 2 == 1
    last_layer = layer_no == 2 * BLOCKS - 1
    length, rows, steps = sizes(inter, groups)
    stream_shape = (HALF_PAD * groups, 128)
    count = length // steps
    coef_block = (steps, 6, rows, UNITS)
    if last_layer:
        out = [stream_shape, (LAYER_ROWS + HEAD_ROWS, 128)]
    elif layer_no:
        out = [stream_shape, stream_shape, (LAYER_ROWS, 128)]
    else:
        out = [(LAYER_ROWS + 8, 128)]
    streams = [] if layer_no else [pltpu.VMEM(stream_shape, F32), pltpu.VMEM(stream_shape, F32)]
    return pl.pallas_call(
        functools.partial(backward_kernel, layer_no, groups, steps),
        grid=(count,),
        in_specs=[pl.BlockSpec(memory_space=pltpu.SMEM)]
        + [whole(a.shape) for a in before]
        + [pl.BlockSpec(coef_block, lambda j: (count - 1 - j, 0, 0, 0)), layer_spec(layer_no)],
        out_specs=[whole(shape) for shape in out],
        out_shape=[jax.ShapeDtypeStruct(shape, F32) for shape in out],
        scratch_shapes=[
            pltpu.VMEM((2, 2 * GATES, 128), BF16), pltpu.VMEM((2, GATES, 128), BF16),
            pltpu.VMEM((GATES, 256), BF16), pltpu.VMEM((GATES, 128), BF16),
            pltpu.VMEM((2, 256, 128), BF16), pltpu.VMEM((2, 128, 128), BF16),
            pltpu.VMEM((UNITS, 128), F32),
            pltpu.VMEM(stream_shape, F32), pltpu.VMEM((steps * rows, UNITS), F32),
            pltpu.VMEM((2, steps * HALF_PAD, GATES) if inter else (1, steps * rows, GATES), F32),
            pltpu.VMEM((rows, GATES), F32), pltpu.VMEM((rows, UNITS), F32),
            pltpu.VMEM((256, GATES), F32), pltpu.VMEM((2, UNITS, 128), F32), pltpu.VMEM((8, GATES), F32),
        ]
        + streams,
        compiler_params=pltpu.CompilerParams(vmem_limit_bytes=VMEM_MAX),
        name="backward_inter" if inter else "backward_intra",
    )(dir_no, *before, coef, flat)


def run_head(groups, streams, flat, stream, column, active, masker, decoder):
    valid = HOP * groups
    stream_shape = (HALF_PAD * groups, 128)
    first, _, _ = window(2 * BLOCKS - 1)
    out = [stream_shape, (8, 128), stream_shape, (HEAD_ROWS, 128), (valid, FILTERS), (8, 128)]
    wide = SOURCES * FILTERS
    return pl.pallas_call(
        functools.partial(head_kernel, groups),
        grid=(1,),
        in_specs=[whole(a.shape) for a in streams]
        + [layer_spec(2 * BLOCKS - 1)]
        + [whole(a.shape) for a in (stream, column, active, masker, decoder)],
        out_specs=[whole(shape) for shape in out],
        out_shape=[jax.ShapeDtypeStruct(shape, F32) for shape in out],
        scratch_shapes=[
            pltpu.VMEM(stream_shape, F32), pltpu.VMEM((valid, wide), F32), pltpu.VMEM((valid, 128), F32),
            pltpu.VMEM((valid + groups, 128), F32), pltpu.VMEM((valid + groups, 128), F32),
            pltpu.VMEM((2 * FILTERS, wide), BF16), pltpu.VMEM((FILTERS, wide), BF16),
            pltpu.VMEM((2 * wide, FILTERS), BF16), pltpu.VMEM((wide, FILTERS), BF16),
            pltpu.VMEM((2 * wide, 256), BF16), pltpu.VMEM((wide, 256), BF16),
            pltpu.VMEM((512, wide), BF16), pltpu.VMEM((256, wide), BF16),
            pltpu.VMEM((FILTERS, wide), F32), pltpu.VMEM((wide, 256), F32),
            pltpu.VMEM((FILTERS, 128), F32), pltpu.VMEM((FILTERS, 128), F32),
        ],
        compiler_params=pltpu.CompilerParams(vmem_limit_bytes=VMEM_MAX),
        name="head",
    )(*streams, flat, stream, column, active, masker, decoder)


def run_finish(layers, params, first_moment, second_moment):
    entries = params.shape[0]
    rows = -(-entries // 128)
    depths = lax.axis_size("frames")
    chips = lax.axis_size("batch") // 2
    width = -(-(rows + 8) // (8 * depths)) * 8 * depths
    shards = [
        jnp.pad(a, (0, rows * 128 - entries)).reshape(rows, 128) for a in (params, first_moment, second_moment)
    ]
    out = [((rows, 128), F32), ((rows, 128), BF16), ((rows, 128), F32), ((rows, 128), F32), ((8, 128), F32)]
    vmem = pl.BlockSpec(memory_space=pltpu.VMEM)
    block = (width, 128)
    piece = (width // depths, 128)
    sems = pltpu.SemaphoreType.DMA
    found = pl.pallas_call(
        functools.partial(finish_kernel, chips, depths, entries, width),
        in_specs=[vmem] * 7,
        out_specs=[vmem] * 5,
        out_shape=[jax.ShapeDtypeStruct(shape, dtype) for shape, dtype in out],
        scratch_shapes=[
            pltpu.VMEM((6792 + width, 128), F32),
            pltpu.VMEM((chips,) + block, F32), pltpu.VMEM((chips - 1,) + block, F32),
            pltpu.VMEM((chips - 1,) + block, F32), pltpu.VMEM(block, F32),
            pltpu.VMEM((depths - 1,) + piece, F32), pltpu.VMEM(piece, F32), pltpu.VMEM(block, F32),
            pltpu.VMEM((8, 128), F32), pltpu.VMEM((depths - 1, 8, 128), F32), pltpu.VMEM((2 * chips, 8, 128), F32),
            sems((2, chips)), sems((2, chips - 1)), sems((2, depths - 1)), sems((2, depths - 1)),
            sems((2, depths - 1)), sems((2, 2 * chips - 1)),
        ],
        compiler_params=pltpu.CompilerParams(
            vmem_limit_bytes=VMEM_MAX, collective_id=1, has_side_effects=True
        ),
        name="finish",
    )(*layers, *shards)
    return [a.reshape(-1)[:entries] for a in found[:4]] + [found[4]]


def local(params, first_moment, second_moment, mixture, sources, speakers, lengths):
    flat = lax.all_gather(params, "batch", axis=0, tiled=True)
    items = mixture.shape[0]
    frames_size = lax.axis_size("frames")
    samples = mixture.shape[1] * frames_size
    groups = samples // HOP
    core = lax.axis_index("batch") % 2
    depth = lax.axis_index("frames")
    column = 2 * items
    copies = frames_size // column
    mine = depth // copies
    weight = jnp.where(depth % copies == 0, 1.0, 0.0).astype(F32)
    pairs = [[2 * b, 2 * b + 1] for b in range(lax.axis_size("batch") // 2)]
    swap = [(b, b + 1 if b % 2 == 0 else b - 1) for b in range(lax.axis_size("batch"))]

    signals = jnp.concatenate([mixture[:, None], sources], 1)
    signals = lax.all_gather(signals, "frames", axis=2, tiled=True)
    scalars = jnp.stack([speakers, lengths], 1).astype(F32)
    signals = lax.all_gather(signals, "batch", axis=0, tiled=True, axis_index_groups=pairs)
    scalars = lax.all_gather(scalars, "batch", axis=0, tiled=True, axis_index_groups=pairs)
    signal = lax.dynamic_slice_in_dim(signals, mine, 1, 0)[0]
    scalar = lax.dynamic_slice_in_dim(scalars, mine, 1, 0)[0]
    mix = signal[0]
    following = jnp.concatenate([mix[1:], jnp.zeros((1,), F32)])

    def by_row(array):
        return array.reshape(array.shape[:-1] + (groups, HOP)).swapaxes(-1, -2).reshape(array.shape[:-1] + (groups * HOP,))

    mix_row = by_row(mix)
    follow_row = by_row(following)
    encoder = flat[:2 * FILTERS].reshape(FILTERS, 2)
    raw = mix_row[:, None] * encoder[:, 0] + follow_row[:, None] * encoder[:, 1]
    encoded = jax.nn.softplus(raw)

    def later(array):
        three = array.reshape(HOP, groups, -1)
        return jnp.concatenate([three[:, 1:], jnp.zeros_like(three[:, :1])], 1).reshape(array.shape)

    def earlier(array):
        three = array.reshape(HOP, groups, -1)
        return jnp.concatenate([jnp.zeros_like(three[:, :1]), three[:, :-1]], 1).reshape(array.shape)

    pad = ((0, (HALF_PAD - HOP) * groups), (0, 0))
    stream = jnp.pad(jnp.concatenate([encoded, later(encoded)], 1), pad)
    dir_no = core.reshape(1).astype(jnp.int32)
    view = flat.reshape(-1, 128)

    def exchange(array):
        return lax.ppermute(array, "batch", swap)

    kept = []
    below = (stream,)
    for layer_no in range(2 * BLOCKS):
        found = run_forward(layer_no, groups, dir_no, below, view)
        x = found[0] if layer_no else stream
        if layer_no:
            kept[-1][:0] = found[1:3]
        h_all, coef, part = found[-3:]
        kept.append([x, h_all, coef])
        below = (x, part, exchange(part))

    position = by_row(jnp.arange(samples).astype(F32))
    valid = jnp.where(position < scalar[1], 1.0, 0.0) * weight
    active = jnp.where(jnp.arange(SOURCES).astype(F32) < scalar[0], 1.0, 0.0)
    target = by_row(signal[1:]) * active[:, None]
    wide = SOURCES * FILTERS
    masker = flat[-FILTERS * wide - 2 * FILTERS:-2 * FILTERS].reshape(FILTERS, wide)
    decoder = flat[-2 * FILTERS:].reshape(FILTERS, 2)
    column = jnp.pad(jnp.concatenate([target, valid[None]], 0).T, ((0, 0), (0, 124)))
    by_source = jnp.pad(jnp.eye(SOURCES, dtype=F32), ((0, 0), (0, 128 - SOURCES)))
    taps = (by_source[:, None, None, :] * decoder[None, :, :, None]).reshape(wide, 256)
    active_wide = jnp.broadcast_to(jnp.repeat(active, FILTERS)[None], (8, wide))
    normed, scale, grad, head_grads, grad_encoded, loss = run_head(
        groups, below, view, stream, column, active_wide, masker, taps
    )
    kept[-1][:0] = [normed, scale]
    lane = jnp.arange(128)
    count_part = jnp.sum(scalars[:, 1]) / frames_size
    loss = jnp.where(lane == 0, loss, jnp.where(lane == 1, count_part, 0.0))
    signal_column = jnp.pad(jnp.stack([mix_row, follow_row], 1), ((0, 0), (0, 126)))
    encoder_rows = jnp.pad(encoder.T, ((0, 6), (0, 0)))
    sums = [None] * (2 * BLOCKS)
    before = (grad, head_grads)
    for layer_no in reversed(range(2 * BLOCKS)):
        normed, scale, x, h_all, coef = kept[layer_no]
        if layer_no == 0:
            before = before + (signal_column, grad_encoded, encoder_rows, loss)
        found = run_backward(layer_no, groups, dir_no, before + (normed, scale, x, h_all), coef, view)
        sums[layer_no] = found[-1]
        if layer_no == 2 * BLOCKS - 1:
            dx = found[0]
        elif layer_no:
            grad, dx = found[:2]
        if layer_no:
            before = (grad, dx, exchange(dx))
    *updated, stats = run_finish(sums, params, first_moment, second_moment)
    return (*updated, stats[0, 2], stats[0, :2])


def solution(mesh):
    placed = (
        P("batch"),
        P("batch"),
        P("batch"),
        P("batch", "frames"),
        P("batch", None, "frames"),
        P("batch"),
        P("batch"),
    )
    return jax.shard_map(
        local,
        mesh=mesh,
        in_specs=placed,
        out_specs=(P("batch"), P("batch"), P("batch"), P("batch"), P(), P()),
        check_vma=False,
    )
```

time: 623 us -> 410 us (0.66)
  the two profiles are of different devices: /device:TPU:0 before, /device:TPU:25 now
where the time goes in v1:
time: 410 us; the launch traced here: 402 us
  Pallas kernels  296 us (72%)
  blocking collectives  42.7 us (10%)
  local copies, waits for them, and re-layouts  28.1 us (7%)
  between operations  15.4 us (4%)
  waiting for transfers between devices  11 us (3%)
  other arithmetic  6.82 us (2%)
    pallas_call x4, Pallas kernels, run_backward(): pl.pallas_call(functools.partial(backward_kernel, layer_no, groups, steps...  128 us
    pallas_call x4, Pallas kernels, run_forward(): pl.pallas_call(functools.partial(forward_kernel, layer_no, groups, steps)...  96.8 us
    pallas_call x1, Pallas kernels, run_finish(): pl.pallas_call(functools.partial(finish_kernel, chips, depths, entries, w...  55.6 us
    all_gather x1, blocking collectives, local(): signals = lax.all_gather(signals, 'frames', axis=2, tiled=True)  36.9 us
    pallas_call x1, Pallas kernels, run_head(): pl.pallas_call(functools.partial(head_kernel, groups), grid=(1,), in_spec...  14.9 us
    unnamed x35, local copies, waits for them, and re-layouts  14.6 us
    ppermute x7, waiting for transfers between devices, exchange(): return lax.ppermute(array, 'batch', swap)  11 us
  transfers between devices with their start and end apart: 8, of which 4 were waited for; matrix products, arithmetic and copies ran while one was open for 3% of the time, Pallas kernels for 0%

profile of v1, /device:TPU:25, one launch (start us, length us, event | category | flops | bytes accessed | tf_op | source)
XLA Modules:
  0.0 401.8 jit_solution(3406773898225681932)
XLA Ops:
  7.2 2.1 reshape.171
  9.9 0.6 pad_maximum_fusion
  10.5 36.9 %all_gather.12 = f32[2,4,2000]{1,0,2:T(2,128)S(1)} all-gather(f32[2,4,500]{1,0,2:T(2,128)S(1)} %pad_maximum_fusion), channel_id=1, replica_groups=mesh['batch'=8,'frames'=4] {'frames'}, dimensions={2}, use_global_device_ids=true | all-gather | bytes 80000 | tf_op jit(solution)/shard_map/all_gather | solution.py:827
  47.4 1.7 copy.70
  49.2 3.4 all_gather.13
  53.4 0.7 fusion.1
  54.4 0.6 multiply_add_fusion
  55.0 0.6 compare_select_fusion
  55.6 0.7 compare_select_fusion.1
  56.4 1.4 select_maximum_fusion.refs_1_.stream_ref.refs_10_
  57.8 27.7 %forward_intra.2 = (f32[102,40,128]{2,1,0:T(8,128)}, f32[100,6,40,128]{3,2,1,0:T(8,128)}, f32[2240,128]{1,0:T(8,128)}) custom-call(s32[1]{0:T(128)} %bitcast.refs_0_, f32[2240,128]{1,0:T(8,128)} %select_maximum_fusion.refs_1_.stream_ref.refs_10_, f32[6792,128]{1,0:T(8,128)} %bitcast.37), custom_call_target="tpu_custom_call" | custom-call | tf_op jit(solution)/shard_map/forward_intra/pallas_call | solution.py:687
  85.9 2.7 collective-permute-done.refs_3_
  88.5 1.0 copy-done.4
  89.5 19.3 %forward_inter.2 = (f32[2240,128]{1,0:T(8,128)}, f32[2240,128]{1,0:T(8,128)}, f32[8,128]{1,0:T(8,128)}, f32[42,112,128]{2,1,0:T(8,128)}, f32[40,6,112,128]{3,2,1,0:T(8,128)}, /*index=5*/f32[2240,128]{1,0:T(8,128)}) custom-call(s32[1]{0:T(128)} %bitcast.refs_0_, f32[2240,128]{1,0:T(8,128)} %select_maximum_fusion.refs_1_.stream_ref.refs_10_, ...), custom_call_target="tpu_custom_call" | custom-call | tf_op jit(solution)/shard_map/forward_inter/pallas_call | solution.py:687
  109.2 2.7 collective-permute-done.1.refs_3_
  111.8 1.0 copy-done.5
  112.9 30.4 %forward_intra.3 = (f32[2240,128]{1,0:T(8,128)}, f32[2240,128]{1,0:T(8,128)}, f32[8,128]{1,0:T(8,128)}, f32[102,40,128]{2,1,0:T(8,128)}, f32[100,6,40,128]{3,2,1,0:T(8,128)}, /*index=5*/f32[2240,128]{1,0:T(8,128)}) custom-call(s32[1]{0:T(128)} %bitcast.refs_0_, f32[2240,128]{1,0:T(8,128)} %get-tuple-element.47.refs_1_.refs_6_, ...), custom_call_target="tpu_custom_call" | custom-call | tf_op jit(solution)/shard_map/forward_intra/pallas_call | solution.py:687
  143.7 2.3 all-gather.1
  146.7 0.7 fusion
  147.4 1.1 copy-done.1
  148.4 19.4 %forward_inter.3 = (f32[2240,128]{1,0:T(8,128)}, f32[2240,128]{1,0:T(8,128)}, f32[8,128]{1,0:T(8,128)}, f32[42,112,128]{2,1,0:T(8,128)}, f32[40,6,112,128]{3,2,1,0:T(8,128)}, /*index=5*/f32[2240,128]{1,0:T(8,128)}) custom-call(s32[1]{0:T(128)} %bitcast.refs_0_, f32[2240,128]{1,0:T(8,128)} %get-tuple-element.49.refs_1_.refs_6_, ...), custom_call_target="tpu_custom_call" | custom-call | tf_op jit(solution)/shard_map/forward_inter/pallas_call | solution.py:687
  168.1 0.6 compare_select_fusion.3
  169.7 1.1 pad.25.column_ref
  170.9 0.8 slice.91
  172.0 0.7 copy.89
  172.7 0.7 reshape.160.masker_ref
  173.4 0.6 broadcast_in_dim.56.active_ref
  174.4 14.9 %head.1 = (f32[2240,128]{1,0:T(8,128)}, f32[8,128]{1,0:T(8,128)}, f32[2240,128]{1,0:T(8,128)}, f32[160,128]{1,0:T(8,128)}, f32[2000,64]{1,0:T(8,128)}, /*index=5*/f32[8,128]{1,0:T(8,128)}) custom-call(f32[2240,128]{1,0:T(8,128)} %get-tuple-element.51.prev_ref.refs_5_, f32[2240,128]{1,0:T(8,128)} %get-tuple-element.52.pa_ref, f32[2240,128]{1,0:T(8,128)} %copy-done.6, ...), custom_call_target="tpu_custom_call" | custom-call | tf_op jit(solution)/shard_map/head/pallas_call | solution.py:752
  189.3 24.8 %backward_inter.2 = (f32[2240,128]{1,0:T(8,128)}, f32[1840,128]{1,0:T(8,128)}) custom-call(s32[1]{0:T(128)} %bitcast.refs_0_, f32[2240,128]{1,0:T(8,128)} %get-tuple-element.53.refs_1_, f32[160,128]{1,0:T(8,128)} %get-tuple-element.54.refs_2_, f32[2240,128]{1,0:T(8,128)} %get-tuple-element.55.refs_3_, f32[8,128]{1,0:T(8,128)} %get-tuple-element.56.refs_4_, ...), custom_call_target="tpu_custom_call" | custom-call | tf_op jit(solution)/shard_map/backward_inter/pallas_call | solution.py:722
  214.3 2.8 collective-permute-done.4.refs_3_
  217.1 1.0 copy-done.2
  218.2 38.2 %backward_intra.2 = (f32[2240,128]{1,0:T(8,128)}, f32[2240,128]{1,0:T(8,128)}, f32[1680,128]{1,0:T(8,128)}) custom-call(s32[1]{0:T(128)} %bitcast.refs_0_, f32[2240,128]{1,0:T(8,128)} %get-tuple-element.53.refs_1_, f32[2240,128]{1,0:T(8,128)} %get-tuple-element.59.refs_2_, f32[2240,128]{1,0:T(8,128)} %copy-done.2, f32[2240,128]{1,0:T(8,128)} %get-tuple-element.60.refs_4_, ...), custom_call_target="tpu_custom_call" | custom-call | tf_op jit(solution)/shard_map/backward_intra/pallas_call | solution.py:722
  256.6 2.8 collective-permute-done.5.refs_3_
  259.4 1.0 copy-done.3
  260.4 25.9 %backward_inter.3 = (f32[2240,128]{1,0:T(8,128)}, f32[2240,128]{1,0:T(8,128)}, f32[1680,128]{1,0:T(8,128)}) custom-call(s32[1]{0:T(128)} %bitcast.refs_0_, f32[2240,128]{1,0:T(8,128)} %get-tuple-element.64.refs_1_, f32[2240,128]{1,0:T(8,128)} %get-tuple-element.65.refs_2_, f32[2240,128]{1,0:T(8,128)} %copy-done.3, f32[2240,128]{1,0:T(8,128)} %get-tuple-element.66.refs_4_, ...), custom_call_target="tpu_custom_call" | custom-call | tf_op jit(solution)/shard_map/backward_inter/pallas_call | solution.py:722
  287.1 1.0 pad.28.refs_4_
  288.2 0.7 slice_reduce_fusion.2
  289.6 0.6 pad.29.refs_6_
  290.2 0.6 broadcast_select_fusion.refs_7_
  290.8 1.0 copy-done
  291.8 39.5 %backward_intra.3.r0 = f32[1688,128]{1,0:T(8,128)} custom-call(s32[1]{0:T(128)} %bitcast.refs_0_, f32[2240,128]{1,0:T(8,128)} %get-tuple-element.70.refs_1_, f32[2240,128]{1,0:T(8,128)} %get-tuple-element.71.refs_2_, f32[2240,128]{1,0:T(8,128)} %copy-done, f32[2000,128]{1,0:T(8,128)} %pad.28.refs_4_, f32[2000,64]{1,0:T(8,128)} %get-tuple-element.72.refs_5_, ...), custom_call_target="tpu_custom_call" | custom-call | tf_op jit(solution)/shard_map/backward_intra/pallas_call | solution.py:722
  331.3 55.6 %finish.1 = (f32[849,128]{1,0:T(8,128)}, bf16[849,128]{1,0:T(8,128)(2,1)}, f32[849,128]{1,0:T(8,128)}, f32[849,128]{1,0:T(8,128)}, f32[8,128]{1,0:T(8,128)}) custom-call(f32[1688,128]{1,0:T(8,128)} %backward_intra.3.r0, f32[1680,128]{1,0:T(8,128)} %get-tuple-element.78.r1, f32[1680,128]{1,0:T(8,128)} %get-tuple-element.79.r2, ...), custom_call_target="tpu_custom_call" | custom-call | tf_op jit(solution)/shard_map/finish/pallas_call | solution.py:789
  387.0 1.3 slice.85
  388.4 1.2 slice_bitcast_fusion
  389.5 1.8 copy.94
  391.3 1.6 copy.95
  393.0 0.8 copy.96
  393.8 0.8 copy.97
  (74 shorter events, 6.8 us)
Async XLA Ops:
  7.2 2.2 copy-start.10
  7.2 2.4 copy-start.9
  7.2 46.2 %all-gather.4.cloned.1.call-start = ((), (), s32[]{:S(2)}) async-start(), calls=%async_computation | async-start | bytes 3912192 | tf_op jit(solution)/shard_map/all_gather | solution.py:812
  85.5 3.0 collective-permute-start
  88.5 1.0 copy-start.4
  108.8 3.0 collective-permute-start.1
  111.8 1.0 copy-start.5
  112.8 30.8 %copy-start.12 = (s32[2]{0:T(128)S(1)}, s32[2]{0:T(128)}, u32[]{:S(2)}) copy-start(s32[2]{0:T(128)} %param.13) | copy-start | bytes 28
  112.8 30.8 %copy-start.13 = (s32[2]{0:T(128)S(1)}, s32[2]{0:T(128)}, u32[]{:S(2)}) copy-start(s32[2]{0:T(128)} %param.12) | copy-start | bytes 28
  143.3 4.1 %collective-permute-start.2 = (f32[2240,128]{1,0:T(8,128)}, f32[2240,128]{1,0:T(8,128)S(1)}, u32[]{:S(2)}, u32[]{:S(2)}) collective-permute-start(f32[2240,128]{1,0:T(8,128)} %get-tuple-element.50.refs_2_), channel_id=1, source_target_pairs={{0,4},{4,0},{8,12},{12,8},{16,20},{20,16},{24,28},{28,24},{1,5},{5... | collective-permute-start | bytes 3440648 | tf_op jit(solution)/shard_map/ppermute | solution.py:859
  147.4 1.1 copy-start.1
  167.8 5.6 %collective-permute-start.3 = (f32[2240,128]{1,0:T(8,128)}, f32[2240,128]{1,0:T(8,128)S(1)}, u32[]{:S(2)}, u32[]{:S(2)}) collective-permute-start(f32[2240,128]{1,0:T(8,128)} %get-tuple-element.52.pa_ref), channel_id=1, source_target_pairs={{0,4},{4,0},{8,12},{12,8},{16,20},{20,16},{24,28},{28,24},{1,5},{5... | collective-permute-start | bytes 3440648 | tf_op jit(solution)/shard_map/ppermute | solution.py:859
  173.4 1.0 copy-start.6
  214.1 3.0 collective-permute-start.4
  217.1 1.0 copy-start.2
  256.4 3.0 collective-permute-start.5
  259.4 1.0 copy-start.3
  286.3 4.5 %collective-permute-start.6 = (f32[2240,128]{1,0:T(8,128)}, f32[2240,128]{1,0:T(8,128)S(1)}, u32[]{:S(2)}, u32[]{:S(2)}) collective-permute-start(f32[2240,128]{1,0:T(8,128)} %get-tuple-element.71.refs_2_), channel_id=1, source_target_pairs={{0,4},{4,0},{8,12},{12,8},{16,20},{20,16},{24,28},{28,24},{1,5},{5... | collective-permute-start | bytes 3440648 | tf_op jit(solution)/shard_map/ppermute | solution.py:859
  287.1 3.1 copy-start.11
  290.8 1.0 copy-start
  387.0 6.0 %copy-start.8 = (f32[849,128]{1,0:T(8,128)S(1)}, f32[849,128]{1,0:T(8,128)}, u32[]{:S(2)}) copy-start(f32[849,128]{1,0:T(8,128)} %get-tuple-element.83) | copy-start | bytes 1304068
  387.0 6.8 %copy-start.7 = (f32[849,128]{1,0:T(8,128)S(1)}, f32[849,128]{1,0:T(8,128)}, u32[]{:S(2)}) copy-start(f32[849,128]{1,0:T(8,128)} %get-tuple-element.84) | copy-start | bytes 1304068
Sparse Core Ops, SparseCore 0:
  10.5 35.1 all-gather.3

commit v2 on v1

--- a/solution.py
+++ b/solution.py
@@ -52,6 +52,82 @@
     a_hi, a_lo = split(a)
     b_hi, b_lo = split(b)
     return dot_rows(a_hi, b_hi) + dot_rows(a_lo, b_hi) + dot_rows(a_hi, b_lo)
+
+
+SIDE_ROWS = 772
+PROJ_ROWS = 2 * SIDE_ROWS
+VEC_ROW = PROJ_ROWS + 128
+LAYER_ROWS = 1680
+HEAD_ROWS = 160
+WINDOW = 1688
+
+
+def window(layer_no):
+    at = 2 + 3347 * layer_no
+    return at // 16 * 8, at // 2 % 8, at % 2
+
+
+def pick(ref, base, odd, start, count, stride=1):
+    def load(at):
+        return ref[pl.ds(at, count, stride=stride), :] if stride > 1 else ref[pl.ds(at, count), :]
+
+    first = load(base + start)
+    if not odd:
+        return first
+    return jnp.concatenate([first[:, 64:], load(base + start + 1)[:, :64]], 1)
+
+
+def load_weights(ref, base, odd, dir_no, proj_s):
+    at = SIDE_ROWS * dir_no
+    win = jnp.concatenate([pick(ref, base, odd, at + q, FILTERS, 4) for q in range(4)], 1)
+    wrec = jnp.concatenate([pick(ref, base, odd, at + 256 + q, UNITS, 4) for q in range(4)], 1)
+    bias = jnp.concatenate([pick(ref, base, odd, at + 768 + q, 1) for q in range(4)], 1)
+    pairs = pick(ref, base, odd, PROJ_ROWS + 64 * dir_no, 64)
+    proj_s[pl.ds(0, 64, stride=2), :] = pairs
+    proj_s[pl.ds(1, 64, stride=2), :] = pltpu.roll(pairs, 64, 1)
+    return win, wrec, bias, proj_s[:, :FILTERS]
+
+
+def load_vec(ref, base, odd):
+    first = pick(ref, base, odd, VEC_ROW, 1)
+    turned = pltpu.roll(jnp.broadcast_to(first, (8, 128)), 64, 1)[0:1]
+    if odd:
+        last = ref[base + VEC_ROW + 1:base + VEC_ROW + 2, :]
+        last = jnp.concatenate([last[:, 64:], last[:, 64:]], 1)
+    else:
+        last = ref[base + VEC_ROW + 1:base + VEC_ROW + 2, :]
+        last = jnp.concatenate([last[:, :64], last[:, :64]], 1)
+    low = lax.broadcasted_iota(jnp.int32, (1, 128), 1) < 64
+    return jnp.where(low, first, turned), jnp.where(low, turned, first), last
+
+
+def put_split(w, twice_ref, low_ref):
+    hi, lo = split(w)
+    twice_ref[...] = jnp.concatenate([hi, hi], 0)
+    low_ref[...] = lo
+
+
+def times(dir_no, chunk_no, length, steps):
+    return [dir_no * (length - 1) + (1 - 2 * dir_no) * (chunk_no * steps + u) for u in range(steps)]
+
+
+def stream_rows(inter, groups, at):
+    if inter:
+        return pl.ds(at, HALF_PAD, stride=groups)
+    return pl.ds(pl.multiple_of(lax.rem(at, HOP) * groups, 8), groups)
+
+
+def gather(ref, inter, groups, positions):
+    return jnp.concatenate([ref[stream_rows(inter, groups, at), :] for at in positions], 0)
+
+
+def to_sides(inter, steps, array):
+    if not inter:
+        return [array]
+    three = array.reshape(steps, 2 * HALF_PAD, array.shape[-1])
+    return [
+        three[:, side * HALF_PAD:(side + 1) * HALF_PAD].reshape(steps * HALF_PAD, array.shape[-1]) for side in range(2)
+    ]
 
 
 SIDE_ROWS = 772
@@ -130,29 +206,120 @@
     scale_ref[...] = jnp.broadcast_to(scale, scale_ref.shape)
 
 
+def greet_sibling():
+    b = lax.axis_index("batch")
+    device = (b + 1 - 2 * lax.rem(b, 2), lax.axis_index("frames"))
+    return device, pltpu.get_barrier_semaphore()
+
+
+def fetch(flat_ref, layer_no, window_s, sem):
+    first, _, _ = window(layer_no)
+    copy = pltpu.make_async_copy(flat_ref.at[pl.ds(first, WINDOW)], window_s, sem)
+    copy.start()
+    return copy
+
+
+def swap_with_sibling(src_ref, dst_ref, sems):
+    device, barrier = greet_sibling()
+    pl.semaphore_wait(barrier, 1)
+    copy = pltpu.make_async_remote_copy(
+        src_ref=src_ref, dst_ref=dst_ref, send_sem=sems.at[0], recv_sem=sems.at[1],
+        device_id=device, device_id_type=pl.DeviceIdType.MESH,
+    )
+    copy.start()
+    copy.wait()
+
+
 def forward_kernel(layer_no, groups, steps, *refs):
     inter = layer_no % 2 == 1
-    first_layer = layer_no == 0
-    if first_layer:
-        (dir_ref, x_ref, flat_ref,
-         h_ref, coef_ref, part_ref,
-         wi2, wil, wr2, wrl, pj2, pjl, proj_s, bias_s, gin, c_s, h_s) = refs
-    else:
-        (dir_ref, prev_ref, pa_ref, pb_ref, below_ref, flat_ref,
-         x_ref, normed_ref, scale_ref, h_ref, coef_ref, part_ref,
-         wi2, wil, wr2, wrl, pj2, pjl, proj_s, bias_s, gin, c_s, h_s) = refs
-    chunk_no = pl.program_id(0)
-    count = pl.num_programs(0)
-    dir_no = dir_ref[0]
+    (x_ref, flat_ref,
+     next_ref, normed_ref, scale_ref, h_ref, coef_ref,
+     wi2, wil, wr2, wrl, pj2, pjl, proj_s, bias_s, gin_a, gin_b, h_a, h_b, c_s, part_ref, peer_ref, sems, window_s, fetch_sem) = refs
+    turn_no = pl.program_id(0)
+    last_turn = pl.num_programs(0) - 1
+    chunks = 2 * pl.num_programs(0)
+    length = chunks * steps
+    dir_no = lax.rem(lax.axis_index("batch"), 2)
     rows = 2 * HALF_PAD if inter else groups
     valid = HOP * groups
 
-    @pl.when(chunk_no == 0)
+    def before(chunk_no, gin):
+        chunk_no = lax.rem(chunk_no, chunks)
+        positions = times(dir_no, chunk_no, length, steps)
+        xs_hi, xs_lo = split(gather(x_ref, inter, groups, positions))
+        both = jnp.concatenate([xs_hi, xs_lo], 1)
+        half = 0 if inter else lax.div(positions[0], HOP)
+
+        def gate(q):
+            cut = slice(q * UNITS, (q + 1) * UNITS)
+            for side in range(2) if inter else [half]:
+                found = dot(both, wi2[side, :, cut]) + dot(xs_hi, wil[side, :, cut]) + bias_s[0:1, cut]
+                if inter:
+                    for u in range(steps):
+                        at = u * rows + side * HALF_PAD
+                        gin[at:at + HALF_PAD, cut] = found[u * HALF_PAD:(u + 1) * HALF_PAD]
+                else:
+                    gin[:, cut] = found
+
+        return [functools.partial(gate, q) for q in range(4)]
+
+    def after(chunk_no, hs):
+        chunk_no = lax.rem(chunk_no + chunks, chunks)
+        positions = times(dir_no, chunk_no, length, steps)
+
+        def project():
+            if inter:
+                found = 0.0
+                for side, part in enumerate(to_sides(inter, steps, hs[...])):
+                    found = found + dot3(part, pj2[side], pjl[side])
+                for u in range(steps):
+                    part_ref[stream_rows(inter, groups, positions[u]), :] = found[u * HALF_PAD:(u + 1) * HALF_PAD]
+            else:
+                half = lax.div(positions[0], HOP)
+                found = dot3(hs[...], pj2[half], pjl[half])
+                for u in range(steps):
+                    here = stream_rows(inter, groups, positions[u])
+                    part_ref[here, :] = part_ref[here, :] + found[u * groups:(u + 1) * groups]
+
+        return [project]
+
+    def walk(gin, hs, h, c, sub, beside):
+        for u in range(steps):
+            hi, lo = split(h)
+            z = dot(jnp.concatenate([hi, lo], 1), wr2[...]) + dot(hi, wrl[...])
+            for task in beside[u::steps]:
+                task()
+            z = z + gin[u * rows:(u + 1) * rows]
+            th = jnp.tanh(z)
+            ti, tf, g, to = (th[:, q * UNITS:(q + 1) * UNITS] for q in range(4))
+            i_g = 0.5 * ti + 0.5
+            f_g = 0.5 * tf + 0.5
+            o_g = 0.5 * to + 0.5
+            c_prev = c
+            c = f_g * c + i_g * g
+            tc = jnp.tanh(c)
+            h = o_g * tc
+            at = sub * steps + u
+            hs[u * rows:(u + 1) * rows] = h
+            h_ref[at] = h
+            coef_ref[at, 0] = tc * (0.25 - 0.25 * to * to)
+            coef_ref[at, 1] = o_g * (1.0 - tc * tc)
+            coef_ref[at, 2] = g * (0.25 - 0.25 * ti * ti)
+            coef_ref[at, 3] = c_prev * (0.25 - 0.25 * tf * tf)
+            coef_ref[at, 4] = i_g * (1.0 - g * g)
+            coef_ref[at, 5] = f_g
+        return h, c
+
+    @pl.when(turn_no == 0)
     def _():
+        device, barrier = greet_sibling()
+        pl.semaphore_signal(barrier, inc=1, device_id=device, device_id_type=pl.DeviceIdType.MESH)
+        fetch(flat_ref, layer_no, window_s, fetch_sem).wait()
+        part_ref[...] = jnp.zeros_like(part_ref)
         column = lax.broadcasted_iota(jnp.int32, (1, GATES), 1)
         scaling = jnp.where((column >= 2 * UNITS) & (column < 3 * UNITS), 1.0, 0.5)
         _, base, odd = window(layer_no)
-        win, wrec, bias, proj = load_weights(flat_ref, base, odd, dir_no, proj_s)
+        win, wrec, bias, proj = load_weights(window_s, base, odd, dir_no, proj_s)
         win = win * scaling
         none = jnp.zeros_like(win)
         for half in range(2):
@@ -163,104 +330,142 @@
         for half in range(2):
             put_split(jnp.concatenate([proj, none] if half == 0 else [none, proj], 1), pj2.at[half], pjl.at[half])
         c_s[...] = jnp.zeros_like(c_s)
-        h_s[...] = jnp.zeros_like(h_s)
-        h_ref[0] = jnp.zeros((rows, UNITS), F32)
-        h_ref[h_ref.shape[0] - 1] = jnp.zeros((rows, UNITS), F32)
-        if not first_layer:
-            _, below_base, below_odd = window(layer_no - 1)
-            norm_stage(
-                prev_ref, pa_ref, pb_ref, below_ref, below_base, below_odd, valid, normed_ref, scale_ref, x_ref
-            )
-
-    first, half, row = place(dir_no, chunk_no, count, steps, inter, groups)
-    if inter:
-        xs = jnp.concatenate(
-            [x_ref[pl.ds(first + u, HALF_PAD, stride=groups), :] for u in range(steps)], 0
-        )
-        for side in range(2):
-            found = dot3(xs, wi2[side], wil[side]) + bias_s[0:1]
-            for u in range(steps):
-                gin[pl.ds(u * rows + side * HALF_PAD, HALF_PAD)] = found[u * HALF_PAD:(u + 1) * HALF_PAD]
-    else:
-        xs = x_ref[pl.ds(row, steps * groups), :]
-        gin[...] = dot3(xs, wi2[half], wil[half]) + bias_s[0:1]
-
-    h = h_s[...]
-    c = c_s[...]
-    for u in range(steps):
-        v = jnp.where(dir_no == 0, u, steps - 1 - u)
-        hi, lo = split(h)
-        z = (
-            gin[pl.ds(pl.multiple_of(v * rows, 8), rows)]
-            + dot(jnp.concatenate([hi, lo], 1), wr2[...])
-            + dot(hi, wrl[...])
-        )
-        th = jnp.tanh(z)
-        ti, tf, g, to = (th[:, q * UNITS:(q + 1) * UNITS] for q in range(4))
-        i_g = 0.5 * ti + 0.5
-        f_g = 0.5 * tf + 0.5
-        o_g = 0.5 * to + 0.5
-        c_prev = c
-        c = f_g * c + i_g * g
-        tc = jnp.tanh(c)
-        h = o_g * tc
-        h_ref[first + v + 1] = h
-        coef_ref[u, 0] = tc * (0.25 - 0.25 * to * to)
-        coef_ref[u, 1] = o_g * (1.0 - tc * tc)
-        coef_ref[u, 2] = g * (0.25 - 0.25 * ti * ti)
-        coef_ref[u, 3] = c_prev * (0.25 - 0.25 * tf * tf)
-        coef_ref[u, 4] = i_g * (1.0 - g * g)
-        coef_ref[u, 5] = f_g
-    h_s[...] = h
+        h_b[...] = jnp.zeros_like(h_b)
+        for task in before(0, gin_a):
+            task()
+
+    h, c = h_b[(steps - 1) * rows:], c_s[...]
+    h, c = walk(gin_a, h_a, h, c, 0, after(2 * turn_no - 1, h_b) + before(2 * turn_no + 1, gin_b))
+    h, c = walk(gin_b, h_b, h, c, 1, after(2 * turn_no, h_a) + before(2 * turn_no + 2, gin_a))
     c_s[...] = c
 
-    hs = h_ref[pl.ds(first + 1, steps)]
-    if inter:
-        low_half = hs[:, :HALF_PAD].reshape(steps * HALF_PAD, UNITS)
-        top_half = hs[:, HALF_PAD:].reshape(steps * HALF_PAD, UNITS)
-        found = dot3(low_half, pj2[0], pjl[0]) + dot3(top_half, pj2[1], pjl[1])
-        for u in range(steps):
-            part_ref[pl.ds(first + u, HALF_PAD, stride=groups), :] = found[u * HALF_PAD:(u + 1) * HALF_PAD]
-    else:
-        found = dot3(hs.reshape(steps * groups, UNITS), pj2[half], pjl[half])
-        here = pl.ds(row, steps * groups)
-
-        @pl.when(2 * chunk_no < count)
-        def _():
-            part_ref[here] = found
-
-        @pl.when(2 * chunk_no >= count)
-        def _():
-            part_ref[here] = part_ref[here] + found
+    @pl.when(turn_no == last_turn)
+    def _():
+        for task in after(chunks - 1, h_b):
+            task()
+        swap_with_sibling(part_ref, peer_ref, sems)
+        _, base, odd = window(layer_no)
+        norm_stage(x_ref, part_ref, peer_ref, window_s, base, odd, valid, normed_ref, scale_ref, next_ref)
 
 
 def backward_kernel(layer_no, groups, steps, *refs):
     inter = layer_no % 2 == 1
     last_layer = layer_no == 2 * BLOCKS - 1
+    g_ref, normed_ref, scale_ref, x_ref, h_ref, coef_ref, flat_ref, *rest = refs
     if last_layer:
-        (dir_ref, g_ref, hg_ref, normed_ref, scale_ref, x_ref, h_ref, coef_ref, flat_ref,
-         dx_ref, grad_ref,
-         wi2, wil, wrw, wrt, pj2, pjl, proj_s, dmx, dhc, dzs, dz_s, dc_s, awin, aproj, abias) = refs
-    elif layer_no:
-        (dir_ref, res_ref, da_ref, db2_ref, normed_ref, scale_ref, x_ref, h_ref, coef_ref, flat_ref,
-         g_ref, dx_ref, grad_ref,
-         wi2, wil, wrw, wrt, pj2, pjl, proj_s, dmx, dhc, dzs, dz_s, dc_s, awin, aproj, abias) = refs
+        hg_ref, *rest = rest
+    if layer_no == 0:
+        column_ref, denc_ref, encoder_ref, loss_ref, *rest = rest
     else:
-        (dir_ref, res_ref, da_ref, db2_ref, column_ref, denc_ref, encoder_ref, loss_ref,
-         normed_ref, scale_ref, x_ref, h_ref, coef_ref, flat_ref,
-         grad_ref,
-         wi2, wil, wrw, wrt, pj2, pjl, proj_s, dmx, dhc, dzs, dz_s, dc_s, awin, aproj, abias, g_ref, dx_ref) = refs
-    back_no = pl.program_id(0)
-    count = pl.num_programs(0)
-    chunk_no = count - 1 - back_no
-    dir_no = dir_ref[0]
+        below_ref, *rest = rest
+    (grad_ref,
+     wi2, wil, wrw, wrt, pj2, pjl, proj_s, dmx, dh_a, dh_b, dz_a, dz_b, dc_s, awin, aproj, abias,
+     dx_ref, peer_ref, sems, window_s, fetch_sem) = rest
+    turn_no = pl.program_id(0)
+    last_turn = pl.num_programs(0) - 1
+    chunks = 2 * pl.num_programs(0)
+    length = chunks * steps
+    dir_no = lax.rem(lax.axis_index("batch"), 2)
     rows = 2 * HALF_PAD if inter else groups
     valid = HOP * groups
 
-    @pl.when(back_no == 0)
+    def before(back_no, dhc):
+        chunk_no = chunks - 1 - lax.rem(back_no, chunks)
+        positions = times(dir_no, chunk_no, length, steps)
+
+        def outward():
+            dms = gather(dmx, inter, groups, positions)
+            if inter:
+                for side in range(2):
+                    found = dot3(dms, pj2[side], pjl[side])
+                    for u in range(steps):
+                        at = u * rows + side * HALF_PAD
+                        dhc[at:at + HALF_PAD] = found[u * HALF_PAD:(u + 1) * HALF_PAD]
+            else:
+                half = lax.div(positions[0], HOP)
+                dhc[...] = dot3(dms, pj2[half], pjl[half])
+
+        return [outward]
+
+    def after(back_no, dzs):
+        used = back_no >= 0
+        chunk_no = chunks - 1 - lax.rem(back_no + chunks, chunks)
+        positions = times(dir_no, chunk_no, length, steps)
+        half = 0 if inter else lax.div(positions[0], HOP)
+        xs = gather(x_ref, inter, groups, positions)
+        at = chunk_no * steps
+        hs = h_ref[pl.ds(at, steps)].reshape(steps * rows, UNITS)
+        early = h_ref[lax.rem(at + length - 1, length)] * jnp.where(at == 0, 0.0, 1.0)
+        hp = jnp.concatenate([early, hs[:(steps - 1) * rows]], 0)
+        if inter:
+            lhs = [
+                jnp.concatenate([xs if side == 0 else pltpu.roll(xs, FILTERS, 1), hp_side], 1)
+                for side, hp_side in enumerate(to_sides(inter, steps, hp))
+            ]
+            lhs = jnp.concatenate(lhs, 0)
+        else:
+            lhs = jnp.concatenate([jnp.where(half == 0, xs, pltpu.roll(xs, FILTERS, 1)), hp], 1)
+        lhs_t = lhs.T
+        lhs_hi, lhs_lo = split(lhs_t)
+
+        def gate(q):
+            cut = slice(q * UNITS, (q + 1) * UNITS)
+            dz = dzs[:, cut]
+            abias[0:1, cut] += jnp.sum(dz, 0, keepdims=True)
+            if inter:
+                dz = jnp.concatenate(to_sides(inter, steps, dz), 0)
+            dz_hi, dz_lo = split(dz)
+            awin[:, cut] += dot(lhs_hi, dz_hi) + dot(lhs_lo, dz_hi) + dot(lhs_hi, dz_lo)
+
+        def project():
+            dms = gather(dmx, inter, groups, positions) * jnp.where(used, 1.0, 0.0)
+            if inter:
+                aproj[...] += dot_rows3(jnp.concatenate(to_sides(inter, steps, hs), 1), dms)
+            else:
+                turned = jnp.where(half == 0, dms, pltpu.roll(dms, FILTERS, 1))
+                aproj[...] += dot_rows3(hs, turned)
+
+        def inward():
+            if inter:
+                found = 0.0
+                for side, dz_side in enumerate(to_sides(inter, steps, dzs[...])):
+                    found = found + dot3(dz_side, wi2[side], wil[side])
+                for u in range(steps):
+                    dx_ref[stream_rows(inter, groups, positions[u]), :] = found[u * HALF_PAD:(u + 1) * HALF_PAD]
+            else:
+                found = dot3(dzs[...], wi2[half], wil[half])
+                for u in range(steps):
+                    here = stream_rows(inter, groups, positions[u])
+                    dx_ref[here, :] = dx_ref[here, :] + found[u * groups:(u + 1) * groups]
+
+        return [functools.partial(gate, q) for q in range(4)] + [inward, project]
+
+    def walk(dhc, dzs, dz, dc_next, sub, beside):
+        for u in reversed(range(steps)):
+            at = sub * steps + u
+            hi, lo = split(dz)
+            wide = dot(hi, wrw[...])
+            dh = wide[:, :UNITS] + wide[:, UNITS:] + dot(lo, wrt[...])
+            for task in beside[steps - 1 - u::steps]:
+                task()
+            dh = dh + dhc[u * rows:(u + 1) * rows]
+            dc = dh * coef_ref[at, 1] + dc_next
+            dz = jnp.concatenate(
+                [dc * coef_ref[at, 2], dc * coef_ref[at, 3], dc * coef_ref[at, 4], dh * coef_ref[at, 0]], 1
+            )
+            dc_next = dc * coef_ref[at, 5]
+            dzs[u * rows:(u + 1) * rows] = dz
+        return dz, dc_next
+
+    @pl.when(turn_no == 0)
     def _():
+        if layer_no:
+            device, barrier = greet_sibling()
+            pl.semaphore_signal(barrier, inc=1, device_id=device, device_id_type=pl.DeviceIdType.MESH)
+        fetch(flat_ref, layer_no, window_s, fetch_sem).wait()
+        dx_ref[...] = jnp.zeros_like(dx_ref)
         _, base, odd = window(layer_no)
-        win, wrec, _, proj = load_weights(flat_ref, base, odd, dir_no, proj_s)
+        win, wrec, _, proj = load_weights(window_s, base, odd, dir_no, proj_s)
         win_t = win.T
         none = jnp.zeros_like(win_t)
         for half in range(2):
@@ -272,18 +477,15 @@
         none = jnp.zeros_like(proj_t)
         for half in range(2):
             put_split(jnp.concatenate([proj_t, none] if half == 0 else [none, proj_t], 0), pj2.at[half], pjl.at[half])
-        dz_s[...] = jnp.zeros_like(dz_s)
+        dz_b[...] = jnp.zeros_like(dz_b)
         dc_s[...] = jnp.zeros_like(dc_s)
         awin[...] = jnp.zeros_like(awin)
         aproj[...] = jnp.zeros_like(aproj)
         abias[...] = jnp.zeros_like(abias)
         grad_ref[...] = jnp.zeros_like(grad_ref)
-        if not last_layer:
-            g_ref[:valid] = res_ref[:valid] + da_ref[:valid] + db2_ref[:valid]
-            g_ref[valid:] = jnp.zeros((g_ref.shape[0] - valid, 128), F32)
         g = g_ref[:valid]
         normed = normed_ref[:valid]
-        _, gain, _ = load_vec(flat_ref, base, odd)
+        _, gain, _ = load_vec(window_s, base, odd)
         g_n = g * gain
         total = 2.0 * valid * FILTERS
         mean_one = jnp.sum(g_n) / total
@@ -302,88 +504,29 @@
         if last_layer:
             grad_ref[LAYER_ROWS:] = hg_ref[...] * lead
 
-    first, half, row = place(dir_no, chunk_no, count, steps, inter, groups)
-    here = pl.ds(row, steps * groups)
-    if inter:
-        dms = jnp.concatenate(
-            [dmx[pl.ds(first + u, HALF_PAD, stride=groups), :] for u in range(steps)], 0
-        )
-        for side in range(2):
-            found = dot3(dms, pj2[side], pjl[side])
-            for u in range(steps):
-                dhc[pl.ds(u * rows + side * HALF_PAD, HALF_PAD)] = found[u * HALF_PAD:(u + 1) * HALF_PAD]
-    else:
-        dms = dmx[here, :]
-        dhc[...] = dot3(dms, pj2[half], pjl[half])
-
-    dz = dz_s[...]
-    dc_next = dc_s[...]
-    for u in reversed(range(steps)):
-        v = jnp.where(dir_no == 0, u, steps - 1 - u)
-        hi, lo = split(dz)
-        wide = dot(hi, wrw[...])
-        dh = (
-            dhc[pl.ds(pl.multiple_of(v * rows, 8), rows)]
-            + wide[:, :UNITS] + wide[:, UNITS:] + dot(lo, wrt[...])
-        )
-        dc = dh * coef_ref[u, 1] + dc_next
-        dz = jnp.concatenate(
-            [dc * coef_ref[u, 2], dc * coef_ref[u, 3], dc * coef_ref[u, 4], dh * coef_ref[u, 0]], 1
-        )
-        dc_next = dc * coef_ref[u, 5]
-        if inter:
-            dzs[0, pl.ds(pl.multiple_of(v * HALF_PAD, 8), HALF_PAD)] = dz[:HALF_PAD]
-            dzs[1, pl.ds(pl.multiple_of(v * HALF_PAD, 8), HALF_PAD)] = dz[HALF_PAD:]
-        else:
-            dzs[0, pl.ds(pl.multiple_of(v * rows, 8), rows)] = dz
-    dz_s[...] = dz
+        for task in before(0, dh_a):
+            task()
+
+    dz, dc_next = dz_b[:rows], dc_s[...]
+    dz, dc_next = walk(dh_a, dz_a, dz, dc_next, 1, after(2 * turn_no - 1, dz_b) + before(2 * turn_no + 1, dh_b))
+    dz, dc_next = walk(dh_b, dz_b, dz, dc_next, 0, after(2 * turn_no, dz_a) + before(2 * turn_no + 2, dh_a))
     dc_s[...] = dc_next
 
-    hs = h_ref[pl.ds(first + 1, steps)]
-    hp = h_ref[pl.ds(first + 2 * dir_no, steps)]
-    if inter:
-        xs = jnp.concatenate(
-            [x_ref[pl.ds(first + u, HALF_PAD, stride=groups), :] for u in range(steps)], 0
-        )
-        found = 0.0
-        for side in range(2):
-            cut = slice(side * HALF_PAD, (side + 1) * HALF_PAD)
-            dzc = dzs[side]
-            found = found + dot3(dzc, wi2[side], wil[side])
-            turned = xs if side == 0 else pltpu.roll(xs, FILTERS, 1)
-            awin[...] += dot_rows3(
-                jnp.concatenate([turned, hp[:, cut].reshape(steps * HALF_PAD, UNITS)], 1), dzc
-            )
-            aproj[side] += dot_rows3(hs[:, cut].reshape(steps * HALF_PAD, UNITS), dms)
-            abias[0:1] += jnp.sum(dzc, 0, keepdims=True)
-        for u in range(steps):
-            dx_ref[pl.ds(first + u, HALF_PAD, stride=groups), :] = found[u * HALF_PAD:(u + 1) * HALF_PAD]
-    else:
-        xs = x_ref[here, :]
-        dzc = dzs[0]
-        turned = jnp.where(half == 0, xs, pltpu.roll(xs, FILTERS, 1))
-        awin[...] += dot_rows3(jnp.concatenate([turned, hp.reshape(steps * groups, UNITS)], 1), dzc)
-        aproj[half] += dot_rows3(hs.reshape(steps * groups, UNITS), dms)
-        abias[0:1] += jnp.sum(dzc, 0, keepdims=True)
-        found = dot3(dzc, wi2[half], wil[half])
-
-        @pl.when(2 * back_no < count)
-        def _():
-            dx_ref[here] = found
-
-        @pl.when(2 * back_no >= count)
-        def _():
-            dx_ref[here] = dx_ref[here] + found
-
-    @pl.when(back_no == count - 1)
+    @pl.when(turn_no == last_turn)
     def _():
+        for task in after(chunks - 1, dz_b):
+            task()
+        if layer_no:
+            swap_with_sibling(dx_ref, peer_ref, sems)
+            below_ref[:valid] = g_ref[:valid] + dx_ref[:valid] + peer_ref[:valid]
+            below_ref[valid:] = jnp.zeros((below_ref.shape[0] - valid, 128), F32)
         at = SIDE_ROWS * dir_no
         for q in range(4):
             cut = slice(q * UNITS, (q + 1) * UNITS)
             grad_ref[pl.ds(at + q, FILTERS, stride=4), :] = awin[:FILTERS, cut]
             grad_ref[pl.ds(at + 256 + q, UNITS, stride=4), :] = awin[2 * FILTERS:, cut]
             grad_ref[pl.ds(at + 768 + q, 1), :] = abias[0:1, cut]
-        proj_s[...] = aproj[0] + pltpu.roll(aproj[1], FILTERS, 1)
+        proj_s[...] = aproj[:UNITS] + pltpu.roll(aproj[UNITS:], FILTERS, 1) if inter else aproj[...]
         even = proj_s[pl.ds(0, 64, stride=2), :]
         odd_rows = proj_s[pl.ds(1, 64, stride=2), :]
         grad_ref[pl.ds(PROJ_ROWS + 64 * dir_no, 64), :] = jnp.concatenate(
@@ -404,13 +547,11 @@
             grad_ref[LAYER_ROWS + 1:LAYER_ROWS + 2] = loss_ref[0:1] * lead
 
 
-def head_kernel(groups, prev_ref, pa_ref, pb_ref, below_ref, stream_ref, column_ref, active_ref, masker_ref, decoder_ref,
-                normed_ref, scale_ref, g_ref, hg_ref, denc_ref, loss_ref,
-                sep, sig_s, now_s, before_s, slope_s, mk2, mkl, mt2, mtl, dk2, dkl, dt2, dtl, amask, adec, m_low, m_top):
+def head_kernel(groups, sep, stream_ref, column_ref, active_ref, masker_ref, decoder_ref,
+                g_ref, hg_ref, denc_ref, loss_ref,
+                sig_s, now_s, before_s, slope_s, mk2, mkl, mt2, mtl, dk2, dkl, dt2, dtl, amask, adec, m_low, m_top):
     valid = HOP * groups
     block = 10 * groups
-    _, below_base, below_odd = window(2 * BLOCKS - 1)
-    norm_stage(prev_ref, pa_ref, pb_ref, below_ref, below_base, below_odd, valid, normed_ref, scale_ref, sep)
     put_split(masker_ref[...], mk2, mkl)
     put_split(masker_ref[...].T, mt2, mtl)
     put_split(decoder_ref[...], dk2, dkl)
@@ -657,39 +798,29 @@
 
 def sizes(inter, groups):
     if inter:
-        return groups, 2 * HALF_PAD, 8
-    return 2 * HOP, groups, 10
+        return groups, 2 * HALF_PAD, 4
+    return 2 * HOP, groups, 5
 
 
 def whole(shape):
     return pl.BlockSpec(shape, lambda j: (0,) * len(shape))
 
 
-def layer_spec(layer_no):
-    first, _, _ = window(layer_no)
-    return pl.BlockSpec((pl.Element(WINDOW), pl.Element(128)), lambda j: (first, 0))
-
-
-def run_forward(layer_no, groups, dir_no, stream, flat):
+def run_forward(layer_no, groups, stream, flat):
     inter = layer_no % 2 == 1
     length, rows, steps = sizes(inter, groups)
     stream_shape = (HALF_PAD * groups, 128)
-    coef_block = (steps, 6, rows, UNITS)
     out = [
-        ((length + 2, rows, UNITS), whole((length + 2, rows, UNITS))),
-        ((length, 6, rows, UNITS), pl.BlockSpec(coef_block, lambda j: (j, 0, 0, 0))),
         (stream_shape, whole(stream_shape)),
+        (stream_shape, whole(stream_shape)),
+        ((8, 128), whole((8, 128))),
+        ((length, rows, UNITS), pl.BlockSpec((2 * steps, rows, UNITS), lambda j: (j, 0, 0))),
+        ((length, 6, rows, UNITS), pl.BlockSpec((2 * steps, 6, rows, UNITS), lambda j: (j, 0, 0, 0))),
     ]
-    layers = [layer_no]
-    if layer_no:
-        out = [(stream_shape, whole(stream_shape)), (stream_shape, whole(stream_shape)), ((8, 128), whole((8, 128)))] + out
-        layers = [layer_no - 1, layer_no]
     return pl.pallas_call(
         functools.partial(forward_kernel, layer_no, groups, steps),
-        grid=(length // steps,),
-        in_specs=[pl.BlockSpec(memory_space=pltpu.SMEM)]
-        + [whole(a.shape) for a in stream]
-        + [layer_spec(n) for n in layers],
+        grid=(length // (2 * steps),),
+        in_specs=[whole(stream_shape), pl.BlockSpec(memory_space=pl.ANY)],
         out_specs=[spec for _, spec in out],
         out_shape=[jax.ShapeDtypeStruct(shape, F32) for shape, _ in out],
         scratch_shapes=[
@@ -697,34 +828,37 @@
             pltpu.VMEM((256, GATES), BF16), pltpu.VMEM((128, GATES), BF16),
             pltpu.VMEM((2, 256, 128), BF16), pltpu.VMEM((2, 128, 128), BF16),
             pltpu.VMEM((UNITS, 128), F32),
-            pltpu.VMEM((8, GATES), F32), pltpu.VMEM((steps * rows, GATES), F32),
-            pltpu.VMEM((rows, UNITS), F32), pltpu.VMEM((rows, UNITS), F32),
+            pltpu.VMEM((8, GATES), F32),
+            pltpu.VMEM((steps * rows, GATES), F32), pltpu.VMEM((steps * rows, GATES), F32),
+            pltpu.VMEM((steps * rows, UNITS), F32), pltpu.VMEM((steps * rows, UNITS), F32),
+            pltpu.VMEM((rows, UNITS), F32),
+            pltpu.VMEM(stream_shape, F32), pltpu.VMEM(stream_shape, F32), pltpu.SemaphoreType.DMA((2,)),
+            pltpu.VMEM((WINDOW, 128), F32), pltpu.SemaphoreType.DMA,
         ],
-        compiler_params=pltpu.CompilerParams(vmem_limit_bytes=VMEM_MAX),
+        compiler_params=pltpu.CompilerParams(
+            vmem_limit_bytes=VMEM_MAX, collective_id=2 + layer_no, has_side_effects=True
+        ),
         name="forward_inter" if inter else "forward_intra",
-    )(dir_no, *stream, *[flat for _ in layers])
-
-
-def run_backward(layer_no, groups, dir_no, before, coef, flat):
+    )(stream, flat)
+
+
+def run_backward(layer_no, groups, grad, kept, flat, extra):
     inter = layer_no % 2 == 1
     last_layer = layer_no == 2 * BLOCKS - 1
     length, rows, steps = sizes(inter, groups)
     stream_shape = (HALF_PAD * groups, 128)
-    count = length // steps
-    coef_block = (steps, 6, rows, UNITS)
-    if last_layer:
-        out = [stream_shape, (LAYER_ROWS + HEAD_ROWS, 128)]
-    elif layer_no:
-        out = [stream_shape, stream_shape, (LAYER_ROWS, 128)]
-    else:
-        out = [(LAYER_ROWS + 8, 128)]
-    streams = [] if layer_no else [pltpu.VMEM(stream_shape, F32), pltpu.VMEM(stream_shape, F32)]
+    count = length // (2 * steps)
+    out = [(LAYER_ROWS + (HEAD_ROWS if last_layer else 0 if layer_no else 8), 128)]
+    if layer_no:
+        out = [stream_shape] + out
+    x, normed, scale, h_all, coef = kept
+    remote = dict(collective_id=6 + layer_no, has_side_effects=True) if layer_no else {}
     return pl.pallas_call(
         functools.partial(backward_kernel, layer_no, groups, steps),
         grid=(count,),
-        in_specs=[pl.BlockSpec(memory_space=pltpu.SMEM)]
-        + [whole(a.shape) for a in before]
-        + [pl.BlockSpec(coef_block, lambda j: (count - 1 - j, 0, 0, 0)), layer_spec(layer_no)],
+        in_specs=[whole(a.shape) for a in (grad, normed, scale, x, h_all)]
+        + [pl.BlockSpec((2 * steps, 6, rows, UNITS), lambda j: (count - 1 - j, 0, 0, 0)), pl.BlockSpec(memory_space=pl.ANY)]
+        + [whole(a.shape) for a in extra],
         out_specs=[whole(shape) for shape in out],
         out_shape=[jax.ShapeDtypeStruct(shape, F32) for shape in out],
         scratch_shapes=[
@@ -732,33 +866,34 @@
             pltpu.VMEM((GATES, 256), BF16), pltpu.VMEM((GATES, 128), BF16),
             pltpu.VMEM((2, 256, 128), BF16), pltpu.VMEM((2, 128, 128), BF16),
             pltpu.VMEM((UNITS, 128), F32),
-            pltpu.VMEM(stream_shape, F32), pltpu.VMEM((steps * rows, UNITS), F32),
-            pltpu.VMEM((2, steps * HALF_PAD, GATES) if inter else (1, steps * rows, GATES), F32),
-            pltpu.VMEM((rows, GATES), F32), pltpu.VMEM((rows, UNITS), F32),
-            pltpu.VMEM((256, GATES), F32), pltpu.VMEM((2, UNITS, 128), F32), pltpu.VMEM((8, GATES), F32),
-        ]
-        + streams,
-        compiler_params=pltpu.CompilerParams(vmem_limit_bytes=VMEM_MAX),
+            pltpu.VMEM(stream_shape, F32),
+            pltpu.VMEM((steps * rows, UNITS), F32), pltpu.VMEM((steps * rows, UNITS), F32),
+            pltpu.VMEM((steps * rows, GATES), F32), pltpu.VMEM((steps * rows, GATES), F32),
+            pltpu.VMEM((rows, UNITS), F32),
+            pltpu.VMEM((256, GATES), F32), pltpu.VMEM((2 * UNITS if inter else UNITS, 128), F32),
+            pltpu.VMEM((8, GATES), F32),
+            pltpu.VMEM(stream_shape, F32), pltpu.VMEM(stream_shape, F32), pltpu.SemaphoreType.DMA((2,)),
+            pltpu.VMEM((WINDOW, 128), F32), pltpu.SemaphoreType.DMA,
+        ],
+        compiler_params=pltpu.CompilerParams(vmem_limit_bytes=VMEM_MAX, **remote),
         name="backward_inter" if inter else "backward_intra",
-    )(dir_no, *before, coef, flat)
-
-
-def run_head(groups, streams, flat, stream, column, active, masker, decoder):
+    )(grad, normed, scale, x, h_all, coef, flat, *extra)
+
+
+def run_head(groups, separated, stream, column, active, masker, decoder):
     valid = HOP * groups
     stream_shape = (HALF_PAD * groups, 128)
-    first, _, _ = window(2 * BLOCKS - 1)
-    out = [stream_shape, (8, 128), stream_shape, (HEAD_ROWS, 128), (valid, FILTERS), (8, 128)]
+    out = [stream_shape, (HEAD_ROWS, 128), (valid, FILTERS), (8, 128)]
     wide = SOURCES * FILTERS
+    operands = (separated, stream, column, active, masker, decoder)
     return pl.pallas_call(
         functools.partial(head_kernel, groups),
         grid=(1,),
-        in_specs=[whole(a.shape) for a in streams]
-        + [layer_spec(2 * BLOCKS - 1)]
-        + [whole(a.shape) for a in (stream, column, active, masker, decoder)],
+        in_specs=[whole(a.shape) for a in operands],
         out_specs=[whole(shape) for shape in out],
         out_shape=[jax.ShapeDtypeStruct(shape, F32) for shape in out],
         scratch_shapes=[
-            pltpu.VMEM(stream_shape, F32), pltpu.VMEM((valid, wide), F32), pltpu.VMEM((valid, 128), F32),
+            pltpu.VMEM((valid, wide), F32), pltpu.VMEM((valid, 128), F32),
             pltpu.VMEM((valid + groups, 128), F32), pltpu.VMEM((valid + groups, 128), F32),
             pltpu.VMEM((2 * FILTERS, wide), BF16), pltpu.VMEM((FILTERS, wide), BF16),
             pltpu.VMEM((2 * wide, FILTERS), BF16), pltpu.VMEM((wide, FILTERS), BF16),
@@ -769,7 +904,7 @@
         ],
         compiler_params=pltpu.CompilerParams(vmem_limit_bytes=VMEM_MAX),
         name="head",
-    )(*streams, flat, stream, column, active, masker, decoder)
+    )(*operands)
 
 
 def run_finish(layers, params, first_moment, second_moment):
@@ -814,14 +949,12 @@
     frames_size = lax.axis_size("frames")
     samples = mixture.shape[1] * frames_size
     groups = samples // HOP
-    core = lax.axis_index("batch") % 2
     depth = lax.axis_index("frames")
     column = 2 * items
     copies = frames_size // column
     mine = depth // copies
     weight = jnp.where(depth % copies == 0, 1.0, 0.0).astype(F32)
     pairs = [[2 * b, 2 * b + 1] for b in range(lax.axis_size("batch") // 2)]
-    swap = [(b, b + 1 if b % 2 == 0 else b - 1) for b in range(lax.axis_size("batch"))]
 
     signals = jnp.concatenate([mixture[:, None], sources], 1)
     signals = lax.all_gather(signals, "frames", axis=2, tiled=True)
@@ -852,22 +985,13 @@
 
     pad = ((0, (HALF_PAD - HOP) * groups), (0, 0))
     stream = jnp.pad(jnp.concatenate([encoded, later(encoded)], 1), pad)
-    dir_no = core.reshape(1).astype(jnp.int32)
     view = flat.reshape(-1, 128)
-
-    def exchange(array):
-        return lax.ppermute(array, "batch", swap)
-
     kept = []
-    below = (stream,)
+    x = stream
     for layer_no in range(2 * BLOCKS):
-        found = run_forward(layer_no, groups, dir_no, below, view)
-        x = found[0] if layer_no else stream
-        if layer_no:
-            kept[-1][:0] = found[1:3]
-        h_all, coef, part = found[-3:]
-        kept.append([x, h_all, coef])
-        below = (x, part, exchange(part))
+        after, normed, scale, h_all, coef = run_forward(layer_no, groups, x, view)
+        kept.append((x, normed, scale, h_all, coef))
+        x = after
 
     position = by_row(jnp.arange(samples).astype(F32))
     valid = jnp.where(position < scalar[1], 1.0, 0.0) * weight
@@ -880,29 +1004,20 @@
     by_source = jnp.pad(jnp.eye(SOURCES, dtype=F32), ((0, 0), (0, 128 - SOURCES)))
     taps = (by_source[:, None, None, :] * decoder[None, :, :, None]).reshape(wide, 256)
     active_wide = jnp.broadcast_to(jnp.repeat(active, FILTERS)[None], (8, wide))
-    normed, scale, grad, head_grads, grad_encoded, loss = run_head(
-        groups, below, view, stream, column, active_wide, masker, taps
-    )
-    kept[-1][:0] = [normed, scale]
+    grad, head_grads, grad_encoded, loss = run_head(groups, x, stream, column, active_wide, masker, taps)
     lane = jnp.arange(128)
     count_part = jnp.sum(scalars[:, 1]) / frames_size
     loss = jnp.where(lane == 0, loss, jnp.where(lane == 1, count_part, 0.0))
     signal_column = jnp.pad(jnp.stack([mix_row, follow_row], 1), ((0, 0), (0, 126)))
     encoder_rows = jnp.pad(encoder.T, ((0, 6), (0, 0)))
     sums = [None] * (2 * BLOCKS)
-    before = (grad, head_grads)
+    extras = {0: (signal_column, grad_encoded, encoder_rows, loss), 2 * BLOCKS - 1: (head_grads,)}
     for layer_no in reversed(range(2 * BLOCKS)):
-        normed, scale, x, h_all, coef = kept[layer_no]
-        if layer_no == 0:
-            before = before + (signal_column, grad_encoded, encoder_rows, loss)
-        found = run_backward(layer_no, groups, dir_no, before + (normed, scale, x, h_all), coef, view)
-        sums[layer_no] = found[-1]
-        if layer_no == 2 * BLOCKS - 1:
-            dx = found[0]
-        elif layer_no:
-            grad, dx = found[:2]
+        *found, sums[layer_no] = run_backward(
+            layer_no, groups, grad, kept[layer_no], view, extras.get(layer_no, ())
+        )
         if layer_no:
-            before = (grad, dx, exchange(dx))
+            grad = found[0]
     *updated, stats = run_finish(sums, params, first_moment, second_moment)
     return (*updated, stats[0, 2], stats[0, :2])
 

time: 410 us -> 388 us (0.946)
  the two profiles are of different devices: /device:TPU:25 before, /device:TPU:0 now
where the time goes in v2:
time: 388 us; the launch traced here: 382 us
  Pallas kernels  294 us (76%)
  blocking collectives  42.8 us (11%)
  local copies, waits for them, and re-layouts  21.6 us (6%)
  between operations  15.2 us (4%)
  other arithmetic  7.48 us (2%)
    pallas_call x4, Pallas kernels, run_backward(): pl.pallas_call(functools.partial(backward_kernel, layer_no, groups, steps...  130 us
    pallas_call x4, Pallas kernels, run_forward(): pl.pallas_call(functools.partial(forward_kernel, layer_no, groups, steps)...  97 us
    pallas_call x1, Pallas kernels, run_finish(): pl.pallas_call(functools.partial(finish_kernel, chips, depths, entries, w...  54.4 us
    all_gather x1, blocking collectives, local(): signals = lax.all_gather(signals, 'frames', axis=2, tiled=True)  39 us
    pallas_call x1, Pallas kernels, run_head(): pl.pallas_call(functools.partial(head_kernel, groups), grid=(1,), in_spec...  13.1 us
    unnamed x19, local copies, waits for them, and re-layouts  8.06 us
  transfers between devices with their start and end apart: 1, of which 0 were waited for; matrix products, arithmetic and copies ran while one was open for 3% of the time, Pallas kernels for 0%

profile of v2, /device:TPU:0, one launch (start us, length us, event | category | flops | bytes accessed | tf_op | source)
XLA Modules:
  0.0 381.6 jit_solution(9209390536910157136)
XLA Ops:
  7.3 2.1 reshape.167
  9.5 1.9 all-gather.1
  11.4 0.3 copy.68
  11.7 0.3 copy.69
  11.9 0.6 pad_maximum_fusion
  12.5 39.0 %all_gather.12 = f32[2,4,2000]{1,0,2:T(2,128)S(1)} all-gather(f32[2,4,500]{1,0,2:T(2,128)S(1)} %pad_maximum_fusion), channel_id=1, replica_groups=mesh['batch'=8,'frames'=4] {'frames'}, dimensions={2}, use_global_device_ids=true | all-gather | bytes 80000 | tf_op jit(solution)/shard_map/all_gather | solution.py:960
  51.5 1.7 copy.70
  53.3 1.9 all_gather.13
  56.4 0.1 reshape.155
  56.6 0.6 fusion.2
  57.1 0.7 fusion
  57.9 0.7 compare_select_fusion.3
  58.6 0.4 copy.77
  59.2 0.4 copy.79
  59.6 1.1 pad.25.column_ref
  60.6 1.1 pad.28.refs_7_
  61.7 0.7 slice_reduce_fusion.2
  63.1 0.7 fusion.1
  63.8 0.8 slice.91
  64.6 0.1 slice.72
  64.8 0.2 slice_reduce_fusion.1
  65.0 0.6 multiply_add_fusion
  65.6 0.6 compare_select_fusion
  66.3 0.7 compare_select_fusion.1
  67.0 1.4 select_maximum_fusion.refs_0_.stream_ref.refs_3_
  68.4 28.5 %forward_intra.2 = (f32[2240,128]{1,0:T(8,128)}, f32[2240,128]{1,0:T(8,128)}, f32[8,128]{1,0:T(8,128)}, f32[100,40,128]{2,1,0:T(8,128)}, f32[100,6,40,128]{3,2,1,0:T(8,128)}) custom-call(f32[2240,128]{1,0:T(8,128)} %select_maximum_fusion.refs_0_.stream_ref.refs_3_, f32[6792,128]{1,0:T(8,128)} %bitcast.37), custom_call_target="tpu_custom_call" | custom-call | tf_op jit(solution)/shard_map/forward_intra/pallas_call | solution.py:820
  96.9 19.9 %forward_inter.2 = (f32[2240,128]{1,0:T(8,128)}, f32[2240,128]{1,0:T(8,128)}, f32[8,128]{1,0:T(8,128)}, f32[40,112,128]{2,1,0:T(8,128)}, f32[40,6,112,128]{3,2,1,0:T(8,128)}) custom-call(f32[2240,128]{1,0:T(8,128)} %get-tuple-element.41.refs_0_.refs_3_, f32[6792,128]{1,0:T(8,128)} %bitcast.38), custom_call_target="tpu_custom_call" | custom-call | tf_op jit(solution)/shard_map/forward_inter/pallas_call | solution.py:820
  116.8 28.6 %forward_intra.3 = (f32[2240,128]{1,0:T(8,128)}, f32[2240,128]{1,0:T(8,128)}, f32[8,128]{1,0:T(8,128)}, f32[100,40,128]{2,1,0:T(8,128)}, f32[100,6,40,128]{3,2,1,0:T(8,128)}) custom-call(f32[2240,128]{1,0:T(8,128)} %get-tuple-element.42.refs_0_.refs_3_, f32[6792,128]{1,0:T(8,128)} %bitcast.39), custom_call_target="tpu_custom_call" | custom-call | tf_op jit(solution)/shard_map/forward_intra/pallas_call | solution.py:820
  145.4 20.0 %forward_inter.3 = (f32[2240,128]{1,0:T(8,128)}, f32[2240,128]{1,0:T(8,128)}, f32[8,128]{1,0:T(8,128)}, f32[40,112,128]{2,1,0:T(8,128)}, f32[40,6,112,128]{3,2,1,0:T(8,128)}) custom-call(f32[2240,128]{1,0:T(8,128)} %get-tuple-element.43.refs_0_.refs_3_, f32[6792,128]{1,0:T(8,128)} %bitcast.40), custom_call_target="tpu_custom_call" | custom-call | tf_op jit(solution)/shard_map/forward_inter/pallas_call | solution.py:820
  165.5 0.1 slice.83
  165.6 0.1 broadcast_multiply_fusion
  165.7 0.7 copy.89
  166.4 0.7 reshape.156.masker_ref
  167.1 0.6 pad.29.refs_9_
  167.7 0.6 broadcast_in_dim.56.active_ref
  168.3 13.1 %head.1 = (f32[2240,128]{1,0:T(8,128)}, f32[160,128]{1,0:T(8,128)}, f32[2000,64]{1,0:T(8,128)}, f32[8,128]{1,0:T(8,128)}) custom-call(f32[2240,128]{1,0:T(8,128)} %get-tuple-element.44.sep, f32[2240,128]{1,0:T(8,128)} %select_maximum_fusion.refs_0_.stream_ref.refs_3_, f32[2000,128]{1,0:T(8,128)} %pad.25.column_ref, f32[8,192]{1,0:T(8,128)} %broadcast_in_dim.56.active_ref, ...), custom_call_target="tpu_custom_call" | custom-call | tf_op jit(solution)/shard_map/head/pallas_call | solution.py:889
  181.5 1.3 broadcast_select_fusion.refs_10_
  182.7 30.9 %backward_inter.2 = (f32[2240,128]{1,0:T(8,128)}, f32[1840,128]{1,0:T(8,128)}) custom-call(f32[2240,128]{1,0:T(8,128)} %get-tuple-element.45.refs_0_, f32[2240,128]{1,0:T(8,128)} %get-tuple-element.46.refs_1_, f32[8,128]{1,0:T(8,128)} %get-tuple-element.47.refs_2_, f32[2240,128]{1,0:T(8,128)} %get-tuple-element.43.refs_0_.refs_3_, ...), custom_call_target="tpu_custom_call" | custom-call | tf_op jit(solution)/shard_map/backward_inter/pallas_call | solution.py:856
  213.6 34.6 %backward_intra.2 = (f32[2240,128]{1,0:T(8,128)}, f32[1680,128]{1,0:T(8,128)}) custom-call(f32[2240,128]{1,0:T(8,128)} %get-tuple-element.51.refs_0_, f32[2240,128]{1,0:T(8,128)} %get-tuple-element.52.refs_1_, f32[8,128]{1,0:T(8,128)} %get-tuple-element.53.refs_2_, f32[2240,128]{1,0:T(8,128)} %get-tuple-element.42.refs_0_.refs_3_, ...), custom_call_target="tpu_custom_call" | custom-call | tf_op jit(solution)/shard_map/backward_intra/pallas_call | solution.py:856
  248.2 31.1 %backward_inter.3 = (f32[2240,128]{1,0:T(8,128)}, f32[1680,128]{1,0:T(8,128)}) custom-call(f32[2240,128]{1,0:T(8,128)} %get-tuple-element.56.refs_0_, f32[2240,128]{1,0:T(8,128)} %get-tuple-element.57.refs_1_, f32[8,128]{1,0:T(8,128)} %get-tuple-element.58.refs_2_, f32[2240,128]{1,0:T(8,128)} %get-tuple-element.41.refs_0_.refs_3_, ...), custom_call_target="tpu_custom_call" | custom-call | tf_op jit(solution)/shard_map/backward_inter/pallas_call | solution.py:856
  279.3 33.2 %backward_intra.3.r0 = f32[1688,128]{1,0:T(8,128)} custom-call(f32[2240,128]{1,0:T(8,128)} %get-tuple-element.61.refs_0_, f32[2240,128]{1,0:T(8,128)} %get-tuple-element.62.refs_1_, f32[8,128]{1,0:T(8,128)} %get-tuple-element.63.refs_2_, f32[2240,128]{1,0:T(8,128)} %select_maximum_fusion.refs_0_.stream_ref.refs_3_, ...), custom_call_target="tpu_custom_call" | custom-call | tf_op jit(solution)/shard_map/backward_intra/pallas_call | solution.py:856
  312.6 54.4 %finish.1 = (f32[849,128]{1,0:T(8,128)}, bf16[849,128]{1,0:T(8,128)(2,1)}, f32[849,128]{1,0:T(8,128)}, f32[849,128]{1,0:T(8,128)}, f32[8,128]{1,0:T(8,128)}) custom-call(f32[1688,128]{1,0:T(8,128)} %backward_intra.3.r0, f32[1680,128]{1,0:T(8,128)} %get-tuple-element.68.r1, f32[1680,128]{1,0:T(8,128)} %get-tuple-element.69.r2, ...), custom_call_target="tpu_custom_call" | custom-call | tf_op jit(solution)/shard_map/finish/pallas_call | solution.py:924
  367.0 1.3 slice.85
  368.4 1.2 slice_bitcast_fusion
  369.6 1.8 copy.94
  371.4 1.6 copy.95
  373.0 0.8 copy.96
  373.8 0.8 copy.97
  (44 shorter events, 1.9 us)
Async XLA Ops:
  7.2 2.2 copy-start.5
  7.2 2.2 copy-start.4
  7.2 4.2 %copy-start.3 = (f32[2,500]{1,0:T(2,128)S(1)}, f32[2,500]{1,0:T(2,128)}, u32[]{:S(2)}) copy-start(f32[2,500]{1,0:T(2,128)} %param.10) | copy-start | bytes 12004
  7.2 4.5 %copy-start.2 = (f32[2,3,500]{2,0,1:T(2,128)S(1)}, f32[2,3,500]{2,0,1:T(2,128)}, u32[]{:S(2)}) copy-start(f32[2,3,500]{2,0,1:T(2,128)} %param.11) | copy-start | bytes 36004
  7.2 55.9 %all-gather.4.cloned.1.call-start = ((), (), s32[]{:S(2)}) async-start(), calls=%async_computation | async-start | bytes 3912192 | tf_op jit(solution)/shard_map/all_gather | solution.py:947
  367.0 6.0 %copy-start.1 = (f32[849,128]{1,0:T(8,128)S(1)}, f32[849,128]{1,0:T(8,128)}, u32[]{:S(2)}) copy-start(f32[849,128]{1,0:T(8,128)} %get-tuple-element.73) | copy-start | bytes 1304068
  367.0 6.8 %copy-start = (f32[849,128]{1,0:T(8,128)S(1)}, f32[849,128]{1,0:T(8,128)}, u32[]{:S(2)}) copy-start(f32[849,128]{1,0:T(8,128)} %get-tuple-element.74) | copy-start | bytes 1304068
Sparse Core Ops, SparseCore 0:
  10.5 36.4 all-gather.3

commit v3 on v2

--- a/solution.py
+++ b/solution.py
@@ -59,7 +59,13 @@
 VEC_ROW = PROJ_ROWS + 128
 LAYER_ROWS = 1680
 HEAD_ROWS = 160
+OWN_PROJ = SIDE_ROWS
+OWN_VEC = SIDE_ROWS + 64
+OWN_EXTRA = SIDE_ROWS + 68
+OWN_ROWS = (OWN_EXTRA + 8, OWN_EXTRA, OWN_EXTRA, OWN_EXTRA + HEAD_ROWS)
 WINDOW = 1688
+TAIL_ROW = 6688
+TAIL_ROWS = 104
 
 
 def window(layer_no):
@@ -135,7 +141,13 @@
 VEC_ROW = PROJ_ROWS + 128
 LAYER_ROWS = 1680
 HEAD_ROWS = 160
+OWN_PROJ = SIDE_ROWS
+OWN_VEC = SIDE_ROWS + 64
+OWN_EXTRA = SIDE_ROWS + 68
+OWN_ROWS = (OWN_EXTRA + 8, OWN_EXTRA, OWN_EXTRA, OWN_EXTRA + HEAD_ROWS)
 WINDOW = 1688
+TAIL_ROW = 6688
+TAIL_ROWS = 104
 
 
 def window(layer_no):
@@ -219,15 +231,130 @@
     return copy
 
 
-def swap_with_sibling(src_ref, dst_ref, sems):
+def swap_with_sibling(src_ref, dst_ref, sems, greeted=False):
     device, barrier = greet_sibling()
-    pl.semaphore_wait(barrier, 1)
+    if not greeted:
+        pl.semaphore_wait(barrier, 1)
     copy = pltpu.make_async_remote_copy(
         src_ref=src_ref, dst_ref=dst_ref, send_sem=sems.at[0], recv_sem=sems.at[1],
         device_id=device, device_id_type=pl.DeviceIdType.MESH,
     )
     copy.start()
-    copy.wait()
+    return copy
+
+
+def reduced_rows(rows, chips, depths):
+    return -(-rows // (8 * chips * depths)) * 8 * chips * depths
+
+
+def reducer_scratch(rows, chips, depths):
+    quarter = rows // chips
+    part = quarter // depths
+    sems = pltpu.SemaphoreType.DMA
+    return [
+        pltpu.VMEM((2, rows, 128), F32), pltpu.VMEM((chips - 1, quarter, 128), F32), pltpu.VMEM((quarter, 128), F32),
+        pltpu.VMEM((depths - 1, part, 128), F32), pltpu.VMEM((part, 128), F32), pltpu.VMEM((quarter, 128), F32),
+        sems((2, chips - 1)), sems((2, depths - 1)), sems((2, depths - 1)), sems((2, chips - 1)), sems((2, 1)),
+    ]
+
+
+def greet_all(chips, depths):
+    b = lax.axis_index("batch")
+    z = lax.axis_index("frames")
+    barrier = pltpu.get_barrier_semaphore()
+    devices = [(b + 1 - 2 * lax.rem(b, 2), z)]
+    devices += [(lax.rem(b + 2 * step, 2 * chips), z) for step in range(1, chips)]
+    devices += [(b, lax.rem(z + step, depths)) for step in range(1, depths)]
+    for device in devices:
+        pl.semaphore_signal(barrier, inc=1, device_id=device, device_id_type=pl.DeviceIdType.MESH)
+    return barrier, len(devices)
+
+
+def reducer(src, chips, depths, refs):
+    red, plane_in, mine, depth_in, piece, joined, s_plane, s_depth, s_spread, s_gather, s_back = refs
+    b = lax.axis_index("batch")
+    z = lax.axis_index("frames")
+    core = lax.rem(b, 2)
+    chip = lax.div(b, 2)
+    quarter = mine.shape[0]
+    part = piece.shape[0]
+
+    def rows(at, count):
+        return pl.ds(pl.multiple_of(at, 8), count)
+
+    def send(src_ref, dst_ref, sems, slot, device):
+        return pltpu.make_async_remote_copy(
+            src_ref=src_ref, dst_ref=dst_ref, send_sem=sems.at[0, slot], recv_sem=sems.at[1, slot],
+            device_id=device, device_id_type=pl.DeviceIdType.MESH,
+        )
+
+    over_plane = [(step, (lax.rem(b + 2 * step, 2 * chips), z)) for step in range(1, chips)]
+    over_depth = [(step, (b, lax.rem(z + step, depths))) for step in range(1, depths)]
+    own = rows(chip * quarter, quarter)
+    mine_at = rows(z * part, part)
+
+    def plane():
+        return [
+            send(src.at[rows(lax.rem(chip + step, chips) * quarter, quarter)], plane_in.at[step - 1], s_plane, step - 1, to)
+            for step, to in over_plane
+        ]
+
+    def scatter():
+        return [
+            send(mine.at[rows(lax.rem(z + step, depths) * part, part)], depth_in.at[step - 1], s_depth, step - 1, to)
+            for step, to in over_depth
+        ]
+
+    def spread():
+        return [send(piece, joined.at[mine_at], s_spread, step - 1, to) for step, to in over_depth]
+
+    def gather():
+        return [send(joined, red.at[core, own], s_gather, step - 1, to) for step, to in over_plane]
+
+    def back():
+        return [send(red.at[core], red.at[core], s_back, 0, (b + 1 - 2 * core, z))]
+
+    def start(copies):
+        for copy in copies:
+            copy.start()
+
+    def wait(copies):
+        for copy in copies:
+            copy.wait()
+
+    def first():
+        start(plane())
+
+    def third():
+        wait(plane())
+        total = src[own, :]
+        for step in range(1, chips):
+            total = total + plane_in[step - 1]
+        mine[...] = total
+        start(scatter())
+
+    def fourth():
+        wait(scatter())
+        total = mine[mine_at, :]
+        for step in range(1, depths):
+            total = total + depth_in[step - 1]
+        piece[...] = total
+        joined[mine_at, :] = total
+        start(spread())
+
+    def fifth():
+        wait(spread())
+        red[core, own] = joined[...]
+        start(gather())
+
+    def sixth():
+        wait(gather())
+        start(back())
+
+    def last():
+        wait(back())
+
+    return [first, third, fourth, fifth, sixth, last]
 
 
 def forward_kernel(layer_no, groups, steps, *refs):
@@ -343,12 +470,12 @@
     def _():
         for task in after(chunks - 1, h_b):
             task()
-        swap_with_sibling(part_ref, peer_ref, sems)
+        swap_with_sibling(part_ref, peer_ref, sems).wait()
         _, base, odd = window(layer_no)
         norm_stage(x_ref, part_ref, peer_ref, window_s, base, odd, valid, normed_ref, scale_ref, next_ref)
 
 
-def backward_kernel(layer_no, groups, steps, *refs):
+def backward_kernel(layer_no, groups, steps, chips, depths, *refs):
     inter = layer_no % 2 == 1
     last_layer = layer_no == 2 * BLOCKS - 1
     g_ref, normed_ref, scale_ref, x_ref, h_ref, coef_ref, flat_ref, *rest = refs
@@ -356,11 +483,16 @@
         hg_ref, *rest = rest
     if layer_no == 0:
         column_ref, denc_ref, encoder_ref, loss_ref, *rest = rest
-    else:
+    if not last_layer:
+        upper_ref, *rest = rest
+    if layer_no:
         below_ref, *rest = rest
+    if not last_layer:
+        red_ref, *rest = rest
     (grad_ref,
      wi2, wil, wrw, wrt, pj2, pjl, proj_s, dmx, dh_a, dh_b, dz_a, dz_b, dc_s, awin, aproj, abias,
-     dx_ref, peer_ref, sems, window_s, fetch_sem) = rest
+     dx_ref, peer_ref, sems, window_s, fetch_sem, *rest) = rest
+    stages = [] if last_layer else reducer(upper_ref, chips, depths, rest)
     turn_no = pl.program_id(0)
     last_turn = pl.num_programs(0) - 1
     chunks = 2 * pl.num_programs(0)
@@ -459,9 +591,13 @@
 
     @pl.when(turn_no == 0)
     def _():
-        if layer_no:
+        if last_layer:
             device, barrier = greet_sibling()
             pl.semaphore_signal(barrier, inc=1, device_id=device, device_id_type=pl.DeviceIdType.MESH)
+        else:
+            barrier, count = greet_all(chips, depths)
+            pl.semaphore_wait(barrier, count)
+            stages[0]()
         fetch(flat_ref, layer_no, window_s, fetch_sem).wait()
         dx_ref[...] = jnp.zeros_like(dx_ref)
         _, base, odd = window(layer_no)
@@ -499,13 +635,16 @@
             found = lead * jnp.sum(array, 0, keepdims=True)
             return found[:, :FILTERS] + found[:, FILTERS:]
 
-        grad_ref[VEC_ROW:VEC_ROW + 1] = jnp.concatenate([fold(dmixed), fold(g * normed)], 1)
-        grad_ref[VEC_ROW + 1:VEC_ROW + 2] = jnp.concatenate([fold(g), jnp.zeros((1, FILTERS), F32)], 1)
+        grad_ref[OWN_VEC:OWN_VEC + 1] = jnp.concatenate([fold(dmixed), fold(g * normed)], 1)
+        grad_ref[OWN_VEC + 1:OWN_VEC + 2] = jnp.concatenate([fold(g), jnp.zeros((1, FILTERS), F32)], 1)
         if last_layer:
-            grad_ref[LAYER_ROWS:] = hg_ref[...] * lead
+            grad_ref[OWN_EXTRA:OWN_EXTRA + HEAD_ROWS] = hg_ref[...] * lead
 
         for task in before(0, dh_a):
             task()
+
+    for stage, at in zip(stages[1:], (2, 3, 4) if inter else (3, 5, 6, 9)):
+        pl.when(turn_no == at)(stage)
 
     dz, dc_next = dz_b[:rows], dc_s[...]
     dz, dc_next = walk(dh_a, dz_a, dz, dc_next, 1, after(2 * turn_no - 1, dz_b) + before(2 * turn_no + 1, dh_b))
@@ -517,45 +656,72 @@
         for task in after(chunks - 1, dz_b):
             task()
         if layer_no:
-            swap_with_sibling(dx_ref, peer_ref, sems)
+            swap = swap_with_sibling(dx_ref, peer_ref, sems, not last_layer)
+        for stage in stages[4:] if inter else stages[5:]:
+            stage()
+        if not last_layer:
+            red_ref[...] = rest[0][...]
+        if layer_no:
+            swap.wait()
             below_ref[:valid] = g_ref[:valid] + dx_ref[:valid] + peer_ref[:valid]
             below_ref[valid:] = jnp.zeros((below_ref.shape[0] - valid, 128), F32)
-        at = SIDE_ROWS * dir_no
         for q in range(4):
             cut = slice(q * UNITS, (q + 1) * UNITS)
-            grad_ref[pl.ds(at + q, FILTERS, stride=4), :] = awin[:FILTERS, cut]
-            grad_ref[pl.ds(at + 256 + q, UNITS, stride=4), :] = awin[2 * FILTERS:, cut]
-            grad_ref[pl.ds(at + 768 + q, 1), :] = abias[0:1, cut]
+            grad_ref[pl.ds(q, FILTERS, stride=4), :] = awin[:FILTERS, cut]
+            grad_ref[pl.ds(256 + q, UNITS, stride=4), :] = awin[2 * FILTERS:, cut]
+            grad_ref[768 + q:769 + q, :] = abias[0:1, cut]
         proj_s[...] = aproj[:UNITS] + pltpu.roll(aproj[UNITS:], FILTERS, 1) if inter else aproj[...]
         even = proj_s[pl.ds(0, 64, stride=2), :]
         odd_rows = proj_s[pl.ds(1, 64, stride=2), :]
-        grad_ref[pl.ds(PROJ_ROWS + 64 * dir_no, 64), :] = jnp.concatenate(
+        grad_ref[OWN_PROJ:OWN_VEC, :] = jnp.concatenate(
             [even[:, :FILTERS], odd_rows[:, :FILTERS]], 1
         )
         if layer_no == 0:
             lead = jnp.where(dir_no == 0, 1.0, 0.0)
             streams = lead * g_ref[:valid] + dx_ref[:valid]
             column = column_ref[...]
-            mix, following = column[:, 0:1], column[:, 1:2]
-            raw = mix * encoder_ref[0:1] + following * encoder_ref[1:2]
+            mix, following = column[:, 4:5], column[:, 5:6]
+            raw = mix * encoder_ref[0:1, :FILTERS] + following * encoder_ref[1:2, :FILTERS]
             group_at = lax.broadcasted_iota(jnp.int32, (valid, FILTERS), 0) % groups
             shifted = jnp.where(group_at == 0, 0.0, pltpu.roll(pltpu.roll(streams, FILTERS, 1), 1, 0)[:, :FILTERS])
             grad_raw = (streams[:, :FILTERS] + shifted + lead * denc_ref[...]) * jax.nn.sigmoid(raw)
-            grad_ref[LAYER_ROWS:LAYER_ROWS + 1] = jnp.concatenate(
+            grad_ref[OWN_EXTRA:OWN_EXTRA + 1] = jnp.concatenate(
                 [jnp.sum(grad_raw * mix, 0, keepdims=True), jnp.sum(grad_raw * following, 0, keepdims=True)], 1
             )
-            grad_ref[LAYER_ROWS + 1:LAYER_ROWS + 2] = loss_ref[0:1] * lead
-
-
-def head_kernel(groups, sep, stream_ref, column_ref, active_ref, masker_ref, decoder_ref,
+            grad_ref[OWN_EXTRA + 1:OWN_EXTRA + 2] = loss_ref[0:1] * lead
+
+
+def head_kernel(groups, sep, stream_ref, column_ref, active_ref, note_ref, flat_ref,
                 g_ref, hg_ref, denc_ref, loss_ref,
-                sig_s, now_s, before_s, slope_s, mk2, mkl, mt2, mtl, dk2, dkl, dt2, dtl, amask, adec, m_low, m_top):
+                sig_s, now_s, before_s, slope_s, mk2, mkl, mt2, mtl, dk2, dkl, dt2, dtl, amask, adec, m_low, m_top, tail_s, tail_sem):
     valid = HOP * groups
     block = 10 * groups
-    put_split(masker_ref[...], mk2, mkl)
-    put_split(masker_ref[...].T, mt2, mtl)
-    put_split(decoder_ref[...], dk2, dkl)
-    put_split(decoder_ref[...].T, dt2, dtl)
+    tail = pltpu.make_async_copy(flat_ref.at[pl.ds(TAIL_ROW, TAIL_ROWS)], tail_s, tail_sem)
+    tail.start()
+    tail.wait()
+    first, second, third = (tail_s[pl.ds(6695 - TAIL_ROW + n, 32, stride=3), :] for n in range(3))
+    m_low[pl.ds(0, 32, stride=2), :] = first
+    m_low[pl.ds(1, 32, stride=2), :] = jnp.concatenate([second[:, FILTERS:], third[:, :FILTERS]], 1)
+    m_top[pl.ds(0, 32, stride=2), :] = second
+    m_top[pl.ds(1, 32, stride=2), :] = pltpu.roll(third, FILTERS, 1)
+    masker = jnp.concatenate([m_low[...], m_top[:, :FILTERS]], 1)
+    taps = tail_s[6791 - TAIL_ROW:6792 - TAIL_ROW]
+    lane_at = lax.broadcasted_iota(jnp.int32, (FILTERS, 128), 1)
+    row_at = lax.broadcasted_iota(jnp.int32, (FILTERS, 128), 0)
+    upright = [
+        jnp.sum(jnp.where(lane_at == 2 * row_at + tap, taps, 0.0), 1, keepdims=True) for tap in range(2)
+    ]
+    decoder = jnp.concatenate(
+        [
+            jnp.concatenate([jnp.where(lane_at == j, column, 0.0) for column in upright], 1)
+            for j in range(SOURCES)
+        ],
+        0,
+    )
+    put_split(masker, mk2, mkl)
+    put_split(masker.T, mt2, mtl)
+    put_split(decoder, dk2, dkl)
+    put_split(decoder.T, dt2, dtl)
     amask[...] = jnp.zeros_like(amask)
     adec[...] = jnp.zeros_like(adec)
     active = active_ref[0:1]
@@ -597,7 +763,8 @@
         return total + jnp.sum(kept * (root - 1.0), 0, keepdims=True)
 
     total = lax.fori_loop(0, HOP // 10, losses, jnp.zeros((1, 128), F32))
-    loss_ref[...] = jnp.broadcast_to(jnp.sum(total, 1, keepdims=True), loss_ref.shape)
+    first_lane = lax.broadcasted_iota(jnp.int32, (8, 128), 1) == 0
+    loss_ref[...] = jnp.where(first_lane, jnp.sum(total, 1, keepdims=True), note_ref[...])
     slope_s[valid:] = jnp.where(at == groups - 1, 0.0, pltpu.roll(slope_s[:groups], groups - 1, 0))
 
     def back(n, carry):
@@ -642,158 +809,244 @@
 def assemble(flat, layers):
     lane = lax.broadcasted_iota(jnp.int32, (FILTERS, 128), 1)
     row = lax.broadcasted_iota(jnp.int32, (FILTERS, 128), 0)
-    encoder = jnp.broadcast_to(layers[0][LAYER_ROWS:LAYER_ROWS + 1], (FILTERS, 128))
-    first_tap = jnp.sum(jnp.where(lane == row, encoder, 0.0), 1, keepdims=True)
-    second_tap = jnp.sum(jnp.where(lane == row + FILTERS, encoder, 0.0), 1, keepdims=True)
 
     def interleave(a, b):
         return jnp.sum(jnp.where(lane == 2 * row, a, jnp.where(lane == 2 * row + 1, b, 0.0)), 0, keepdims=True)
 
-    flat[0:1] = interleave(first_tap, second_tap)
     for layer_no, ref in enumerate(layers):
+        if ref is None:
+            continue
         first, inner, odd = window(layer_no)
-        base = first + inner
-        if odd:
-            whole_rows = ref[:LAYER_ROWS - 6]
-            turned = pltpu.roll(whole_rows, FILTERS, 1)
-            flat[base:base + 1, FILTERS:] = turned[0:1, FILTERS:]
-            wide_low = lax.broadcasted_iota(jnp.int32, (LAYER_ROWS - 7, 128), 1) < FILTERS
-            flat[base + 1:base + LAYER_ROWS - 6] = jnp.where(wide_low, turned[:-1], turned[1:])
-        else:
-            flat[base:base + LAYER_ROWS - 6] = ref[:LAYER_ROWS - 6]
-    flat[6695:6791] = layers[3][LAYER_ROWS:LAYER_ROWS + 96]
-    decoder = layers[3][LAYER_ROWS + 96:LAYER_ROWS + HEAD_ROWS]
-    flat[6791:6792] = interleave(decoder[:, 0:1], decoder[:, 1:2])
-    flat[6792:] = jnp.zeros((flat.shape[0] - 6792, 128), F32)
-
-
-def finish_kernel(chips, depths, entries, width, r0, r1, r2, r3, p_ref, m_ref, v_ref,
-                  new_ref, half_ref, first_ref, second_ref, stats_ref,
-                  flat, pair_in, sent, plane_in, held, depth_in, mine, found, note, depth_notes, notes,
-                  pair_sem, plane_sem, depth_sem, spread_sem, note_sem, notes_sem):
+        at = first + inner
+        parts = [(ref[0, :OWN_PROJ], False), (ref[1, :OWN_PROJ], False), (ref[0, OWN_PROJ:OWN_VEC], False)]
+        parts += [(ref[1, OWN_PROJ:OWN_VEC], False), (ref[0, OWN_VEC:OWN_VEC + 2], True)]
+        for rows, ends in parts:
+            count = rows.shape[0]
+            if odd:
+                turned = pltpu.roll(rows, FILTERS, 1) if count >= 8 else jnp.concatenate(
+                    [rows[:, FILTERS:], rows[:, :FILTERS]], 1
+                )
+                wide_low = lax.broadcasted_iota(jnp.int32, (count - 1, 128), 1) < FILTERS
+                flat[at:at + 1, FILTERS:] = turned[0:1, FILTERS:]
+                flat[at + 1:at + count] = jnp.where(wide_low, turned[:-1], turned[1:])
+                if not ends:
+                    flat[at + count:at + count + 1, :FILTERS] = turned[count - 1:, :FILTERS]
+            elif ends:
+                flat[at:at + 1] = rows[0:1]
+                flat[at + 1:at + 2, :FILTERS] = rows[1:2, :FILTERS]
+            else:
+                flat[at:at + count] = rows
+            at += count
+        if layer_no == 0:
+            encoder = ref[0, OWN_EXTRA:OWN_EXTRA + 1] + ref[1, OWN_EXTRA:OWN_EXTRA + 1]
+            encoder = jnp.broadcast_to(encoder, (FILTERS, 128))
+            first_tap = jnp.sum(jnp.where(lane == row, encoder, 0.0), 1, keepdims=True)
+            second_tap = jnp.sum(jnp.where(lane == row + FILTERS, encoder, 0.0), 1, keepdims=True)
+            flat[0:1] = interleave(first_tap, second_tap)
+        if layer_no == 2 * BLOCKS - 1:
+            flat[6695:6791] = ref[0, OWN_EXTRA:OWN_EXTRA + 96]
+            decoder = ref[0, OWN_EXTRA + 96:OWN_EXTRA + HEAD_ROWS]
+            flat[6791:6792] = interleave(decoder[:, 0:1], decoder[:, 1:2])
+            flat[6792:] = jnp.zeros((flat.shape[0] - 6792, 128), F32)
+
+
+def finish_kernel(chips, depths, entries, own_ref, r1, r2, r3, grad_ref, note_ref, flat, b1, b2, b3, sems, *rest):
+    b = lax.axis_index("batch")
+    barrier, count = greet_all(chips, depths)
+    pairs = ((r1, b1), (r2, b2), (r3, b3))
+    fetches = [pltpu.make_async_copy(src, dst, sems.at[n]) for n, (src, dst) in enumerate(pairs)]
+    for copy in fetches:
+        copy.start()
+    pl.semaphore_wait(barrier, count)
+    stages = reducer(own_ref, chips, depths, rest)
+    stages[0]()
+    for copy in fetches:
+        copy.wait()
+    assemble(flat, (None, b1, b2, b3))
+    for stage in stages[1:]:
+        stage()
+    r0 = rest[0]
+    assemble(flat, (r0, None, None, None))
+    note_ref[...] = jnp.zeros_like(note_ref)
+    squares = jnp.sum(jnp.sum(flat[...] * flat[...], 0, keepdims=True), 1, keepdims=True)
+    lane = lax.broadcasted_iota(jnp.int32, (1, 128), 1)
+    note_ref[0:1] = jnp.where(lane == 2, squares, r0[0, OWN_EXTRA + 1:OWN_EXTRA + 2])
+    rows = grad_ref.shape[0]
+    row_at, lane_at = lax.div(b * entries, 128), lax.rem(b * entries, 128)
+    gradient = flat[pl.ds(row_at, rows), :]
+    if entries % 128:
+        lane = lax.broadcasted_iota(jnp.int32, (rows, 128), 1)
+        turn = lax.rem(128 - lane_at, 128)
+        gradient = jnp.where(
+            lane < 128 - lane_at, pltpu.roll(gradient, turn, 1), pltpu.roll(flat[pl.ds(row_at + 1, rows), :], turn, 1)
+        )
+    grad_ref[...] = gradient
+
+
+def update_kernel(grad_ref, note_ref, p_ref, m_ref, v_ref, new_ref, half_ref, first_ref, second_ref, norm_ref, loss_ref):
+    rows = grad_ref.shape[0]
+    note = note_ref[0:1]
+    lane = lax.broadcasted_iota(jnp.int32, (1, 128), 1)
+    count = jnp.sum(jnp.where(lane == 1, note, 0.0), 1, keepdims=True)
+    norm = jnp.sqrt(jnp.sum(jnp.where(lane == 2, note, 0.0), 1, keepdims=True)) / count
+    norm_ref[0] = norm[0, 0]
+    loss_ref[0] = note[0, 0]
+    loss_ref[1] = note[0, 1]
+    clipped = grad_ref[...] / count * (CLIP_AT / jnp.maximum(norm, CLIP_AT))
+    new_first = BETA_ONE * m_ref[...].reshape(rows, 128) + (1.0 - BETA_ONE) * clipped
+    new_second = BETA_TWO * v_ref[...].reshape(rows, 128) + (1.0 - BETA_TWO) * clipped * clipped
+    step_size = (
+        new_first / (1.0 - BETA_ONE**STEP) / (jnp.sqrt(new_second / (1.0 - BETA_TWO**STEP)) + ADAM_EPS)
+    )
+    params = p_ref[...].reshape(rows, 128)
+    new_params = params - LEARN_RATE * (step_size + DECAY_RATE * params)
+    new_ref[...] = new_params.reshape(new_ref.shape)
+    half_ref[...] = new_params.astype(BF16).reshape(half_ref.shape)
+    first_ref[...] = new_first.reshape(first_ref.shape)
+    second_ref[...] = new_second.reshape(second_ref.shape)
+
+
+def start_kernel(chips, depths, items, groups, gathers, p_ref, mail_ref, *refs):
+    if gathers:
+        flat_ref, *refs = refs
+    else:
+        flat_ref = p_ref
+    (stream_ref, column_ref, active_ref, encoder_ref, note_ref,
+     inbox, planes, plane_sem, pair_sem, own_sem, mail_sem) = refs
     b = lax.axis_index("batch")
     z = lax.axis_index("frames")
     core = lax.rem(b, 2)
-    chip = b // 2
-    piece = width // depths
-    rows = p_ref.shape[0]
-
-    def start(shard):
-        return pl.multiple_of(shard * entries // 1024 * 8, 8)
+    chip = lax.div(b, 2)
+    sibling = (b + 1 - 2 * core, z)
+    entries = p_ref.shape[0]
+    copies = depths // (2 * items)
+    share = groups // depths
+    valid = HOP * groups
+    mail_rows = mail_ref.shape[0] // items
+    mesh = pl.DeviceIdType.MESH
+
+    barrier = pltpu.get_barrier_semaphore()
+    for step in range(1, chips):
+        pl.semaphore_signal(barrier, inc=1, device_id=(lax.rem(b + 2 * step, 2 * chips), z), device_id_type=mesh)
+    for step in range(1, depths):
+        pl.semaphore_signal(barrier, inc=1, device_id=(b, lax.rem(z + step, depths)), device_id_type=mesh)
+    for step in range(depths):
+        pl.semaphore_signal(barrier, inc=1, device_id=(sibling[0], lax.rem(z + step, depths)), device_id_type=mesh)
+    pl.semaphore_wait(barrier, chips - 1 + 2 * depths - 1)
+
+    def shard(at):
+        return flat_ref.at[pl.ds(pl.multiple_of(at * entries, 128), entries)]
 
     def send(src, dst, sems, slot, device):
-        copy = pltpu.make_async_remote_copy(
+        return pltpu.make_async_remote_copy(
             src_ref=src, dst_ref=dst, send_sem=sems.at[0, slot], recv_sem=sems.at[1, slot],
-            device_id=device, device_id_type=pl.DeviceIdType.MESH,
+            device_id=device, device_id_type=mesh,
         )
-        copy.start()
-        return copy
-
-    barrier = pltpu.get_barrier_semaphore()
-    for step in range(1, 2 * chips):
-        pl.semaphore_signal(
-            barrier, inc=1, device_id=(lax.rem(b + step, 2 * chips), z), device_id_type=pl.DeviceIdType.MESH
+
+    if gathers:
+        across = [
+            send(p_ref, shard(b), plane_sem, step - 1, (lax.rem(b + 2 * step, 2 * chips), z))
+            for step in range(1, chips)
+        ]
+        for copy in across:
+            copy.start()
+        beside = [send(p_ref, shard(b), pair_sem, 0, sibling)]
+        beside[0].start()
+        own = pltpu.make_async_copy(p_ref, shard(b), own_sem)
+        own.start()
+    letters = []
+    for item in range(items):
+        for other in range(2):
+            for copy_no in range(copies):
+                depth = (items * core + item) * copies + copy_no
+                here = (core == other) & (z == depth)
+                src = mail_ref.at[pl.ds(item * mail_rows, mail_rows)]
+                far = pltpu.make_async_remote_copy(
+                    src_ref=src, dst_ref=inbox.at[z], send_sem=mail_sem.at[1, len(letters)], recv_sem=mail_sem.at[0, z],
+                    device_id=(2 * chip + other, depth), device_id_type=mesh,
+                )
+                near = pltpu.make_async_copy(src, inbox.at[z], mail_sem.at[0, z])
+
+                @pl.when(here)
+                def _():
+                    near.start()
+
+                @pl.when(jnp.logical_not(here))
+                def _():
+                    far.start()
+
+                letters.append((here, far))
+    for depth in range(depths):
+        pltpu.make_async_copy(inbox.at[depth], inbox.at[depth], mail_sem.at[0, depth]).wait()
+    for here, far in letters:
+        @pl.when(jnp.logical_not(here))
+        def _():
+            far.wait_send()
+
+    for signal in range(1 + SOURCES):
+        planes[signal] = jnp.concatenate(
+            [inbox[depth, signal * share:(signal + 1) * share] for depth in range(depths)], 0
         )
-    for step in range(1, depths):
-        pl.semaphore_signal(
-            barrier, inc=1, device_id=(b, lax.rem(z + step, depths)), device_id_type=pl.DeviceIdType.MESH
-        )
-    assemble(flat, (r0, r1, r2, r3))
-    note[...] = jnp.broadcast_to(r0[LAYER_ROWS + 1:LAYER_ROWS + 2], note.shape)
-    pl.semaphore_wait(barrier, 2 * chips - 1 + depths - 1)
-
-    order = list(range(1, chips)) + [0]
-    pairs = {}
-    for step in order:
-        other = 2 * lax.rem(chip + step, chips) + 1 - core
-        pairs[step] = send(
-            flat.at[pl.ds(start(other), width)], pair_in.at[step], pair_sem, step, (2 * chip + 1 - core, z)
-        )
-    loss_copies = [
-        send(note, depth_notes.at[step - 1], note_sem, step - 1, (b, lax.rem(z + step, depths)))
-        for step in range(1, depths)
-    ]
-    planes = []
-    for step in order:
-        pairs[step].wait_recv()
-        owner = 2 * lax.rem(chip + step, chips) + core
-        total = flat[pl.ds(start(owner), width), :] + pair_in[step]
-        if step:
-            sent[step - 1] = total
-            planes.append(send(sent.at[step - 1], plane_in.at[step - 1], plane_sem, step - 1, (owner, z)))
-        else:
-            held[...] = total
-    for step in order:
-        pairs[step].wait_send()
-    total = held[...]
-    for step in range(1, chips):
-        planes[step - 1].wait()
-        total = total + plane_in[step - 1]
-    held[...] = total
-    copies = []
-    for step in range(1, depths):
-        other = lax.rem(z + step, depths)
-        copies.append(
-            send(held.at[pl.ds(pl.multiple_of(other * piece, 8), piece)], depth_in.at[step - 1], depth_sem, step - 1, (b, other))
-        )
-    here = pl.ds(pl.multiple_of(z * piece, 8), piece)
-    total = held[here, :]
-    for step in range(1, depths):
-        copies[step - 1].wait()
-        total = total + depth_in[step - 1]
-    mine[...] = total
-    copies = [
-        send(mine, found.at[here], spread_sem, step - 1, (b, lax.rem(z + step, depths)))
-        for step in range(1, depths)
-    ]
-    losses = note[...]
-    for step in range(1, depths):
-        loss_copies[step - 1].wait()
-        losses = losses + depth_notes[step - 1]
-    for copy in copies:
-        copy.wait()
-    found[here, :] = mine[...]
-
-    at = b * entries - start(b) * 128
-    row_at, lane_at = at // 128, lax.rem(at, 128)
-    gradient = found[pl.ds(row_at, rows), :]
-    counted = gradient
-    if entries % 128:
-        lane = lax.broadcasted_iota(jnp.int32, (rows, 128), 1)
-        row = lax.broadcasted_iota(jnp.int32, (rows, 128), 0)
-        turn = lax.rem(128 - lane_at, 128)
-        gradient = jnp.where(
-            lane < 128 - lane_at, pltpu.roll(gradient, turn, 1), pltpu.roll(found[pl.ds(row_at + 1, rows), :], turn, 1)
-        )
-        counted = jnp.where(128 * row + lane < entries, gradient, 0.0)
-    squares = jnp.sum(jnp.sum(counted * counted, 0, keepdims=True), 1, keepdims=True)
-    lane = lax.broadcasted_iota(jnp.int32, note.shape, 1)
-    note[...] = jnp.where(lane == 2, squares, losses)
-    copies = [
-        send(note, notes.at[b], notes_sem, step - 1, (lax.rem(b + step, 2 * chips), z))
-        for step in range(1, 2 * chips)
-    ]
-    for copy in copies:
-        copy.wait()
-    notes[b] = note[...]
-    totals = notes[0]
-    for other in range(1, 2 * chips):
-        totals = totals + notes[other]
-    count = jnp.sum(jnp.where(lane == 1, totals, 0.0), 1, keepdims=True)[0:1]
-    norm = jnp.sqrt(jnp.sum(jnp.where(lane == 2, totals, 0.0), 1, keepdims=True)[0:1]) / count
-    stats_ref[...] = jnp.where(lane == 2, norm, totals)
-    clipped = gradient / count * (CLIP_AT / jnp.maximum(norm, CLIP_AT))
-    new_first = BETA_ONE * m_ref[...] + (1.0 - BETA_ONE) * clipped
-    new_second = BETA_TWO * v_ref[...] + (1.0 - BETA_TWO) * clipped * clipped
-    step_size = (
-        new_first / (1.0 - BETA_ONE**STEP) / (jnp.sqrt(new_second / (1.0 - BETA_TWO**STEP)) + ADAM_EPS)
-    )
-    params = p_ref[...]
-    new_params = params - LEARN_RATE * (step_size + DECAY_RATE * params)
-    new_ref[...] = new_params
-    half_ref[...] = new_params.astype(BF16)
-    first_ref[...] = new_first
-    second_ref[...] = new_second
+    facts = inbox[0, (1 + SOURCES) * share:(1 + SOURCES) * share + 1]
+    speakers, length = facts[:, 0:1], facts[:, 1:2]
+    whole_item = jnp.where(lax.rem(z, copies) == 0, 1.0, 0.0)
+    lead = jnp.where(core == 0, whole_item, 0.0)
+    lane = lax.broadcasted_iota(jnp.int32, (groups, 128), 1)
+    group = lax.broadcasted_iota(jnp.int32, (groups, 128), 0)
+    first_lane = lane[:8]
+    note_ref[...] = jnp.where(first_lane == 1, lead * length, 0.0)
+    wide = SOURCES * FILTERS
+    source = lax.broadcasted_iota(jnp.int32, (8, wide), 1) // FILTERS
+    active_ref[...] = jnp.where(source.astype(F32) < speakers, 1.0, 0.0)
+    mix = planes[0]
+    next_start = jnp.where(group == groups - 1, 0.0, pltpu.roll(mix, groups - 1, 0))
+    following = jnp.where(lane == HOP - 1, pltpu.roll(next_start, HOP - 1, 1), pltpu.roll(mix, 127, 1))
+
+    def columns(k, carry):
+        def take(array):
+            return jnp.broadcast_to(pltpu.roll(array, lax.rem(128 - k, 128), 1)[:, 0:1], (groups, 128))
+
+        found = jnp.where((group * HOP + k).astype(F32) < length, whole_item, 0.0)
+        for j in range(SOURCES):
+            found = jnp.where(lane == j, jnp.where(speakers > j, take(planes[1 + j]), 0.0), found)
+        found = jnp.where(lane == 4, take(mix), found)
+        found = jnp.where(lane == 5, take(following), found)
+        column_ref[pl.ds(pl.multiple_of(k * groups, 8), groups), :] = found
+        return carry
+
+    lax.fori_loop(0, HOP, columns, 0)
+
+    if gathers:
+        for step in range(1, chips):
+            across[step - 1].wait_recv()
+            at = lax.rem(b + 2 * chips - 2 * step, 2 * chips)
+            beside.append(send(shard(at), shard(at), pair_sem, step, sibling))
+            beside[-1].start()
+        for copy in across:
+            copy.wait_send()
+        own.wait()
+        for copy in beside:
+            copy.wait()
+
+    taps = flat_ref[0:128].reshape(1, 128)
+    at_lane = lax.broadcasted_iota(jnp.int32, (128, 128), 1)
+    at_row = lax.broadcasted_iota(jnp.int32, (128, 128), 0)
+    upright = jnp.sum(jnp.where(at_lane == at_row, taps, 0.0), 1, keepdims=True)
+    twice = 2 * lax.rem(at_lane, FILTERS)
+    tap_rows = [jnp.sum(jnp.where(at_row == twice + tap, upright, 0.0), 0, keepdims=True) for tap in range(2)]
+    encoder_ref[...] = jnp.where(at_row[:8] == 0, tap_rows[0], jnp.where(at_row[:8] == 1, tap_rows[1], 0.0))
+
+    def encode(k, carry):
+        rows = pl.ds(pl.multiple_of(k * groups, 8), groups)
+        column = column_ref[rows, :]
+        raw = column[:, 4:5] * tap_rows[0] + column[:, 5:6] * tap_rows[1]
+        encoded = jnp.maximum(raw, 0.0) + jnp.log1p(jnp.exp(-jnp.abs(raw)))
+        later = jnp.where(group == groups - 1, 0.0, pltpu.roll(encoded, groups - 1, 0))
+        stream_ref[rows, :] = jnp.where(lane < FILTERS, encoded, later)
+        return carry
+
+    lax.fori_loop(0, HOP, encode, 0, unroll=5)
+    stream_ref[valid:] = jnp.zeros((stream_ref.shape[0] - valid, 128), F32)
 
 
 def sizes(inter, groups):
@@ -804,6 +1057,47 @@
 
 def whole(shape):
     return pl.BlockSpec(shape, lambda j: (0,) * len(shape))
+
+
+def run_start(params, mixture, sources, speakers, lengths):
+    items, samples_here = mixture.shape
+    depths = lax.axis_size("frames")
+    chips = lax.axis_size("batch") // 2
+    groups = samples_here * depths // HOP
+    share = groups // depths
+    valid = HOP * groups
+    copies = depths // (2 * items)
+    signals = jnp.concatenate([mixture[:, None], sources], 1).reshape(items, (1 + SOURCES) * share, HOP)
+    facts = jnp.stack([speakers, lengths], 1).astype(F32)[:, None]
+    mail_rows = -(-((1 + SOURCES) * share + 1) // 8) * 8
+    mail = jnp.concatenate(
+        [jnp.pad(signals, ((0, 0), (0, 0), (0, 128 - HOP))), jnp.pad(facts, ((0, 0), (0, 0), (0, 126)))], 1
+    )
+    mail = jnp.pad(mail, ((0, 0), (0, mail_rows - mail.shape[1]), (0, 0))).reshape(items * mail_rows, 128)
+    stream_shape = (HALF_PAD * groups, 128)
+    out = [stream_shape, (valid, 128), (8, SOURCES * FILTERS), (8, 128), (8, 128)]
+    gathers = params.shape[0] % 128 == 0
+    if gathers:
+        out = [(params.shape[0] * 2 * chips,)] + out
+    else:
+        params = lax.all_gather(params, "batch", axis=0, tiled=True)
+    vmem = pl.BlockSpec(memory_space=pltpu.VMEM)
+    sems = pltpu.SemaphoreType.DMA
+    found = pl.pallas_call(
+        functools.partial(start_kernel, chips, depths, items, groups, gathers),
+        in_specs=[vmem] * 2,
+        out_specs=[vmem] * len(out),
+        out_shape=[jax.ShapeDtypeStruct(shape, F32) for shape in out],
+        scratch_shapes=[
+            pltpu.VMEM((depths, mail_rows, 128), F32), pltpu.VMEM((1 + SOURCES, groups, 128), F32),
+            sems((2, chips - 1)), sems((2, chips)), sems, sems((2, max(depths, 2 * items * copies))),
+        ],
+        compiler_params=pltpu.CompilerParams(
+            vmem_limit_bytes=VMEM_MAX, collective_id=10, has_side_effects=True
+        ),
+        name="start",
+    )(params, mail)
+    return found if gathers else [params, *found]
 
 
 def run_forward(layer_no, groups, stream, flat):
@@ -848,13 +1142,19 @@
     length, rows, steps = sizes(inter, groups)
     stream_shape = (HALF_PAD * groups, 128)
     count = length // (2 * steps)
-    out = [(LAYER_ROWS + (HEAD_ROWS if last_layer else 0 if layer_no else 8), 128)]
+    depths = lax.axis_size("frames")
+    chips = lax.axis_size("batch") // 2
+    out = [(reduced_rows(OWN_ROWS[layer_no], chips, depths), 128)]
+    scratch = []
+    if not last_layer:
+        upper_rows = reduced_rows(OWN_ROWS[layer_no + 1], chips, depths)
+        out = [(2, upper_rows, 128)] + out
+        scratch = reducer_scratch(upper_rows, chips, depths)
     if layer_no:
         out = [stream_shape] + out
     x, normed, scale, h_all, coef = kept
-    remote = dict(collective_id=6 + layer_no, has_side_effects=True) if layer_no else {}
     return pl.pallas_call(
-        functools.partial(backward_kernel, layer_no, groups, steps),
+        functools.partial(backward_kernel, layer_no, groups, steps, chips, depths),
         grid=(count,),
         in_specs=[whole(a.shape) for a in (grad, normed, scale, x, h_all)]
         + [pl.BlockSpec((2 * steps, 6, rows, UNITS), lambda j: (count - 1 - j, 0, 0, 0)), pl.BlockSpec(memory_space=pl.ANY)]
@@ -874,22 +1174,23 @@
             pltpu.VMEM((8, GATES), F32),
             pltpu.VMEM(stream_shape, F32), pltpu.VMEM(stream_shape, F32), pltpu.SemaphoreType.DMA((2,)),
             pltpu.VMEM((WINDOW, 128), F32), pltpu.SemaphoreType.DMA,
-        ],
-        compiler_params=pltpu.CompilerParams(vmem_limit_bytes=VMEM_MAX, **remote),
+        ]
+        + scratch,
+        compiler_params=pltpu.CompilerParams(vmem_limit_bytes=VMEM_MAX, collective_id=6 + layer_no, has_side_effects=True),
         name="backward_inter" if inter else "backward_intra",
     )(grad, normed, scale, x, h_all, coef, flat, *extra)
 
 
-def run_head(groups, separated, stream, column, active, masker, decoder):
+def run_head(groups, separated, stream, column, active, note, flat):
     valid = HOP * groups
     stream_shape = (HALF_PAD * groups, 128)
     out = [stream_shape, (HEAD_ROWS, 128), (valid, FILTERS), (8, 128)]
     wide = SOURCES * FILTERS
-    operands = (separated, stream, column, active, masker, decoder)
+    operands = (separated, stream, column, active, note)
     return pl.pallas_call(
         functools.partial(head_kernel, groups),
         grid=(1,),
-        in_specs=[whole(a.shape) for a in operands],
+        in_specs=[whole(a.shape) for a in operands] + [pl.BlockSpec(memory_space=pl.ANY)],
         out_specs=[whole(shape) for shape in out],
         out_shape=[jax.ShapeDtypeStruct(shape, F32) for shape in out],
         scratch_shapes=[
@@ -901,10 +1202,11 @@
             pltpu.VMEM((512, wide), BF16), pltpu.VMEM((256, wide), BF16),
             pltpu.VMEM((FILTERS, wide), F32), pltpu.VMEM((wide, 256), F32),
             pltpu.VMEM((FILTERS, 128), F32), pltpu.VMEM((FILTERS, 128), F32),
+            pltpu.VMEM((TAIL_ROWS, 128), F32), pltpu.SemaphoreType.DMA,
         ],
         compiler_params=pltpu.CompilerParams(vmem_limit_bytes=VMEM_MAX),
         name="head",
-    )(*operands)
+    )(*operands, flat)
 
 
 def run_finish(layers, params, first_moment, second_moment):
@@ -912,79 +1214,42 @@
     rows = -(-entries // 128)
     depths = lax.axis_size("frames")
     chips = lax.axis_size("batch") // 2
-    width = -(-(rows + 8) // (8 * depths)) * 8 * depths
-    shards = [
-        jnp.pad(a, (0, rows * 128 - entries)).reshape(rows, 128) for a in (params, first_moment, second_moment)
-    ]
-    out = [((rows, 128), F32), ((rows, 128), BF16), ((rows, 128), F32), ((rows, 128), F32), ((8, 128), F32)]
     vmem = pl.BlockSpec(memory_space=pltpu.VMEM)
-    block = (width, 128)
-    piece = (width // depths, 128)
-    sems = pltpu.SemaphoreType.DMA
-    found = pl.pallas_call(
-        functools.partial(finish_kernel, chips, depths, entries, width),
-        in_specs=[vmem] * 7,
-        out_specs=[vmem] * 5,
-        out_shape=[jax.ShapeDtypeStruct(shape, dtype) for shape, dtype in out],
-        scratch_shapes=[
-            pltpu.VMEM((6792 + width, 128), F32),
-            pltpu.VMEM((chips,) + block, F32), pltpu.VMEM((chips - 1,) + block, F32),
-            pltpu.VMEM((chips - 1,) + block, F32), pltpu.VMEM(block, F32),
-            pltpu.VMEM((depths - 1,) + piece, F32), pltpu.VMEM(piece, F32), pltpu.VMEM(block, F32),
-            pltpu.VMEM((8, 128), F32), pltpu.VMEM((depths - 1, 8, 128), F32), pltpu.VMEM((2 * chips, 8, 128), F32),
-            sems((2, chips)), sems((2, chips - 1)), sems((2, depths - 1)), sems((2, depths - 1)),
-            sems((2, depths - 1)), sems((2, 2 * chips - 1)),
-        ],
+    gradient, note = pl.pallas_call(
+        functools.partial(finish_kernel, chips, depths, entries),
+        in_specs=[vmem] + [pl.BlockSpec(memory_space=pl.ANY)] * 3,
+        out_specs=[vmem] * 2,
+        out_shape=[jax.ShapeDtypeStruct(shape, F32) for shape in ((rows, 128), (8, 128))],
+        scratch_shapes=[pltpu.VMEM((6808, 128), F32)]
+        + [pltpu.VMEM(a.shape, F32) for a in layers[1:]]
+        + [pltpu.SemaphoreType.DMA((3,))]
+        + reducer_scratch(layers[0].shape[0], chips, depths),
         compiler_params=pltpu.CompilerParams(
             vmem_limit_bytes=VMEM_MAX, collective_id=1, has_side_effects=True
         ),
         name="finish",
-    )(*layers, *shards)
-    return [a.reshape(-1)[:entries] for a in found[:4]] + [found[4]]
+    )(*layers)
+    shards = [params, first_moment, second_moment]
+    shape = (entries,)
+    if entries % 128:
+        shape = (rows, 128)
+        shards = [jnp.pad(a, (0, rows * 128 - entries)).reshape(shape) for a in shards]
+    smem = pl.BlockSpec(memory_space=pltpu.SMEM)
+    out = [(shape, F32), (shape, BF16), (shape, F32), (shape, F32), ((1,), F32), ((2,), F32)]
+    found = pl.pallas_call(
+        update_kernel,
+        in_specs=[vmem] * 5,
+        out_specs=[vmem] * 4 + [smem] * 2,
+        out_shape=[jax.ShapeDtypeStruct(shape, dtype) for shape, dtype in out],
+        compiler_params=pltpu.CompilerParams(vmem_limit_bytes=VMEM_MAX),
+        name="update",
+    )(gradient, note, *shards)
+    return [a.reshape(-1)[:entries] for a in found[:4]] + [found[4][0], found[5]]
 
 
 def local(params, first_moment, second_moment, mixture, sources, speakers, lengths):
-    flat = lax.all_gather(params, "batch", axis=0, tiled=True)
-    items = mixture.shape[0]
-    frames_size = lax.axis_size("frames")
-    samples = mixture.shape[1] * frames_size
-    groups = samples // HOP
-    depth = lax.axis_index("frames")
-    column = 2 * items
-    copies = frames_size // column
-    mine = depth // copies
-    weight = jnp.where(depth % copies == 0, 1.0, 0.0).astype(F32)
-    pairs = [[2 * b, 2 * b + 1] for b in range(lax.axis_size("batch") // 2)]
-
-    signals = jnp.concatenate([mixture[:, None], sources], 1)
-    signals = lax.all_gather(signals, "frames", axis=2, tiled=True)
-    scalars = jnp.stack([speakers, lengths], 1).astype(F32)
-    signals = lax.all_gather(signals, "batch", axis=0, tiled=True, axis_index_groups=pairs)
-    scalars = lax.all_gather(scalars, "batch", axis=0, tiled=True, axis_index_groups=pairs)
-    signal = lax.dynamic_slice_in_dim(signals, mine, 1, 0)[0]
-    scalar = lax.dynamic_slice_in_dim(scalars, mine, 1, 0)[0]
-    mix = signal[0]
-    following = jnp.concatenate([mix[1:], jnp.zeros((1,), F32)])
-
-    def by_row(array):
-        return array.reshape(array.shape[:-1] + (groups, HOP)).swapaxes(-1, -2).reshape(array.shape[:-1] + (groups * HOP,))
-
-    mix_row = by_row(mix)
-    follow_row = by_row(following)
-    encoder = flat[:2 * FILTERS].reshape(FILTERS, 2)
-    raw = mix_row[:, None] * encoder[:, 0] + follow_row[:, None] * encoder[:, 1]
-    encoded = jax.nn.softplus(raw)
-
-    def later(array):
-        three = array.reshape(HOP, groups, -1)
-        return jnp.concatenate([three[:, 1:], jnp.zeros_like(three[:, :1])], 1).reshape(array.shape)
-
-    def earlier(array):
-        three = array.reshape(HOP, groups, -1)
-        return jnp.concatenate([jnp.zeros_like(three[:, :1]), three[:, :-1]], 1).reshape(array.shape)
-
-    pad = ((0, (HALF_PAD - HOP) * groups), (0, 0))
-    stream = jnp.pad(jnp.concatenate([encoded, later(encoded)], 1), pad)
+    groups = mixture.shape[1] * lax.axis_size("frames") // HOP
+    flat, stream, column, active, encoder, note = run_start(params, mixture, sources, speakers, lengths)
     view = flat.reshape(-1, 128)
     kept = []
     x = stream
@@ -992,34 +1257,22 @@
         after, normed, scale, h_all, coef = run_forward(layer_no, groups, x, view)
         kept.append((x, normed, scale, h_all, coef))
         x = after
-
-    position = by_row(jnp.arange(samples).astype(F32))
-    valid = jnp.where(position < scalar[1], 1.0, 0.0) * weight
-    active = jnp.where(jnp.arange(SOURCES).astype(F32) < scalar[0], 1.0, 0.0)
-    target = by_row(signal[1:]) * active[:, None]
-    wide = SOURCES * FILTERS
-    masker = flat[-FILTERS * wide - 2 * FILTERS:-2 * FILTERS].reshape(FILTERS, wide)
-    decoder = flat[-2 * FILTERS:].reshape(FILTERS, 2)
-    column = jnp.pad(jnp.concatenate([target, valid[None]], 0).T, ((0, 0), (0, 124)))
-    by_source = jnp.pad(jnp.eye(SOURCES, dtype=F32), ((0, 0), (0, 128 - SOURCES)))
-    taps = (by_source[:, None, None, :] * decoder[None, :, :, None]).reshape(wide, 256)
-    active_wide = jnp.broadcast_to(jnp.repeat(active, FILTERS)[None], (8, wide))
-    grad, head_grads, grad_encoded, loss = run_head(groups, x, stream, column, active_wide, masker, taps)
-    lane = jnp.arange(128)
-    count_part = jnp.sum(scalars[:, 1]) / frames_size
-    loss = jnp.where(lane == 0, loss, jnp.where(lane == 1, count_part, 0.0))
-    signal_column = jnp.pad(jnp.stack([mix_row, follow_row], 1), ((0, 0), (0, 126)))
-    encoder_rows = jnp.pad(encoder.T, ((0, 6), (0, 0)))
+    grad, head_grads, grad_encoded, loss = run_head(groups, x, stream, column, active, note, view)
     sums = [None] * (2 * BLOCKS)
-    extras = {0: (signal_column, grad_encoded, encoder_rows, loss), 2 * BLOCKS - 1: (head_grads,)}
     for layer_no in reversed(range(2 * BLOCKS)):
-        *found, sums[layer_no] = run_backward(
-            layer_no, groups, grad, kept[layer_no], view, extras.get(layer_no, ())
-        )
+        extra = ()
+        if layer_no == 2 * BLOCKS - 1:
+            extra = (head_grads,)
+        if layer_no == 0:
+            extra = (column, grad_encoded, encoder, loss)
+        if layer_no < 2 * BLOCKS - 1:
+            extra = extra + (sums[layer_no + 1],)
+        *found, sums[layer_no] = run_backward(layer_no, groups, grad, kept[layer_no], view, extra)
+        if layer_no < 2 * BLOCKS - 1:
+            sums[layer_no + 1] = found[-1]
         if layer_no:
             grad = found[0]
-    *updated, stats = run_finish(sums, params, first_moment, second_moment)
-    return (*updated, stats[0, 2], stats[0, :2])
+    return tuple(run_finish(sums, params, first_moment, second_moment))
 
 
 def solution(mesh):

time: 388 us -> 337 us (0.87); the launches traced: 382 us -> 335 us
  blocking collectives: 42.8 us -> 0 us
  Pallas kernels: 294 us -> 331 us
  local copies, waits for them, and re-layouts: 21.6 us -> 2.2 us
  between operations: 15.2 us -> 1.21 us
  other arithmetic: 7.48 us -> 0.81 us
    all_gather x3 -> x0, blocking collectives: 42.8 us -> none  [the longest x1 39 us: local(): signals = lax.all_gather(signals, 'frames', axis=2, tiled=True)]
    pallas_call x4, Pallas kernels: 130 us -> 144 us  [run_backward(): pl.pallas_call(functools.partial(backward_kernel, layer_no, groups, steps...]
    pallas_call x4, Pallas kernels: 97 us -> 109 us  [run_forward(): pl.pallas_call(functools.partial(forward_kernel, layer_no, groups, steps)...]
    pallas_call x1 -> x3, Pallas kernels: 54.4 us -> 64.1 us  [the longest x1 33.5 us: run_start(): pl.pallas_call(functools.partial(start_kernel, chips, depths, items, grou...]
    unnamed x19 -> x0, local copies, waits for them, and re-layouts: 8.06 us -> none
    slice x11 -> x0, local copies, waits for them, and re-layouts: 4.07 us -> none  [the longest x1 1.34 us: local(): return (*updated, stats[0, 2], stats[0, :2])]
    select_n x6 -> x0, other arithmetic: 3.88 us -> none  [the longest x2 1.31 us: local(): encoded = jax.nn.softplus(raw)]
  transfers between devices with their start and end apart: 1 -> 0, of which waited for: 0 -> 0; matrix products, arithmetic and copies ran while one was open for 3% -> 0% of each run, Pallas kernels for 0% -> 0%
where the time goes in v3:
time: 337 us; the launch traced here: 335 us
  Pallas kernels  331 us (98%)
    pallas_call x4, Pallas kernels, run_backward(): pl.pallas_call(functools.partial(backward_kernel, layer_no, groups, steps...  144 us
    pallas_call x4, Pallas kernels, run_forward(): pl.pallas_call(functools.partial(forward_kernel, layer_no, groups, steps)...  109 us
    pallas_call x1, Pallas kernels, run_start(): pl.pallas_call(functools.partial(start_kernel, chips, depths, items, grou...  33.5 us
    pallas_call x1, Pallas kernels, run_finish(): pl.pallas_call(functools.partial(finish_kernel, chips, depths, entries),...  27.5 us
    pallas_call x1, Pallas kernels, run_head(): pl.pallas_call(functools.partial(head_kernel, groups), grid=(1,), in_spec...  14.1 us

profile of v3, /device:TPU:0, one launch (start us, length us, event | category | flops | bytes accessed | tf_op | source)
XLA Modules:
  0.0 334.9 jit_solution(14853299056191189200)
XLA Ops:
  0.6 0.7 copy.15
  1.4 0.7 copy.16
  2.1 0.1 add_convert_fusion
  2.2 0.7 pad_maximum_fusion
  2.9 0.1 reshape.52
  3.0 0.6 pad.14
  3.7 33.5 %start.1 = (f32[869376]{0:T(1024)}, f32[2240,128]{1,0:T(8,128)}, f32[2000,128]{1,0:T(8,128)}, f32[8,192]{1,0:T(8,128)}, f32[8,128]{1,0:T(8,128)}, /*index=5*/f32[8,128]{1,0:T(8,128)}) custom-call(f32[108672]{0:T(1024)} %p_ref.3, f32[96,128]{1,0:T(8,128)} %bitcast.15), custom_call_target="tpu_custom_call" | custom-call | tf_op jit(solution)/shard_map/start/pallas_call | solution.py:1086
  37.2 28.6 %forward_intra.2 = (f32[2240,128]{1,0:T(8,128)}, f32[2240,128]{1,0:T(8,128)}, f32[8,128]{1,0:T(8,128)}, f32[100,40,128]{2,1,0:T(8,128)}, f32[100,6,40,128]{3,2,1,0:T(8,128)}) custom-call(f32[2240,128]{1,0:T(8,128)} %get-tuple-element.54.refs_0_.stream_ref.refs_3_, f32[6792,128]{1,0:T(8,128)} %bitcast.6), custom_call_target="tpu_custom_call" | custom-call | tf_op jit(solution)/shard_map/forward_intra/pallas_call | solution.py:1114
  65.8 19.8 %forward_inter.2 = (f32[2240,128]{1,0:T(8,128)}, f32[2240,128]{1,0:T(8,128)}, f32[8,128]{1,0:T(8,128)}, f32[40,112,128]{2,1,0:T(8,128)}, f32[40,6,112,128]{3,2,1,0:T(8,128)}) custom-call(f32[2240,128]{1,0:T(8,128)} %get-tuple-element.56.refs_0_.refs_3_, f32[6792,128]{1,0:T(8,128)} %bitcast.7), custom_call_target="tpu_custom_call" | custom-call | tf_op jit(solution)/shard_map/forward_inter/pallas_call | solution.py:1114
  85.6 28.7 %forward_intra.3 = (f32[2240,128]{1,0:T(8,128)}, f32[2240,128]{1,0:T(8,128)}, f32[8,128]{1,0:T(8,128)}, f32[100,40,128]{2,1,0:T(8,128)}, f32[100,6,40,128]{3,2,1,0:T(8,128)}) custom-call(f32[2240,128]{1,0:T(8,128)} %get-tuple-element.57.refs_0_.refs_3_, f32[6792,128]{1,0:T(8,128)} %bitcast.8), custom_call_target="tpu_custom_call" | custom-call | tf_op jit(solution)/shard_map/forward_intra/pallas_call | solution.py:1114
  114.3 31.7 %forward_inter.3 = (f32[2240,128]{1,0:T(8,128)}, f32[2240,128]{1,0:T(8,128)}, f32[8,128]{1,0:T(8,128)}, f32[40,112,128]{2,1,0:T(8,128)}, f32[40,6,112,128]{3,2,1,0:T(8,128)}) custom-call(f32[2240,128]{1,0:T(8,128)} %get-tuple-element.58.refs_0_.refs_3_, f32[6792,128]{1,0:T(8,128)} %bitcast.9), custom_call_target="tpu_custom_call" | custom-call | tf_op jit(solution)/shard_map/forward_inter/pallas_call | solution.py:1114
  146.0 14.1 %head.1 = (f32[2240,128]{1,0:T(8,128)}, f32[160,128]{1,0:T(8,128)}, f32[2000,64]{1,0:T(8,128)}, f32[8,128]{1,0:T(8,128)}) custom-call(f32[2240,128]{1,0:T(8,128)} %get-tuple-element.59.sep, f32[2240,128]{1,0:T(8,128)} %get-tuple-element.54.refs_0_.stream_ref.refs_3_, f32[2000,128]{1,0:T(8,128)} %get-tuple-element.60.column_ref.refs_7_, ...), custom_call_target="tpu_custom_call" | custom-call | tf_op jit(solution)/shard_map/head/pallas_call | solution.py:1190
  160.1 30.6 %backward_inter.2 = (f32[2240,128]{1,0:T(8,128)}, f32[1024,128]{1,0:T(8,128)}) custom-call(f32[2240,128]{1,0:T(8,128)} %get-tuple-element.63.refs_0_, f32[2240,128]{1,0:T(8,128)} %get-tuple-element.64.refs_1_, f32[8,128]{1,0:T(8,128)} %get-tuple-element.65.refs_2_, f32[2240,128]{1,0:T(8,128)} %get-tuple-element.58.refs_0_.refs_3_, ...), custom_call_target="tpu_custom_call" | custom-call | tf_op jit(solution)/shard_map/backward_inter/pallas_call | solution.py:1156
  190.7 39.3 %backward_intra.2 = (f32[2240,128]{1,0:T(8,128)}, f32[2,1024,128]{2,1,0:T(8,128)}, f32[896,128]{1,0:T(8,128)}) custom-call(f32[2240,128]{1,0:T(8,128)} %get-tuple-element.69.refs_0_, f32[2240,128]{1,0:T(8,128)} %get-tuple-element.70.refs_1_, f32[8,128]{1,0:T(8,128)} %get-tuple-element.71.refs_2_, f32[2240,128]{1,0:T(8,128)} %get-tuple-element.57.refs_0_.refs_3_, ...), custom_call_target="tpu_custom_call" | custom-call | tf_op jit(solution)/shard_map/backward_intra/pallas_call | solution.py:1156
  230.0 35.1 %backward_inter.3 = (f32[2240,128]{1,0:T(8,128)}, f32[2,896,128]{2,1,0:T(8,128)}, f32[896,128]{1,0:T(8,128)}) custom-call(f32[2240,128]{1,0:T(8,128)} %get-tuple-element.75.refs_0_, f32[2240,128]{1,0:T(8,128)} %get-tuple-element.76.refs_1_, f32[8,128]{1,0:T(8,128)} %get-tuple-element.77.refs_2_, f32[2240,128]{1,0:T(8,128)} %get-tuple-element.56.refs_0_.refs_3_, ...), custom_call_target="tpu_custom_call" | custom-call | tf_op jit(solution)/shard_map/backward_inter/pallas_call | solution.py:1156
  265.1 38.7 %backward_intra.3 = (f32[2,896,128]{2,1,0:T(8,128)}, f32[896,128]{1,0:T(8,128)}) custom-call(f32[2240,128]{1,0:T(8,128)} %get-tuple-element.81.refs_0_, f32[2240,128]{1,0:T(8,128)} %get-tuple-element.82.refs_1_, f32[8,128]{1,0:T(8,128)} %get-tuple-element.83.refs_2_, f32[2240,128]{1,0:T(8,128)} %get-tuple-element.54.refs_0_.stream_ref.refs_3_, ...), custom_call_target="tpu_custom_call" | custom-call | tf_op jit(solution)/shard_map/backward_intra/pallas_call | solution.py:1156
  303.8 27.5 %finish.1 = (f32[849,128]{1,0:T(8,128)}, f32[8,128]{1,0:T(8,128)}) custom-call(f32[896,128]{1,0:T(8,128)} %get-tuple-element.90.own_ref, f32[2,896,128]{2,1,0:T(8,128)} %get-tuple-element.91.r1, f32[2,896,128]{2,1,0:T(8,128)} %get-tuple-element.92.r2, f32[2,1024,128]{2,1,0:T(8,128)} %get-tuple-element.93.r3), custom_call_target="tpu_custom_call" | custom-call | tf_op jit(solution)/shard_map/finish/pallas_call | solution.py:1218
  331.3 3.2 update.1
  (2 shorter events, 0.0 us)

commit v4 on v3

--- a/solution.py
+++ b/solution.py
@@ -66,6 +66,9 @@
 WINDOW = 1688
 TAIL_ROW = 6688
 TAIL_ROWS = 104
+FRAME_LANES = 8
+MIX_LANE = SOURCES
+NEXT_LANE = FRAME_LANES + MIX_LANE
 
 
 def window(layer_no):
@@ -105,6 +108,40 @@
         last = jnp.concatenate([last[:, :64], last[:, :64]], 1)
     low = lax.broadcasted_iota(jnp.int32, (1, 128), 1) < 64
     return jnp.where(low, first, turned), jnp.where(low, turned, first), last
+
+
+def share_of(tasks, number, count):
+    return tasks[number * len(tasks) // count:(number + 1) * len(tasks) // count]
+
+
+def fold_halves(a):
+    return a + pltpu.roll(a, FILTERS, 1)
+
+
+def narrow(a, half):
+    if isinstance(half, int):
+        a = pltpu.roll(a, FILTERS, 1) if half else a
+    else:
+        a = jnp.where(half == 0, a, pltpu.roll(a, FILTERS, 1))
+    low_lanes = lax.broadcasted_iota(jnp.int32, a.shape, 1) < FILTERS
+    hi = a.astype(BF16).astype(F32)
+    lo = pltpu.roll(a - hi, FILTERS, 1)
+    return jnp.concatenate([jnp.where(low_lanes, hi, lo), jnp.where(low_lanes, hi, 0.0)], 1).astype(BF16)
+
+
+def narrow_weights(w):
+    hi, lo = split(w)
+    return jnp.concatenate([hi, hi, lo, jnp.zeros_like(hi)], 0)
+
+
+def side_weights(w):
+    hi, lo = split(w)
+    return jnp.concatenate([hi, lo], 1)
+
+
+def dot_sides(a, w):
+    hi, lo = split(a)
+    return fold_halves(dot(hi, w) + dot(lo, w))
 
 
 def put_split(w, twice_ref, low_ref):
@@ -148,6 +185,9 @@
 WINDOW = 1688
 TAIL_ROW = 6688
 TAIL_ROWS = 104
+FRAME_LANES = 8
+MIX_LANE = SOURCES
+NEXT_LANE = FRAME_LANES + MIX_LANE
 
 
 def window(layer_no):
@@ -224,13 +264,6 @@
     return device, pltpu.get_barrier_semaphore()
 
 
-def fetch(flat_ref, layer_no, window_s, sem):
-    first, _, _ = window(layer_no)
-    copy = pltpu.make_async_copy(flat_ref.at[pl.ds(first, WINDOW)], window_s, sem)
-    copy.start()
-    return copy
-
-
 def swap_with_sibling(src_ref, dst_ref, sems, greeted=False):
     device, barrier = greet_sibling()
     if not greeted:
@@ -361,7 +394,7 @@
     inter = layer_no % 2 == 1
     (x_ref, flat_ref,
      next_ref, normed_ref, scale_ref, h_ref, coef_ref,
-     wi2, wil, wr2, wrl, pj2, pjl, proj_s, bias_s, gin_a, gin_b, h_a, h_b, c_s, part_ref, peer_ref, sems, window_s, fetch_sem) = refs
+     wi4, wr2, wrl, pj, proj_s, bias_s, gin_a, gin_b, h_a, h_b, c_s, part_ref, peer_ref, sems) = refs
     turn_no = pl.program_id(0)
     last_turn = pl.num_programs(0) - 1
     chunks = 2 * pl.num_programs(0)
@@ -373,14 +406,17 @@
     def before(chunk_no, gin):
         chunk_no = lax.rem(chunk_no, chunks)
         positions = times(dir_no, chunk_no, length, steps)
-        xs_hi, xs_lo = split(gather(x_ref, inter, groups, positions))
-        both = jnp.concatenate([xs_hi, xs_lo], 1)
-        half = 0 if inter else lax.div(positions[0], HOP)
+        sides = []
+
+        def prepare():
+            xs = gather(x_ref, inter, groups, positions)
+            for half in [0, 1] if inter else [lax.div(positions[0], HOP)]:
+                sides.append(narrow(xs, half))
 
         def gate(q):
             cut = slice(q * UNITS, (q + 1) * UNITS)
-            for side in range(2) if inter else [half]:
-                found = dot(both, wi2[side, :, cut]) + dot(xs_hi, wil[side, :, cut]) + bias_s[0:1, cut]
+            for side, rows_of in enumerate(sides):
+                found = dot(rows_of, wi4[:, cut]) + bias_s[0:1, cut]
                 if inter:
                     for u in range(steps):
                         at = u * rows + side * HALF_PAD
@@ -388,22 +424,22 @@
                 else:
                     gin[:, cut] = found
 
-        return [functools.partial(gate, q) for q in range(4)]
+        return [prepare] + [functools.partial(gate, q) for q in range(4)]
 
     def after(chunk_no, hs):
         chunk_no = lax.rem(chunk_no + chunks, chunks)
         positions = times(dir_no, chunk_no, length, steps)
 
         def project():
+            found = [dot_sides(part, pj[...]) for part in to_sides(inter, steps, hs[...])]
+            low_lanes = lax.broadcasted_iota(jnp.int32, found[0].shape, 1) < FILTERS
             if inter:
-                found = 0.0
-                for side, part in enumerate(to_sides(inter, steps, hs[...])):
-                    found = found + dot3(part, pj2[side], pjl[side])
+                found = jnp.where(low_lanes, found[0], found[1])
                 for u in range(steps):
                     part_ref[stream_rows(inter, groups, positions[u]), :] = found[u * HALF_PAD:(u + 1) * HALF_PAD]
             else:
                 half = lax.div(positions[0], HOP)
-                found = dot3(hs[...], pj2[half], pjl[half])
+                found = jnp.where(low_lanes == (half == 0), found[0], 0.0)
                 for u in range(steps):
                     here = stream_rows(inter, groups, positions[u])
                     part_ref[here, :] = part_ref[here, :] + found[u * groups:(u + 1) * groups]
@@ -414,7 +450,7 @@
         for u in range(steps):
             hi, lo = split(h)
             z = dot(jnp.concatenate([hi, lo], 1), wr2[...]) + dot(hi, wrl[...])
-            for task in beside[u::steps]:
+            for task in share_of(beside, u, steps):
                 task()
             z = z + gin[u * rows:(u + 1) * rows]
             th = jnp.tanh(z)
@@ -441,21 +477,15 @@
     def _():
         device, barrier = greet_sibling()
         pl.semaphore_signal(barrier, inc=1, device_id=device, device_id_type=pl.DeviceIdType.MESH)
-        fetch(flat_ref, layer_no, window_s, fetch_sem).wait()
         part_ref[...] = jnp.zeros_like(part_ref)
         column = lax.broadcasted_iota(jnp.int32, (1, GATES), 1)
         scaling = jnp.where((column >= 2 * UNITS) & (column < 3 * UNITS), 1.0, 0.5)
         _, base, odd = window(layer_no)
-        win, wrec, bias, proj = load_weights(window_s, base, odd, dir_no, proj_s)
-        win = win * scaling
-        none = jnp.zeros_like(win)
-        for half in range(2):
-            put_split(jnp.concatenate([win, none] if half == 0 else [none, win], 0), wi2.at[half], wil.at[half])
+        win, wrec, bias, proj = load_weights(flat_ref, base, odd, dir_no, proj_s)
+        wi4[...] = narrow_weights(win * scaling)
         put_split(wrec * scaling, wr2, wrl)
         bias_s[...] = jnp.broadcast_to(bias * scaling, bias_s.shape)
-        none = jnp.zeros_like(proj)
-        for half in range(2):
-            put_split(jnp.concatenate([proj, none] if half == 0 else [none, proj], 1), pj2.at[half], pjl.at[half])
+        pj[...] = side_weights(proj)
         c_s[...] = jnp.zeros_like(c_s)
         h_b[...] = jnp.zeros_like(h_b)
         for task in before(0, gin_a):
@@ -472,7 +502,7 @@
             task()
         swap_with_sibling(part_ref, peer_ref, sems).wait()
         _, base, odd = window(layer_no)
-        norm_stage(x_ref, part_ref, peer_ref, window_s, base, odd, valid, normed_ref, scale_ref, next_ref)
+        norm_stage(x_ref, part_ref, peer_ref, flat_ref, base, odd, valid, normed_ref, scale_ref, next_ref)
 
 
 def backward_kernel(layer_no, groups, steps, chips, depths, *refs):
@@ -490,8 +520,8 @@
     if not last_layer:
         red_ref, *rest = rest
     (grad_ref,
-     wi2, wil, wrw, wrt, pj2, pjl, proj_s, dmx, dh_a, dh_b, dz_a, dz_b, dc_s, awin, aproj, abias,
-     dx_ref, peer_ref, sems, window_s, fetch_sem, *rest) = rest
+     wi4, wrw, wrt, pj, proj_s, dmx, dh_a, dh_b, dz_a, dz_b, dc_s, awin, aproj, abias,
+     dx_ref, peer_ref, sems, *rest) = rest
     stages = [] if last_layer else reducer(upper_ref, chips, depths, rest)
     turn_no = pl.program_id(0)
     last_turn = pl.num_programs(0) - 1
@@ -507,15 +537,14 @@
 
         def outward():
             dms = gather(dmx, inter, groups, positions)
-            if inter:
-                for side in range(2):
-                    found = dot3(dms, pj2[side], pjl[side])
+            for side, half in enumerate([0, 1] if inter else [lax.div(positions[0], HOP)]):
+                found = dot(narrow(dms, half), pj[...])
+                if inter:
                     for u in range(steps):
                         at = u * rows + side * HALF_PAD
                         dhc[at:at + HALF_PAD] = found[u * HALF_PAD:(u + 1) * HALF_PAD]
-            else:
-                half = lax.div(positions[0], HOP)
-                dhc[...] = dot3(dms, pj2[half], pjl[half])
+                else:
+                    dhc[...] = found
 
         return [outward]
 
@@ -524,21 +553,26 @@
         chunk_no = chunks - 1 - lax.rem(back_no + chunks, chunks)
         positions = times(dir_no, chunk_no, length, steps)
         half = 0 if inter else lax.div(positions[0], HOP)
-        xs = gather(x_ref, inter, groups, positions)
         at = chunk_no * steps
-        hs = h_ref[pl.ds(at, steps)].reshape(steps * rows, UNITS)
-        early = h_ref[lax.rem(at + length - 1, length)] * jnp.where(at == 0, 0.0, 1.0)
-        hp = jnp.concatenate([early, hs[:(steps - 1) * rows]], 0)
-        if inter:
-            lhs = [
-                jnp.concatenate([xs if side == 0 else pltpu.roll(xs, FILTERS, 1), hp_side], 1)
-                for side, hp_side in enumerate(to_sides(inter, steps, hp))
-            ]
-            lhs = jnp.concatenate(lhs, 0)
-        else:
-            lhs = jnp.concatenate([jnp.where(half == 0, xs, pltpu.roll(xs, FILTERS, 1)), hp], 1)
-        lhs_t = lhs.T
-        lhs_hi, lhs_lo = split(lhs_t)
+        count = UNITS + FILTERS
+        ready = []
+
+        def prepare():
+            xs = gather(x_ref, inter, groups, positions)
+            hs = h_ref[pl.ds(at, steps)].reshape(steps * rows, UNITS)
+            early = h_ref[lax.rem(at + length - 1, length)] * jnp.where(at == 0, 0.0, 1.0)
+            hp = jnp.concatenate([early, hs[:(steps - 1) * rows]], 0)
+            if inter:
+                lhs = [
+                    jnp.concatenate([hp_side, (xs if side == 0 else pltpu.roll(xs, FILTERS, 1))[:, :FILTERS]], 1)
+                    for side, hp_side in enumerate(to_sides(inter, steps, hp))
+                ]
+                lhs = jnp.concatenate(lhs, 0)
+            else:
+                turned = jnp.where(half == 0, xs, pltpu.roll(xs, FILTERS, 1))
+                lhs = jnp.concatenate([hp, turned[:, :FILTERS]], 1)
+            lhs_hi, lhs_lo = split(lhs.T)
+            ready.extend([lhs_hi, jnp.concatenate([lhs_hi, lhs_lo], 0)])
 
         def gate(q):
             cut = slice(q * UNITS, (q + 1) * UNITS)
@@ -547,9 +581,11 @@
             if inter:
                 dz = jnp.concatenate(to_sides(inter, steps, dz), 0)
             dz_hi, dz_lo = split(dz)
-            awin[:, cut] += dot(lhs_hi, dz_hi) + dot(lhs_lo, dz_hi) + dot(lhs_hi, dz_lo)
+            both = dot(ready[1], dz_hi)
+            awin[:, cut] += both[:count] + both[count:] + dot(ready[0], dz_lo)
 
         def project():
+            hs = h_ref[pl.ds(at, steps)].reshape(steps * rows, UNITS)
             dms = gather(dmx, inter, groups, positions) * jnp.where(used, 1.0, 0.0)
             if inter:
                 aproj[...] += dot_rows3(jnp.concatenate(to_sides(inter, steps, hs), 1), dms)
@@ -558,19 +594,19 @@
                 aproj[...] += dot_rows3(hs, turned)
 
         def inward():
+            found = [dot_sides(part, wi4[...]) for part in to_sides(inter, steps, dzs[...])]
+            low_lanes = lax.broadcasted_iota(jnp.int32, found[0].shape, 1) < FILTERS
             if inter:
-                found = 0.0
-                for side, dz_side in enumerate(to_sides(inter, steps, dzs[...])):
-                    found = found + dot3(dz_side, wi2[side], wil[side])
+                found = jnp.where(low_lanes, found[0], found[1])
                 for u in range(steps):
                     dx_ref[stream_rows(inter, groups, positions[u]), :] = found[u * HALF_PAD:(u + 1) * HALF_PAD]
             else:
-                found = dot3(dzs[...], wi2[half], wil[half])
+                found = jnp.where(low_lanes == (half == 0), found[0], 0.0)
                 for u in range(steps):
                     here = stream_rows(inter, groups, positions[u])
                     dx_ref[here, :] = dx_ref[here, :] + found[u * groups:(u + 1) * groups]
 
-        return [functools.partial(gate, q) for q in range(4)] + [inward, project]
+        return [inward, project, prepare] + [functools.partial(gate, q) for q in range(4)]
 
     def walk(dhc, dzs, dz, dc_next, sub, beside):
         for u in reversed(range(steps)):
@@ -578,7 +614,7 @@
             hi, lo = split(dz)
             wide = dot(hi, wrw[...])
             dh = wide[:, :UNITS] + wide[:, UNITS:] + dot(lo, wrt[...])
-            for task in beside[steps - 1 - u::steps]:
+            for task in share_of(beside, steps - 1 - u, steps):
                 task()
             dh = dh + dhc[u * rows:(u + 1) * rows]
             dc = dh * coef_ref[at, 1] + dc_next
@@ -598,21 +634,14 @@
             barrier, count = greet_all(chips, depths)
             pl.semaphore_wait(barrier, count)
             stages[0]()
-        fetch(flat_ref, layer_no, window_s, fetch_sem).wait()
         dx_ref[...] = jnp.zeros_like(dx_ref)
         _, base, odd = window(layer_no)
-        win, wrec, _, proj = load_weights(window_s, base, odd, dir_no, proj_s)
-        win_t = win.T
-        none = jnp.zeros_like(win_t)
-        for half in range(2):
-            put_split(jnp.concatenate([win_t, none] if half == 0 else [none, win_t], 1), wi2.at[half], wil.at[half])
+        win, wrec, _, proj = load_weights(flat_ref, base, odd, dir_no, proj_s)
+        wi4[...] = side_weights(win.T)
         hi, lo = split(wrec.T)
         wrw[...] = jnp.concatenate([hi, lo], 1)
         wrt[...] = hi
-        proj_t = proj.T
-        none = jnp.zeros_like(proj_t)
-        for half in range(2):
-            put_split(jnp.concatenate([proj_t, none] if half == 0 else [none, proj_t], 0), pj2.at[half], pjl.at[half])
+        pj[...] = narrow_weights(proj.T)
         dz_b[...] = jnp.zeros_like(dz_b)
         dc_s[...] = jnp.zeros_like(dc_s)
         awin[...] = jnp.zeros_like(awin)
@@ -621,7 +650,7 @@
         grad_ref[...] = jnp.zeros_like(grad_ref)
         g = g_ref[:valid]
         normed = normed_ref[:valid]
-        _, gain, _ = load_vec(window_s, base, odd)
+        _, gain, _ = load_vec(flat_ref, base, odd)
         g_n = g * gain
         total = 2.0 * valid * FILTERS
         mean_one = jnp.sum(g_n) / total
@@ -643,8 +672,9 @@
         for task in before(0, dh_a):
             task()
 
-    for stage, at in zip(stages[1:], (2, 3, 4) if inter else (3, 5, 6, 9)):
-        pl.when(turn_no == at)(stage)
+    for stage, at in zip(stages[1:], (2, 3, 4, None) if inter else (3, 5, 6, 9)):
+        if at is not None:
+            pl.when(turn_no == at)(stage)
 
     dz, dc_next = dz_b[:rows], dc_s[...]
     dz, dc_next = walk(dh_a, dz_a, dz, dc_next, 1, after(2 * turn_no - 1, dz_b) + before(2 * turn_no + 1, dh_b))
@@ -667,8 +697,8 @@
             below_ref[valid:] = jnp.zeros((below_ref.shape[0] - valid, 128), F32)
         for q in range(4):
             cut = slice(q * UNITS, (q + 1) * UNITS)
-            grad_ref[pl.ds(q, FILTERS, stride=4), :] = awin[:FILTERS, cut]
-            grad_ref[pl.ds(256 + q, UNITS, stride=4), :] = awin[2 * FILTERS:, cut]
+            grad_ref[pl.ds(q, FILTERS, stride=4), :] = awin[UNITS:, cut]
+            grad_ref[pl.ds(256 + q, UNITS, stride=4), :] = awin[:UNITS, cut]
             grad_ref[768 + q:769 + q, :] = abias[0:1, cut]
         proj_s[...] = aproj[:UNITS] + pltpu.roll(aproj[UNITS:], FILTERS, 1) if inter else aproj[...]
         even = proj_s[pl.ds(0, 64, stride=2), :]
@@ -680,7 +710,7 @@
             lead = jnp.where(dir_no == 0, 1.0, 0.0)
             streams = lead * g_ref[:valid] + dx_ref[:valid]
             column = column_ref[...]
-            mix, following = column[:, 4:5], column[:, 5:6]
+            mix, following = column[:, MIX_LANE:MIX_LANE + 1], column[:, NEXT_LANE:NEXT_LANE + 1]
             raw = mix * encoder_ref[0:1, :FILTERS] + following * encoder_ref[1:2, :FILTERS]
             group_at = lax.broadcasted_iota(jnp.int32, (valid, FILTERS), 0) % groups
             shifted = jnp.where(group_at == 0, 0.0, pltpu.roll(pltpu.roll(streams, FILTERS, 1), 1, 0)[:, :FILTERS])
@@ -691,14 +721,11 @@
             grad_ref[OWN_EXTRA + 1:OWN_EXTRA + 2] = loss_ref[0:1] * lead
 
 
-def head_kernel(groups, sep, stream_ref, column_ref, active_ref, note_ref, flat_ref,
+def head_kernel(groups, sep, stream_ref, column_ref, active_ref, note_ref, tail_s,
                 g_ref, hg_ref, denc_ref, loss_ref,
-                sig_s, now_s, before_s, slope_s, mk2, mkl, mt2, mtl, dk2, dkl, dt2, dtl, amask, adec, m_low, m_top, tail_s, tail_sem):
+                sig_s, now_s, before_s, slope_s, mk2, mkl, mt2, mtl, dk2, dkl, dt2, dtl, amask, adec, m_low, m_top):
     valid = HOP * groups
     block = 10 * groups
-    tail = pltpu.make_async_copy(flat_ref.at[pl.ds(TAIL_ROW, TAIL_ROWS)], tail_s, tail_sem)
-    tail.start()
-    tail.wait()
     first, second, third = (tail_s[pl.ds(6695 - TAIL_ROW + n, 32, stride=3), :] for n in range(3))
     m_low[pl.ds(0, 32, stride=2), :] = first
     m_low[pl.ds(1, 32, stride=2), :] = jnp.concatenate([second[:, FILTERS:], third[:, :FILTERS]], 1)
@@ -755,8 +782,11 @@
     def losses(n, total):
         column = column_ref[rows(n), :]
         lane = lax.broadcasted_iota(jnp.int32, (block, 128), 1)
-        target = jnp.where(lane < SOURCES, column, 0.0)
-        kept = jnp.broadcast_to(column[:, SOURCES:SOURCES + 1], (block, 128))
+        active_lane = (lane < SOURCES) & (lane.astype(F32) < active_ref[1:2, :128])
+        target = jnp.where(active_lane, column, 0.0)
+        row = lax.broadcasted_iota(jnp.int32, (block, 128), 0)
+        frame = HOP * (row % groups) + row // groups + 10 * n
+        kept = jnp.where(frame.astype(F32) < active_ref[2:3, :128], active_ref[3:4, :128], 0.0)
         differ = now_s[rows(n), :] + before_s[rows(n), :] - target
         root = jnp.sqrt(differ * differ + 1.0)
         slope_s[rows(n), :] = kept * differ / root
@@ -907,10 +937,12 @@
 
 
 def start_kernel(chips, depths, items, groups, gathers, p_ref, mail_ref, *refs):
+    *views, refs = *refs[:5], refs[5:]
     if gathers:
-        flat_ref, *refs = refs
+        *refs, flat_ref = refs
     else:
         flat_ref = p_ref
+    *refs, view_sem = refs
     (stream_ref, column_ref, active_ref, encoder_ref, note_ref,
      inbox, planes, plane_sem, pair_sem, own_sem, mail_sem) = refs
     b = lax.axis_index("batch")
@@ -983,38 +1015,29 @@
         def _():
             far.wait_send()
 
-    for signal in range(1 + SOURCES):
-        planes[signal] = jnp.concatenate(
-            [inbox[depth, signal * share:(signal + 1) * share] for depth in range(depths)], 0
-        )
-    facts = inbox[0, (1 + SOURCES) * share:(1 + SOURCES) * share + 1]
+    frames = jnp.concatenate([inbox[depth, :share] for depth in range(depths)], 0)
+    facts = inbox[0, share:share + 1]
     speakers, length = facts[:, 0:1], facts[:, 1:2]
     whole_item = jnp.where(lax.rem(z, copies) == 0, 1.0, 0.0)
     lead = jnp.where(core == 0, whole_item, 0.0)
     lane = lax.broadcasted_iota(jnp.int32, (groups, 128), 1)
     group = lax.broadcasted_iota(jnp.int32, (groups, 128), 0)
-    first_lane = lane[:8]
-    note_ref[...] = jnp.where(first_lane == 1, lead * length, 0.0)
+    note_ref[...] = jnp.where(lane[:8] == 1, lead * length, 0.0)
     wide = SOURCES * FILTERS
     source = lax.broadcasted_iota(jnp.int32, (8, wide), 1) // FILTERS
-    active_ref[...] = jnp.where(source.astype(F32) < speakers, 1.0, 0.0)
-    mix = planes[0]
-    next_start = jnp.where(group == groups - 1, 0.0, pltpu.roll(mix, groups - 1, 0))
-    following = jnp.where(lane == HOP - 1, pltpu.roll(next_start, HOP - 1, 1), pltpu.roll(mix, 127, 1))
-
-    def columns(k, carry):
-        def take(array):
-            return jnp.broadcast_to(pltpu.roll(array, lax.rem(128 - k, 128), 1)[:, 0:1], (groups, 128))
-
-        found = jnp.where((group * HOP + k).astype(F32) < length, whole_item, 0.0)
-        for j in range(SOURCES):
-            found = jnp.where(lane == j, jnp.where(speakers > j, take(planes[1 + j]), 0.0), found)
-        found = jnp.where(lane == 4, take(mix), found)
-        found = jnp.where(lane == 5, take(following), found)
-        column_ref[pl.ds(pl.multiple_of(k * groups, 8), groups), :] = found
-        return carry
-
-    lax.fori_loop(0, HOP, columns, 0)
+    fact_at = lax.broadcasted_iota(jnp.int32, (8, wide), 0)
+    active = jnp.where(source.astype(F32) < speakers, 1.0, 0.0)
+    active = jnp.where(fact_at == 1, speakers, jnp.where(fact_at == 2, length, active))
+    active_ref[...] = jnp.where(fact_at == 3, whole_item, active)
+    end = HOP * FRAME_LANES
+    tile = end // 128 * 128
+    opening = jnp.where(group == groups - 1, 0.0, pltpu.roll(frames[:, :128], groups - 1, 0))
+    ending = (lane >= end - tile) & (lane < end - tile + FRAME_LANES)
+    planes[:, :tile] = frames[:, :tile]
+    planes[:, tile:tile + 128] = jnp.where(ending, pltpu.roll(opening, end - tile, 1), frames[:, tile:tile + 128])
+    planes[:, tile + 128:] = jnp.zeros((groups, planes.shape[1] - tile - 128), F32)
+    for k in range(HOP):
+        column_ref[k * groups:(k + 1) * groups] = planes[:, FRAME_LANES * k:FRAME_LANES * k + 128]
 
     if gathers:
         for step in range(1, chips):
@@ -1028,6 +1051,13 @@
         for copy in beside:
             copy.wait()
 
+    bounds = [(window(n)[0], WINDOW) for n in range(2 * BLOCKS)] + [(TAIL_ROW, TAIL_ROWS)]
+    stores = [
+        pltpu.make_async_copy(flat_ref.at[pl.ds(128 * at, 128 * count)], view, view_sem.at[n])
+        for n, ((at, count), view) in enumerate(zip(bounds, views))
+    ]
+    for store in stores:
+        store.start()
     taps = flat_ref[0:128].reshape(1, 128)
     at_lane = lax.broadcasted_iota(jnp.int32, (128, 128), 1)
     at_row = lax.broadcasted_iota(jnp.int32, (128, 128), 0)
@@ -1036,17 +1066,23 @@
     tap_rows = [jnp.sum(jnp.where(at_row == twice + tap, upright, 0.0), 0, keepdims=True) for tap in range(2)]
     encoder_ref[...] = jnp.where(at_row[:8] == 0, tap_rows[0], jnp.where(at_row[:8] == 1, tap_rows[1], 0.0))
 
-    def encode(k, carry):
-        rows = pl.ds(pl.multiple_of(k * groups, 8), groups)
+    block = 5 * groups
+    block_lane = lax.broadcasted_iota(jnp.int32, (block, 128), 1)
+    last_group = lax.broadcasted_iota(jnp.int32, (block, 128), 0) % groups == groups - 1
+
+    def encode(n, carry):
+        rows = pl.ds(pl.multiple_of(n * block, 8), block)
         column = column_ref[rows, :]
-        raw = column[:, 4:5] * tap_rows[0] + column[:, 5:6] * tap_rows[1]
+        raw = column[:, MIX_LANE:MIX_LANE + 1] * tap_rows[0] + column[:, NEXT_LANE:NEXT_LANE + 1] * tap_rows[1]
         encoded = jnp.maximum(raw, 0.0) + jnp.log1p(jnp.exp(-jnp.abs(raw)))
-        later = jnp.where(group == groups - 1, 0.0, pltpu.roll(encoded, groups - 1, 0))
-        stream_ref[rows, :] = jnp.where(lane < FILTERS, encoded, later)
+        later = jnp.where(last_group, 0.0, pltpu.roll(encoded, block - 1, 0))
+        stream_ref[rows, :] = jnp.where(block_lane < FILTERS, encoded, later)
         return carry
 
-    lax.fori_loop(0, HOP, encode, 0, unroll=5)
+    lax.fori_loop(0, HOP // 5, encode, 0)
     stream_ref[valid:] = jnp.zeros((stream_ref.shape[0] - valid, 128), F32)
+    for store in stores:
+        store.wait()
 
 
 def sizes(inter, groups):
@@ -1067,37 +1103,44 @@
     share = groups // depths
     valid = HOP * groups
     copies = depths // (2 * items)
-    signals = jnp.concatenate([mixture[:, None], sources], 1).reshape(items, (1 + SOURCES) * share, HOP)
+    signals = jnp.concatenate([sources, mixture[:, None]], 1).transpose(0, 2, 1)
+    signals = jnp.pad(signals, ((0, 0), (0, 0), (0, FRAME_LANES - 1 - SOURCES)))
+    signals = signals.reshape(items, share, HOP * FRAME_LANES)
+    width = -(-HOP * FRAME_LANES // 128) * 128
     facts = jnp.stack([speakers, lengths], 1).astype(F32)[:, None]
-    mail_rows = -(-((1 + SOURCES) * share + 1) // 8) * 8
+    mail_rows = -(-(share + 1) // 8) * 8
     mail = jnp.concatenate(
-        [jnp.pad(signals, ((0, 0), (0, 0), (0, 128 - HOP))), jnp.pad(facts, ((0, 0), (0, 0), (0, 126)))], 1
-    )
-    mail = jnp.pad(mail, ((0, 0), (0, mail_rows - mail.shape[1]), (0, 0))).reshape(items * mail_rows, 128)
+        [
+            jnp.pad(signals, ((0, 0), (0, 0), (0, width - HOP * FRAME_LANES))),
+            jnp.pad(facts, ((0, 0), (0, mail_rows - share - 1), (0, width - 2))),
+        ],
+        1,
+    ).reshape(items * mail_rows, width)
     stream_shape = (HALF_PAD * groups, 128)
     out = [stream_shape, (valid, 128), (8, SOURCES * FILTERS), (8, 128), (8, 128)]
+    out = [(WINDOW * 128,)] * (2 * BLOCKS) + [(TAIL_ROWS * 128,)] + out
     gathers = params.shape[0] % 128 == 0
-    if gathers:
-        out = [(params.shape[0] * 2 * chips,)] + out
-    else:
+    whole_flat = [pltpu.VMEM((params.shape[0] * 2 * chips,), F32)] if gathers else []
+    if not gathers:
         params = lax.all_gather(params, "batch", axis=0, tiled=True)
     vmem = pl.BlockSpec(memory_space=pltpu.VMEM)
     sems = pltpu.SemaphoreType.DMA
     found = pl.pallas_call(
         functools.partial(start_kernel, chips, depths, items, groups, gathers),
         in_specs=[vmem] * 2,
-        out_specs=[vmem] * len(out),
+        out_specs=[pl.BlockSpec(memory_space=pl.ANY)] * 5 + [vmem] * 5,
         out_shape=[jax.ShapeDtypeStruct(shape, F32) for shape in out],
         scratch_shapes=[
-            pltpu.VMEM((depths, mail_rows, 128), F32), pltpu.VMEM((1 + SOURCES, groups, 128), F32),
-            sems((2, chips - 1)), sems((2, chips)), sems, sems((2, max(depths, 2 * items * copies))),
-        ],
+            pltpu.VMEM((depths, mail_rows, width), F32), pltpu.VMEM((groups, width + 128), F32),
+            sems((2, chips - 1)), sems((2, chips)), sems, sems((2, max(depths, 2 * items * copies))), sems((5,)),
+        ]
+        + whole_flat,
         compiler_params=pltpu.CompilerParams(
             vmem_limit_bytes=VMEM_MAX, collective_id=10, has_side_effects=True
         ),
         name="start",
     )(params, mail)
-    return found if gathers else [params, *found]
+    return [a.reshape(-1, 128) for a in found[:5]], found[5:]
 
 
 def run_forward(layer_no, groups, stream, flat):
@@ -1114,20 +1157,19 @@
     return pl.pallas_call(
         functools.partial(forward_kernel, layer_no, groups, steps),
         grid=(length // (2 * steps),),
-        in_specs=[whole(stream_shape), pl.BlockSpec(memory_space=pl.ANY)],
+        in_specs=[whole(stream_shape), whole((WINDOW, 128))],
         out_specs=[spec for _, spec in out],
         out_shape=[jax.ShapeDtypeStruct(shape, F32) for shape, _ in out],
         scratch_shapes=[
-            pltpu.VMEM((2, 256, GATES), BF16), pltpu.VMEM((2, 128, GATES), BF16),
+            pltpu.VMEM((256, GATES), BF16),
             pltpu.VMEM((256, GATES), BF16), pltpu.VMEM((128, GATES), BF16),
-            pltpu.VMEM((2, 256, 128), BF16), pltpu.VMEM((2, 128, 128), BF16),
+            pltpu.VMEM((UNITS, 128), BF16),
             pltpu.VMEM((UNITS, 128), F32),
             pltpu.VMEM((8, GATES), F32),
             pltpu.VMEM((steps * rows, GATES), F32), pltpu.VMEM((steps * rows, GATES), F32),
             pltpu.VMEM((steps * rows, UNITS), F32), pltpu.VMEM((steps * rows, UNITS), F32),
             pltpu.VMEM((rows, UNITS), F32),
             pltpu.VMEM(stream_shape, F32), pltpu.VMEM(stream_shape, F32), pltpu.SemaphoreType.DMA((2,)),
-            pltpu.VMEM((WINDOW, 128), F32), pltpu.SemaphoreType.DMA,
         ],
         compiler_params=pltpu.CompilerParams(
             vmem_limit_bytes=VMEM_MAX, collective_id=2 + layer_no, has_side_effects=True
@@ -1157,23 +1199,22 @@
         functools.partial(backward_kernel, layer_no, groups, steps, chips, depths),
         grid=(count,),
         in_specs=[whole(a.shape) for a in (grad, normed, scale, x, h_all)]
-        + [pl.BlockSpec((2 * steps, 6, rows, UNITS), lambda j: (count - 1 - j, 0, 0, 0)), pl.BlockSpec(memory_space=pl.ANY)]
+        + [pl.BlockSpec((2 * steps, 6, rows, UNITS), lambda j: (count - 1 - j, 0, 0, 0)), whole((WINDOW, 128))]
         + [whole(a.shape) for a in extra],
         out_specs=[whole(shape) for shape in out],
         out_shape=[jax.ShapeDtypeStruct(shape, F32) for shape in out],
         scratch_shapes=[
-            pltpu.VMEM((2, 2 * GATES, 128), BF16), pltpu.VMEM((2, GATES, 128), BF16),
+            pltpu.VMEM((GATES, 128), BF16),
             pltpu.VMEM((GATES, 256), BF16), pltpu.VMEM((GATES, 128), BF16),
-            pltpu.VMEM((2, 256, 128), BF16), pltpu.VMEM((2, 128, 128), BF16),
+            pltpu.VMEM((256, UNITS), BF16),
             pltpu.VMEM((UNITS, 128), F32),
             pltpu.VMEM(stream_shape, F32),
             pltpu.VMEM((steps * rows, UNITS), F32), pltpu.VMEM((steps * rows, UNITS), F32),
             pltpu.VMEM((steps * rows, GATES), F32), pltpu.VMEM((steps * rows, GATES), F32),
             pltpu.VMEM((rows, UNITS), F32),
-            pltpu.VMEM((256, GATES), F32), pltpu.VMEM((2 * UNITS if inter else UNITS, 128), F32),
+            pltpu.VMEM((UNITS + FILTERS, GATES), F32), pltpu.VMEM((2 * UNITS if inter else UNITS, 128), F32),
             pltpu.VMEM((8, GATES), F32),
             pltpu.VMEM(stream_shape, F32), pltpu.VMEM(stream_shape, F32), pltpu.SemaphoreType.DMA((2,)),
-            pltpu.VMEM((WINDOW, 128), F32), pltpu.SemaphoreType.DMA,
         ]
         + scratch,
         compiler_params=pltpu.CompilerParams(vmem_limit_bytes=VMEM_MAX, collective_id=6 + layer_no, has_side_effects=True),
@@ -1181,16 +1222,16 @@
     )(grad, normed, scale, x, h_all, coef, flat, *extra)
 
 
-def run_head(groups, separated, stream, column, active, note, flat):
+def run_head(groups, separated, stream, column, active, note, tail):
     valid = HOP * groups
     stream_shape = (HALF_PAD * groups, 128)
     out = [stream_shape, (HEAD_ROWS, 128), (valid, FILTERS), (8, 128)]
     wide = SOURCES * FILTERS
-    operands = (separated, stream, column, active, note)
+    operands = (separated, stream, column, active, note, tail)
     return pl.pallas_call(
         functools.partial(head_kernel, groups),
         grid=(1,),
-        in_specs=[whole(a.shape) for a in operands] + [pl.BlockSpec(memory_space=pl.ANY)],
+        in_specs=[whole(a.shape) for a in operands],
         out_specs=[whole(shape) for shape in out],
         out_shape=[jax.ShapeDtypeStruct(shape, F32) for shape in out],
         scratch_shapes=[
@@ -1202,11 +1243,10 @@
             pltpu.VMEM((512, wide), BF16), pltpu.VMEM((256, wide), BF16),
             pltpu.VMEM((FILTERS, wide), F32), pltpu.VMEM((wide, 256), F32),
             pltpu.VMEM((FILTERS, 128), F32), pltpu.VMEM((FILTERS, 128), F32),
-            pltpu.VMEM((TAIL_ROWS, 128), F32), pltpu.SemaphoreType.DMA,
         ],
         compiler_params=pltpu.CompilerParams(vmem_limit_bytes=VMEM_MAX),
         name="head",
-    )(*operands, flat)
+    )(*operands)
 
 
 def run_finish(layers, params, first_moment, second_moment):
@@ -1249,15 +1289,14 @@
 
 def local(params, first_moment, second_moment, mixture, sources, speakers, lengths):
     groups = mixture.shape[1] * lax.axis_size("frames") // HOP
-    flat, stream, column, active, encoder, note = run_start(params, mixture, sources, speakers, lengths)
-    view = flat.reshape(-1, 128)
+    views, (stream, column, active, encoder, note) = run_start(params, mixture, sources, speakers, lengths)
     kept = []
     x = stream
     for layer_no in range(2 * BLOCKS):
-        after, normed, scale, h_all, coef = run_forward(layer_no, groups, x, view)
+        after, normed, scale, h_all, coef = run_forward(layer_no, groups, x, views[layer_no])
         kept.append((x, normed, scale, h_all, coef))
         x = after
-    grad, head_grads, grad_encoded, loss = run_head(groups, x, stream, column, active, note, view)
+    grad, head_grads, grad_encoded, loss = run_head(groups, x, stream, column, active, note, views[2 * BLOCKS])
     sums = [None] * (2 * BLOCKS)
     for layer_no in reversed(range(2 * BLOCKS)):
         extra = ()
@@ -1267,7 +1306,7 @@
             extra = (column, grad_encoded, encoder, loss)
         if layer_no < 2 * BLOCKS - 1:
             extra = extra + (sums[layer_no + 1],)
-        *found, sums[layer_no] = run_backward(layer_no, groups, grad, kept[layer_no], view, extra)
+        *found, sums[layer_no] = run_backward(layer_no, groups, grad, kept[layer_no], views[layer_no], extra)
         if layer_no < 2 * BLOCKS - 1:
             sums[layer_no + 1] = found[-1]
         if layer_no:

time: 337 us -> 319 us (0.947)
  Pallas kernels: 331 us -> 309 us
    pallas_call x4, Pallas kernels: 109 us -> 95.2 us  [run_forward(): pl.pallas_call(functools.partial(forward_kernel, layer_no, groups, steps)...]
    pallas_call x4, Pallas kernels: 144 us -> 138 us  [run_backward(): pl.pallas_call(functools.partial(backward_kernel, layer_no, groups, steps...]
where the time goes in v4:
time: 319 us; the launch traced here: 314 us
  Pallas kernels  309 us (97%)
    pallas_call x4, Pallas kernels, run_backward(): pl.pallas_call(functools.partial(backward_kernel, layer_no, groups, steps...  138 us
    pallas_call x4, Pallas kernels, run_forward(): pl.pallas_call(functools.partial(forward_kernel, layer_no, groups, steps)...  95.2 us
    pallas_call x1, Pallas kernels, run_start(): pl.pallas_call(functools.partial(start_kernel, chips, depths, items, grou...  32.8 us
    pallas_call x1, Pallas kernels, run_finish(): pl.pallas_call(functools.partial(finish_kernel, chips, depths, entries),...  27.1 us
    pallas_call x1, Pallas kernels, run_head(): pl.pallas_call(functools.partial(head_kernel, groups), grid=(1,), in_spec...  13.6 us

profile of v4, /device:TPU:0, one launch (start us, length us, event | category | flops | bytes accessed | tf_op | source)
XLA Modules:
  0.0 313.7 jit_solution(819602460762065784)
XLA Ops:
  0.6 0.7 copy.15
  1.4 0.7 copy.16
  2.1 0.1 add_convert_fusion
  2.2 0.7 maximum_bitcast_fusion
  2.9 0.2 copy.17
  3.2 0.2 reshape.64
  3.4 0.6 select_maximum_fusion
  4.0 32.8 %start.1 = (f32[216064]{0:T(1024)}, f32[216064]{0:T(1024)}, f32[216064]{0:T(1024)}, f32[216064]{0:T(1024)}, f32[13312]{0:T(1024)}, /*index=5*/f32[2240,128]{1,0:...) custom-call(f32[108672]{0:T(1024)} %p_ref.3, f32[32,512]{1,0:T(8,128)} %bitcast.20), custom_call_target="tpu_custom_call" | custom-call | tf_op jit(solution)/shard_map/start/pallas_call | solution.py:1128
  36.8 29.3 %forward_intra.2 = (f32[2240,128]{1,0:T(8,128)}, f32[2240,128]{1,0:T(8,128)}, f32[8,128]{1,0:T(8,128)}, f32[100,40,128]{2,1,0:T(8,128)}, f32[100,6,40,128]{3,2,1,0:T(8,128)}) custom-call(f32[2240,128]{1,0:T(8,128)} %get-tuple-element.58.refs_0_.stream_ref.refs_3_, f32[1688,128]{1,0:T(8,128)} %bitcast.18), custom_call_target="tpu_custom_call" | custom-call | tf_op jit(solution)/shard_map/forward_intra/pallas_call | solution.py:1157
  66.1 18.3 %forward_inter.2 = (f32[2240,128]{1,0:T(8,128)}, f32[2240,128]{1,0:T(8,128)}, f32[8,128]{1,0:T(8,128)}, f32[40,112,128]{2,1,0:T(8,128)}, f32[40,6,112,128]{3,2,1,0:T(8,128)}) custom-call(f32[2240,128]{1,0:T(8,128)} %get-tuple-element.60.refs_0_.refs_3_, f32[1688,128]{1,0:T(8,128)} %bitcast.12), custom_call_target="tpu_custom_call" | custom-call | tf_op jit(solution)/shard_map/forward_inter/pallas_call | solution.py:1157
  84.4 29.3 %forward_intra.3 = (f32[2240,128]{1,0:T(8,128)}, f32[2240,128]{1,0:T(8,128)}, f32[8,128]{1,0:T(8,128)}, f32[100,40,128]{2,1,0:T(8,128)}, f32[100,6,40,128]{3,2,1,0:T(8,128)}) custom-call(f32[2240,128]{1,0:T(8,128)} %get-tuple-element.62.refs_0_.refs_3_, f32[1688,128]{1,0:T(8,128)} %bitcast.14), custom_call_target="tpu_custom_call" | custom-call | tf_op jit(solution)/shard_map/forward_intra/pallas_call | solution.py:1157
  113.7 18.3 %forward_inter.3 = (f32[2240,128]{1,0:T(8,128)}, f32[2240,128]{1,0:T(8,128)}, f32[8,128]{1,0:T(8,128)}, f32[40,112,128]{2,1,0:T(8,128)}, f32[40,6,112,128]{3,2,1,0:T(8,128)}) custom-call(f32[2240,128]{1,0:T(8,128)} %get-tuple-element.64.refs_0_.refs_3_, f32[1688,128]{1,0:T(8,128)} %bitcast.16), custom_call_target="tpu_custom_call" | custom-call | tf_op jit(solution)/shard_map/forward_inter/pallas_call | solution.py:1157
  132.0 13.6 %head.1 = (f32[2240,128]{1,0:T(8,128)}, f32[160,128]{1,0:T(8,128)}, f32[2000,64]{1,0:T(8,128)}, f32[8,128]{1,0:T(8,128)}) custom-call(f32[2240,128]{1,0:T(8,128)} %get-tuple-element.66.sep, f32[2240,128]{1,0:T(8,128)} %get-tuple-element.58.refs_0_.stream_ref.refs_3_, f32[2000,128]{1,0:T(8,128)} %get-tuple-element.67.column_ref.refs_7_, ...), custom_call_target="tpu_custom_call" | custom-call | tf_op jit(solution)/shard_map/head/pallas_call | solution.py:1231
  145.6 25.4 %backward_inter.2 = (f32[2240,128]{1,0:T(8,128)}, f32[1024,128]{1,0:T(8,128)}) custom-call(f32[2240,128]{1,0:T(8,128)} %get-tuple-element.71.refs_0_, f32[2240,128]{1,0:T(8,128)} %get-tuple-element.72.refs_1_, f32[8,128]{1,0:T(8,128)} %get-tuple-element.73.refs_2_, f32[2240,128]{1,0:T(8,128)} %get-tuple-element.64.refs_0_.refs_3_, ...), custom_call_target="tpu_custom_call" | custom-call | tf_op jit(solution)/shard_map/backward_inter/pallas_call | solution.py:1198
  171.0 35.7 %backward_intra.2 = (f32[2240,128]{1,0:T(8,128)}, f32[2,1024,128]{2,1,0:T(8,128)}, f32[896,128]{1,0:T(8,128)}) custom-call(f32[2240,128]{1,0:T(8,128)} %get-tuple-element.77.refs_0_, f32[2240,128]{1,0:T(8,128)} %get-tuple-element.78.refs_1_, f32[8,128]{1,0:T(8,128)} %get-tuple-element.79.refs_2_, f32[2240,128]{1,0:T(8,128)} %get-tuple-element.62.refs_0_.refs_3_, ...), custom_call_target="tpu_custom_call" | custom-call | tf_op jit(solution)/shard_map/backward_intra/pallas_call | solution.py:1198
  206.8 41.1 %backward_inter.3 = (f32[2240,128]{1,0:T(8,128)}, f32[2,896,128]{2,1,0:T(8,128)}, f32[896,128]{1,0:T(8,128)}) custom-call(f32[2240,128]{1,0:T(8,128)} %get-tuple-element.83.refs_0_, f32[2240,128]{1,0:T(8,128)} %get-tuple-element.84.refs_1_, f32[8,128]{1,0:T(8,128)} %get-tuple-element.85.refs_2_, f32[2240,128]{1,0:T(8,128)} %get-tuple-element.60.refs_0_.refs_3_, ...), custom_call_target="tpu_custom_call" | custom-call | tf_op jit(solution)/shard_map/backward_inter/pallas_call | solution.py:1198
  247.9 35.3 %backward_intra.3 = (f32[2,896,128]{2,1,0:T(8,128)}, f32[896,128]{1,0:T(8,128)}) custom-call(f32[2240,128]{1,0:T(8,128)} %get-tuple-element.89.refs_0_, f32[2240,128]{1,0:T(8,128)} %get-tuple-element.90.refs_1_, f32[8,128]{1,0:T(8,128)} %get-tuple-element.91.refs_2_, f32[2240,128]{1,0:T(8,128)} %get-tuple-element.58.refs_0_.stream_ref.refs_3_, ...), custom_call_target="tpu_custom_call" | custom-call | tf_op jit(solution)/shard_map/backward_intra/pallas_call | solution.py:1198
  283.2 27.1 %finish.1 = (f32[849,128]{1,0:T(8,128)}, f32[8,128]{1,0:T(8,128)}) custom-call(f32[896,128]{1,0:T(8,128)} %get-tuple-element.98.own_ref, f32[2,896,128]{2,1,0:T(8,128)} %get-tuple-element.99.r1, f32[2,896,128]{2,1,0:T(8,128)} %get-tuple-element.100.r2, f32[2,1024,128]{2,1,0:T(8,128)} %get-tuple-element.101.r3), custom_call_target="tpu_custom_call" | custom-call | tf_op jit(solution)/shard_map/finish/pallas_call | solution.py:1258
  310.3 3.2 %update.1 = (f32[108672]{0:T(1024)}, bf16[108672]{0:T(1024)(128)(2,1)}, f32[108672]{0:T(1024)}, f32[108672]{0:T(1024)}, f32[1]{0:T(128)}, /*index=5*/f32[2]{0:T(128)}) custom-call(f32[849,128]{1,0:T(8,128)} %get-tuple-element.102.grad_ref, f32[8,128]{1,0:T(8,128)} %get-tuple-element.103.note_ref, f32[108672]{0:T(1024)} %p_ref.3, f32[108672]{0:T(1024)} %m_ref.1, ...), custom_call_target="tpu_custom_call" | custom-call | tf_op jit(solution)/shard_map/update/pallas_call | solution.py:1279
  (1 shorter events, 0.0 us)
